TPU v7x, 128 devices: a whole 4x4x4 slice. The times are simulated.
128 devices in a mesh: dp: 8 (over y_hi, x), ctx: 4 (over z), tensor: 4 (over y_lo, core).
Axes of the slice: x: 4, y: 4 (y_hi: 2, y_lo: 2; y = y_hi * 2 + y_lo), z: 4, core: 2. Of those that a mesh axis runs over, the one named last changes fastest.
Arguments:
- tokens: bfloat16 [8, 2048, 8192], P('dp', 'ctx'), may hold values from -16 to 16
- input_proj: bfloat16 [8192, 9216], P(('dp', 'ctx'), 'tensor'), may hold values from -0.0625 to 0.0625
- step_proj: bfloat16 [8192, 128], P(('dp', 'ctx'), 'tensor'), may hold values from -1 to 1
- conv_weight: float32 [4, 9216], P(None, 'tensor'), may hold values from -4 to 4
- conv_bias: float32 [9216], P('tensor'), may hold values from -3 to 3
- step_bias: float32 [128], P('tensor'), may hold values from -5 to -3
- head_rate: float32 [128], P('tensor'), may hold values from 0.00024414062 to 1
- state_pool: bfloat16 [16, 8192, 256], P('dp', 'tensor'), may hold values from -6 to 6
- resume_slot: int32 [8], P('dp'), may hold values from 0 to 15, as said below
- offsets: int32 [8], P('dp'), may hold values from 0 to 1535
Outputs:
- boundary_states: float32 [8, 4, 8192, 256], P('dp', 'ctx', 'tensor')
Inputs may be any that keep to these rules, and one draw needn't show every extreme that they name: `resume_slot`: no two responses name the same slot.
All inputs are finite; a program needn't handle non-finite values.
Results may differ from a plain program's by a relative error of at most 0.0025.
Values may be sent and summed in bfloat16 or wider, within the bound.
No kernel may reach another device: no remote copies, remote signals or barrier semaphores. Data moves between devices by JAX's collectives and lax.ppermute only.
A program may use at most 192 MiB of HBM per device.

v0:
```python
import jax
import jax.numpy as jnp
from jax import lax
from jax.sharding import PartitionSpec as P

GROUP_HEADS = 32
P_SIZE = 64
N = 256


def from_behind(value, axis, by):
    devices = lax.axis_size(axis)
    pairs = [(i, i + by) for i in range(devices) if 0 <= i + by < devices]
    return lax.ppermute(value, axis, pairs)


def prefix(part, axis, combine, identity):
    place = lax.axis_index(axis)
    gathered = jax.tree.map(lambda a: lax.all_gather(a, axis), part)
    state = jax.tree.map(lambda a, e: jnp.zeros_like(a) + jnp.asarray(e, a.dtype), part, identity)

    def one(step, state):
        return combine(
            state, jax.tree.map(lambda a: lax.dynamic_index_in_dim(a, step, 0, False), gathered)
        )

    return lax.fori_loop(0, place, one, state)


def folder(matrix, pieces):
    return (
        jnp.dot(matrix, pieces[0], preferred_element_type=jnp.float32),
        jnp.dot(matrix, pieces[1], preferred_element_type=jnp.float32),
    )


def combine(earlier, later):
    return (earlier[0] * later[0], later[0][:, :, None] * earlier[1] + later[1])


def per_device(
    tokens,
    input_proj,
    step_proj,
    conv_weight,
    conv_bias,
    step_bias,
    head_rate,
    state_pool,
    resume_slot,
    offsets,
):
    answers, length, model_width = tokens.shape
    channels = input_proj.shape[1]
    heads_here = step_proj.shape[1]
    group_width = GROUP_HEADS * P_SIZE + N
    groups_here = channels // group_width
    ctx_index = lax.axis_index("ctx")
    margin = 0
    window = length + margin
    flattened = tokens.reshape(answers * window, model_width)
    projection_total, step_sum = folder(
        flattened,
        (
            lax.all_gather(input_proj, ("dp", "ctx"), axis=0, tiled=True),
            lax.all_gather(step_proj, ("dp", "ctx"), axis=0, tiled=True),
        ),
    )
    projected = projection_total.astype(jnp.bfloat16).reshape(answers, window, channels)
    step_raw = step_sum.reshape(answers, window, heads_here)
    token_places = ctx_index * length - margin + jnp.arange(window, dtype=jnp.int32)
    is_valid = token_places[None, :] >= offsets[:, None]
    masked = jnp.where(is_valid[:, :, None], projected, jnp.zeros_like(projected))
    rim_rows = from_behind(masked[:, length - 3 :, :], "ctx", 1)
    lengthened = jnp.concatenate([rim_rows, masked], axis=1)
    widened = lengthened.astype(jnp.float32)
    convolved = conv_bias + jnp.zeros((answers, length, channels), jnp.float32)
    for tap_index in range(4):
        convolved = convolved + conv_weight[tap_index] * widened[:, tap_index : tap_index + length]
    activated = jax.nn.silu(convolved).astype(jnp.bfloat16)
    own_valid = is_valid.astype(jnp.float32)
    step_size = jax.nn.softplus(step_raw + step_bias) * own_valid[:, :, None]
    log_decay = -head_rate * step_size
    running_total = jnp.cumsum(log_decay, axis=1)
    shard_total = running_total[:, -1]
    weight = jnp.exp(shard_total[:, None] - running_total) * step_size
    group_sorted = activated.reshape(answers, length, groups_here, group_width)
    head_inputs = group_sorted[..., : GROUP_HEADS * P_SIZE].reshape(
        answers, length, groups_here, GROUP_HEADS, P_SIZE
    )
    state_inputs = group_sorted[..., GROUP_HEADS * P_SIZE :]
    scaled = (
        head_inputs.astype(jnp.float32)
        * weight.reshape(answers, length, groups_here, GROUP_HEADS, 1)
    ).astype(jnp.bfloat16)
    within_segment_addend = jnp.einsum(
        "rlghp,rlgn->rghpn", scaled, state_inputs, preferred_element_type=jnp.float32
    )
    within_segment_addend = within_segment_addend.reshape(answers, heads_here * P_SIZE, N)
    factor_rows = jnp.repeat(jnp.exp(shard_total), P_SIZE, axis=1)
    piece = lax.all_gather(state_pool, "dp", axis=0, tiled=True)
    piece_rows = piece.shape[0]
    selector = (resume_slot[:, None] == jnp.arange(piece_rows, dtype=jnp.int32)[None, :]).astype(
        jnp.bfloat16
    )
    initial = jnp.einsum("rk,kqn->rqn", selector, piece, preferred_element_type=jnp.float32)
    prefix_decay, leading_contribution = prefix(
        (factor_rows, within_segment_addend),
        "ctx",
        combine,
        (jnp.ones_like(factor_rows), jnp.zeros_like(within_segment_addend)),
    )
    incoming = prefix_decay[:, :, None] * initial + leading_contribution
    split_point = factor_rows[:, :, None] * incoming + within_segment_addend
    return split_point[:, None]


def solution(mesh):
    return jax.shard_map(
        per_device,
        mesh=mesh,
        in_specs=(
            P("dp", "ctx", None),
            P(("dp", "ctx"), "tensor"),
            P(("dp", "ctx"), "tensor"),
            P(None, "tensor"),
            P("tensor"),
            P("tensor"),
            P("tensor"),
            P("dp", "tensor", None),
            P("dp"),
            P("dp"),
        ),
        out_specs=P("dp", "ctx", "tensor", None),
        check_vma=False,
    )
```

profile of v0, /device:TPU:64, one launch (start us, length us, event | category | flops | bytes accessed | tf_op | source)
XLA Modules:
  0.0 581.7 jit_solution(15660971284029664115)
XLA Ops:
  6.5 0.0 all-gather.4.cloned.1.call-start
  6.5 0.7 all-gather.4.cloned.1.call-update
  7.3 0.0 all-gather.8.cloned.1.call-start
  7.3 0.7 all-gather.8.cloned.1.call-update
  8.0 0.0 all-gather.6.cloned.1.call-start
  8.7 0.7 neg.12
  9.4 94.0 %all_gather.15 = bf16[8192,32]{0,1:T(8,128)(2,1)S(1)} all-gather(bf16[256,32]{0,1:T(8,128)(2,1)} %param.14), channel_id=1, replica_groups=mesh['dp'=8,'ctx'=4,'tensor'=4] {'dp','ctx'}, dimensions={0}, use_global_device_ids=true | all-gather | bytes 540672 | tf_op jit(solution)/shard_map/all_gather | solution.py:66
  103.4 6.0 %fusion.26 = f32[512,32]{0,1:T(8,128)S(1)} fusion(bf16[8192,32]{0,1:T(8,128)(2,1)S(1)} %all_gather.15, bf16[1,512,8192]{2,1,0:T(8,128)(2,1)} %param.12, f32[512]{0:T(512)S(1)} %get-tuple-element.59, f32[32]{0:T(128)} %param.17), kind=kOutput, calls=%fused_computation.33 | convolution fusion | flops 268566528 | bytes 8980608 | tf_op jit(solution)/shard_map/dot_general | solution.py:33
  109.4 0.1 copy_bitcast_fusion
  109.5 1.1 reduce-window.6
  110.6 0.2 slice_reduce_fusion
  110.8 0.1 copy.23
  110.9 0.1 broadcast.69
  111.1 0.2 slice_reduce_fusion.1
  111.3 0.1 fusion.28
  111.4 186.9 %all-gather.4.cloned.1.call-done = bf16[8192,2304]{1,0:T(8,128)(2,1)} async-done(((bf16[256,2304]{1,0:T(8,128)(2,1)}), bf16[8192,2304]{1,0:T(8,128)(2,1)}) %all-gather.4.cloned.1.call-update) | async-done | bytes 37748752 | tf_op jit(solution)/shard_map/all_gather | solution.py:65
  298.3 0.0 copy-start.1
  298.3 27.0 %fusion.16 = bf16[1,512,2304]{2,1,0:T(8,128)(2,1)S(1)} fusion(bf16[8192,2304]{1,0:T(8,128)(2,1)} %all-gather.4.cloned.1.call-done, bf16[1,512,8192]{2,1,0:T(8,128)(2,1)} %param.12, pred[512]{0:T(512)(128)(4,1)S(1)} %get-tuple-element.60), kind=kOutput, calls=%fused_computation.21 | convolution fusion | flops 19329712128 | bytes 48497152 | tf_op jit(solution)/shard_map/dot_general | solution.py:32
  325.3 3.3 collective-permute-start
  328.6 0.0 copy-done.1
  328.7 0.1 slice_reduce_fusion.5
  328.8 2.5 mul.145
  331.2 5.4 copy.24
  336.6 0.0 copy-start.2
  336.6 0.0 collective-permute-done
  336.6 0.5 maximum_convert_fusion
  337.1 0.2 copy-done.2
  337.3 0.0 copy-start
  337.3 3.0 fusion.19
  340.4 0.0 copy-done
  340.4 2.0 multiply_convert_fusion.1
  342.3 3.9 copy.25
  346.3 3.6 fusion.25
  349.9 0.0 all-gather.6.cloned.1.call-update
  349.9 0.1 broadcast_in_dim.38
  350.0 0.1 broadcast_in_dim.42
  350.1 0.1 broadcast_in_dim.39
  350.8 10.7 %all_gather.16 = f32[4,1,2048]{2,1,0:T(1,128)S(1)} all-gather(f32[1,1,2048]{2,1,0:T(1,128)S(1)} %broadcast_in_dim.42), channel_id=1, replica_groups=mesh['dp'=8,'ctx'=4,'tensor'=4] {'ctx'}, dimensions={0}, use_global_device_ids=true | all-gather | bytes 40960 | tf_op jit(solution)/shard_map/all_gather | solution.py:19
  361.5 123.0 %all-gather.8.cloned.1.call-done = bf16[16,2048,256]{2,1,0:T(8,128)(2,1)} async-done(((bf16[2,2048,256]{2,1,0:T(8,128)(2,1)}), bf16[16,2048,256]{2,1,0:T(8,128)(2,1)}) %all-gather.8.cloned.1.call-update) | async-done | bytes 16777232 | tf_op jit(solution)/shard_map/all_gather | solution.py:101
  484.5 16.9 %fusion = f32[1,2048,256]{2,0,1:T(1,128)} fusion(bf16[16,2048,256]{2,1,0:T(8,128)(2,1)} %all-gather.8.cloned.1.call-done, s32[]{:T(128)} %bitcast.90), kind=kOutput, calls=%fused_computation.3 | convolution fusion | flops 16777232 | bytes 18874372 | tf_op jit(solution)/shard_map/rk,kqn->rqn/dot_general | solution.py:106
  501.4 65.6 %all-gather.6.cloned.1.call-done = f32[4,1,2048,256]{3,2,1,0:T(8,128)} async-done(((f32[1,1,2048,256]{3,2,1,0:T(8,128)}), f32[4,1,2048,256]{3,2,1,0:T(8,128)}) %all-gather.6.cloned.1.call-update) | async-done | bytes 8388624 | tf_op jit(solution)/shard_map/all_gather | solution.py:19
  567.0 0.1 broadcast_in_dim.41
  567.2 4.3 while.12
  567.2 2.1 bitcast_add_fusion.5
  569.4 2.1 bitcast_add_fusion.5
  571.5 3.6 fusion.20
  (10 shorter events, 0.2 us)
Async XLA Ops:
  6.5 291.7 %all-gather.4.cloned.1.call-start = ((), (), s32[]{:S(2)}) async-start(), calls=%async_computation | async-start | bytes 38928384 | tf_op jit(solution)/shard_map/all_gather | solution.py:65
  7.3 477.2 %all-gather.8.cloned.1.call-start = ((), (), s32[]{:S(2)}) async-start(), calls=%async_computation.2 | async-start | bytes 18874368 | tf_op jit(solution)/shard_map/all_gather | solution.py:101
  8.0 559.0 %all-gather.6.cloned.1.call-start = ((), (), s32[]{:S(2)}) async-start(), calls=%async_computation.1 | async-start | bytes 10485760 | tf_op jit(solution)/shard_map/all_gather | solution.py:19
  298.3 30.4 %copy-start.1 = (f32[4,2304]{1,0:T(4,128)S(1)}, f32[4,2304]{1,0:T(4,128)}, u32[]{:S(2)}) copy-start(f32[4,2304]{1,0:T(4,128)} %param.15) | copy-start | bytes 110596
  325.3 11.3 %collective-permute-start = (bf16[1,3,2304]{2,1,0:T(4,128)(2,1)S(1)}, bf16[1,3,2304]{2,1,0:T(4,128)(2,1)S(1)}, u32[]{:S(2)}, u32[]{:S(2)}) collective-permute-start(bf16[1,3,2304]{2,1,0:T(4,128)(2,1)S(1)} %slice.58), channel_id=1, source_target_pairs={{0,4},{4,8},{8,12},{1,5},{5,9},{9,13},{2,6},{6,10},{10,14},{3,7},{... | collective-permute-start | bytes 41480 | tf_op jit(solution)/shard_map/ppermute | solution.py:14
  336.6 0.7 copy-start.2
  337.3 3.0 copy-start
Sparse Core Ops, SparseCore 0:
  10.3 287.9 all-gather.3
  300.6 183.8 all-gather.7
  486.2 80.8 all-gather.5
where the time goes:
time: 583 us; the launch traced here: 582 us
  waiting for transfers between devices  377 us (65%)
  blocking collectives  105 us (18%)
  matrix products  53.6 us (9%)
  other arithmetic  15.3 us (3%)
  between operations  14.6 us (3%)
  local copies, waits for them, and re-layouts  13.1 us (2%)
    all_gather x1, waiting for transfers between devices, per_device(): lax.all_gather(input_proj, ('dp', 'ctx'), axis=0, tiled=True)  187 us
    all_gather x1, waiting for transfers between devices, per_device(): piece = lax.all_gather(state_pool, 'dp', axis=0, tiled=True)  123 us
    all_gather x1, blocking collectives, per_device(): lax.all_gather(step_proj, ('dp', 'ctx'), axis=0, tiled=True)  94 us
    all_gather x1, waiting for transfers between devices, prefix(): gathered = jax.tree.map(lambda a: lax.all_gather(a, axis), part)  65.6 us
    dot_general x1, matrix products, folder(): jnp.dot(matrix, pieces[0], preferred_element_type=jnp.float32)  27 us
    dot_general x1, matrix products, per_device(): jnp.einsum('rk,kqn->rqn', selector, piece, preferred_element_type=jnp.flo...  16.9 us
  transfers between devices with their start and end apart: 4, of which 3 were waited for; matrix products, arithmetic and copies ran while one was open for 13% of the time, Pallas kernels for 0%

commit v1 on v0

v1 whole, which is shorter than its diff:
```python
import jax
import jax.numpy as jnp
from jax import lax
from jax.experimental import pallas as pl
from jax.experimental.pallas import tpu as pltpu
from jax.sharding import Mesh
from jax.sharding import PartitionSpec as P

GROUP_HEADS = 32
P_SIZE = 64
N = 256
HALO = 16
ROWS = 512
LONG = ROWS + HALO
PIECE = 256
HALF = 4096
HEAD_COLUMNS = GROUP_HEADS * P_SIZE
F32 = jnp.float32
BF16 = jnp.bfloat16
VMEM_LIMIT = 48 * 1024 * 1024
VMEM = pl.BlockSpec(memory_space=pltpu.VMEM)
SMEM = pl.BlockSpec(memory_space=pltpu.SMEM)
ANY = pl.BlockSpec(memory_space=pltpu.HBM)

CHUNKS = {
    "states": (HEAD_COLUMNS, 256),
    "a": (0, 512),
    "b": (512, 512),
    "c": (1024, 512),
    "d": (1536, 512),
}


def together(*values):
    return lax.optimization_barrier(values)


def shifted(part, axis, by):
    return lax.ppermute(part, axis, [(i, (i + by) % 4) for i in range(4)])


def ring_places():
    x, z = lax.axis_index("x"), lax.axis_index("z")
    index = jnp.arange(16, dtype=jnp.int32)
    step = lambda i: jnp.where(i == 1, 3, jnp.where(i == 2, 1, jnp.where(i == 3, 2, 0)))
    outer, inner = step(index // 4), step(index % 4)
    return (x + inner) % 4 * 4 + (z + outer) % 4, index


def params():
    return pltpu.CompilerParams(vmem_limit_bytes=VMEM_LIMIT)


def pile(parts):
    width = parts[0].shape[1]
    heights = [part.shape[0] for part in parts]

    def kernel(*refs):
        copies = [
            pltpu.make_async_copy(ref, refs[len(parts)].at[pl.ds(sum(heights[:i]), heights[i])], refs[-1].at[i])
            for i, ref in enumerate(refs[: len(parts)])
        ]
        for copy in copies:
            copy.start()
        for copy in copies:
            copy.wait()

    whole = (sum(heights), width)
    return pl.pallas_call(
        kernel,
        out_shape=jax.ShapeDtypeStruct(whole, parts[0].dtype),
        in_specs=[ANY] * len(parts),
        out_specs=VMEM,
        scratch_shapes=[pltpu.SemaphoreType.DMA((len(parts),))],
        compiler_params=params(),
        cost_estimate=pl.CostEstimate(flops=0, bytes_accessed=4 * whole[0] * width, transcendentals=0),
        name="pile",
    )(*parts)


def cut(rows, first, width, pool=None, row=None):
    def kernel(at_ref, rows_ref, *refs):
        out, sems = refs[-2:]
        parts = [(rows_ref.at[:, pl.ds(pl.multiple_of(at_ref[0], PIECE), width)], out.at[:, pl.ds(0, width)])]
        if pool is not None:
            for slot in range(2):
                source = refs[0].at[slot, pl.ds(pl.multiple_of(at_ref[1], 512), 512)]
                parts.append((source, out.at[:, pl.ds(width + slot * N, N)]))
        copies = [pltpu.make_async_copy(source, target, sems.at[i]) for i, (source, target) in enumerate(parts)]
        for copy in copies:
            copy.start()
        for copy in copies:
            copy.wait()

    with_pool = pool is not None
    whole = width + 2 * N if with_pool else width
    return pl.pallas_call(
        kernel,
        out_shape=jax.ShapeDtypeStruct((rows.shape[0], whole), rows.dtype),
        in_specs=[SMEM, ANY] + [ANY] * with_pool,
        out_specs=VMEM,
        scratch_shapes=[pltpu.SemaphoreType.DMA((3,))],
        compiler_params=params(),
        cost_estimate=pl.CostEstimate(flops=0, bytes_accessed=4 * rows.shape[0] * whole, transcendentals=0),
        name="cut",
    )(jnp.stack([first, row if with_pool else first]).astype(jnp.int32), rows, *([pool] if with_pool else []))


NEAR = (768, 1280)


def in_blocks(name, pick, halo, at, *sources):
    def kernel(at_ref, halo_ref, *refs):
        out_ref, sems = refs[len(sources) :]
        parts = [(halo_ref, out_ref.at[:, pl.ds(0, HALO)])]
        for i in range(16):
            source, place = pick(at_ref, refs, i)
            parts.append((source, out_ref.at[place, pl.ds(HALO, ROWS)]))
        copies = [pltpu.make_async_copy(source, target, sems.at[i]) for i, (source, target) in enumerate(parts)]
        for copy in copies:
            copy.start()
        for copy in copies:
            copy.wait()

    return pl.pallas_call(
        kernel,
        out_shape=jax.ShapeDtypeStruct((16, LONG, PIECE), halo.dtype),
        in_specs=[SMEM] + [ANY] * (1 + len(sources)),
        out_specs=VMEM,
        scratch_shapes=[pltpu.SemaphoreType.DMA((17,))],
        compiler_params=params(),
        cost_estimate=pl.CostEstimate(flops=0, bytes_accessed=4 * LONG * HALF, transcendentals=0),
        name=name,
    )(at[None].astype(jnp.int32), halo, *sources)


def own_tokens(rows, halo):
    def pick(at_ref, refs, i):
        return refs[0].at[:, pl.ds(pl.multiple_of(at_ref[0] * HALF + i * PIECE, PIECE), PIECE)], i

    return in_blocks("own_tokens", pick, halo, lax.axis_index("yh"), rows)


def partner_tokens(nears, fars, halo):
    def pick(at_ref, refs, i):
        place = at_ref[0] * 8 + i if i < 8 else (1 - at_ref[0]) * 8 + i - 8
        begin, piece = i % 8 * PIECE, 0
        if begin >= NEAR[0]:
            begin, piece = begin - NEAR[0], 1
        return refs[i // 8 * 2 + piece].at[:, pl.ds(begin, PIECE)], place

    return in_blocks("partner_tokens", pick, halo, lax.axis_index("core"), *nears, *fars)


def project(own, theirs, blocks, places, first, width, steps):
    n_blocks = len(blocks)

    def kernel(places_ref, *refs):
        sides, w_refs, outs, refs = refs[:2], refs[2 : 2 + n_blocks], refs[2 + n_blocks : 4 + n_blocks], refs[4 + n_blocks :]
        accs, held, sems = refs[:2], refs[2], refs[3]
        copies = []
        for j in range(4):
            row = pl.ds(j * 1024, 1024)
            source = w_refs[0].at[row, pl.ds(first, width)] if n_blocks == 1 else w_refs[j]
            copies.append(pltpu.make_async_copy(source, held.at[row], sems.at[j]))
            copies[j].start()
        for j in range(4):
            copies[j].wait()
            w = held[j * 1024 : (j + 1) * 1024]
            for side in range(2):
                lhs = jnp.concatenate([sides[side][places_ref[4 * j + i]] for i in range(4)], axis=1)
                product = jnp.dot(lhs, w, preferred_element_type=F32)
                if j == 0:
                    accs[side][...] = product
                elif j < 3:
                    accs[side][...] += product
                elif side == 0:
                    outs[0][...] = accs[0][...] + product
                else:
                    total = accs[1][...] + product
                    if steps:
                        outs[1][:, :N] = total[:, :N].astype(BF16)
                        exact = total[:, N:]
                        high = exact.astype(BF16)
                        outs[1][:, N : N + 128] = high
                        outs[1][:, N + 128 :] = (exact - high.astype(F32)).astype(BF16)
                    else:
                        outs[1][...] = total.astype(BF16)

    their_width = width + 128 if steps else width
    return pl.pallas_call(
        kernel,
        out_shape=(jax.ShapeDtypeStruct((LONG, width), F32), jax.ShapeDtypeStruct((LONG, their_width), BF16)),
        in_specs=[SMEM, VMEM, VMEM] + [ANY] * n_blocks,
        out_specs=(VMEM, VMEM),
        scratch_shapes=[pltpu.VMEM((LONG, width), F32)] * 2 + [pltpu.VMEM((HALF, width), BF16), pltpu.SemaphoreType.DMA((4,))],
        compiler_params=params(),
        cost_estimate=pl.CostEstimate(flops=4 * LONG * HALF * width, bytes_accessed=8192 * width, transcendentals=0),
        name="project",
    )(places, own, theirs, *blocks)


def activate(info_ref, projected, taps_ref, bias_ref, first, masked):
    projected = projected.astype(BF16).astype(F32)
    place = info_ref[0] + lax.broadcasted_iota(jnp.int32, projected.shape, 0)
    masked[...] = jnp.where(place >= info_ref[1], projected, 0.0)
    columns = slice(first, first + projected.shape[1])
    total = bias_ref[:, columns]
    for k in range(4):
        total = total + taps_ref[k : k + 1, columns] * masked[pl.ds(HALO - 3 + k, ROWS), :]
    return (total * jax.nn.sigmoid(total)).astype(BF16)


def state_kernel(info_ref, own_ref, other_ref, taps_ref, bias_ref, states_out, steps_out, masked):
    projected = own_ref[:, :N] + other_ref[:, :N].astype(F32)
    states_out[...] = activate(info_ref, projected, taps_ref, bias_ref, HEAD_COLUMNS, masked)
    steps = own_ref[HALO:, N : N + 128] + other_ref[HALO:, N : N + 128].astype(F32) + other_ref[HALO:, N + 128 :].astype(F32)
    steps_out[...] = steps[:, :GROUP_HEADS]


def head_kernel(first_head, info_ref, own_ref, other_ref, taps_ref, bias_ref, weight_ref, states_ref, out_ref, masked):
    projected = own_ref[...] + other_ref[...].astype(F32)
    activated = activate(info_ref, projected, taps_ref, bias_ref, first_head * P_SIZE, masked).astype(F32)
    lane = lax.broadcasted_iota(jnp.int32, (ROWS, 128), 1)
    scaled = []
    for i in range(activated.shape[1] // 128):
        head = first_head + 2 * i
        factor = jnp.where(lane < P_SIZE, weight_ref[:, head : head + 1], weight_ref[:, head + 1 : head + 2])
        scaled.append((activated[:, i * 128 : (i + 1) * 128] * factor).astype(BF16))
    scaled = jnp.concatenate(scaled, axis=1)
    out_ref[...] = lax.dot_general(scaled, states_ref[...], (((0,), (0,)), ((), ())), preferred_element_type=F32)


def call(kernel, out, width, *args):
    return pl.pallas_call(
        kernel,
        out_shape=out,
        in_specs=[SMEM] + [VMEM] * (len(args) - 1),
        out_specs=jax.tree.map(lambda _: VMEM, out),
        scratch_shapes=[pltpu.VMEM((LONG, width), F32)],
        compiler_params=params(),
        cost_estimate=pl.CostEstimate(flops=2 * ROWS * N * width, bytes_accessed=8 * LONG * width, transcendentals=ROWS * width),
        name="activate",
    )(*args)


def swap(value, axis):
    return lax.ppermute(value, axis, [(0, 1), (1, 0)])


def halos(rows):
    yh = lax.axis_index("yh")
    last = rows[ROWS - HALO :].reshape(HALO, 2, 16, PIECE).transpose(1, 2, 0, 3)
    mine = lax.ppermute(lax.dynamic_index_in_dim(last, yh, 0, False), "z", [(0, 1), (1, 2), (2, 3)])
    pairs = [(y * 4 + z, (1 - y) * 4 + z + 1) for y in range(2) for z in range(3)]
    return mine, lax.ppermute(lax.dynamic_index_in_dim(last, 1 - yh, 0, False), ("yh", "z"), pairs)


def behind(value, by):
    return lax.ppermute(value, "z", [(i, i + by) for i in range(4 - by)])


def saved_state(near, far, wanted):
    yh, x = lax.axis_index("yh"), lax.axis_index("x")
    slots = []
    for side, value in ((yh, near), (1 - yh, far)):
        for b in range(2):
            slots.append((2 * (side * 4 + x) + b, value[:, NEAR[1] + b * N : NEAR[1] + (b + 1) * N]))
    sent = []
    for i in range(4):
        picked = jnp.zeros((512, N), BF16)
        for slot, value in slots:
            picked = jnp.where(wanted[i] == slot, value, picked)
        sent.append(picked)
    return sent


def per_device(tokens, input_proj, step_proj, conv_weight, conv_bias, step_bias, head_rate, state_pool, resume_slot, offsets):
    yh, x, z, core = (lax.axis_index(a) for a in ("yh", "x", "z", "core"))
    rows = tokens[0]
    info = jnp.stack([z * ROWS - HALO, offsets[0]]).astype(jnp.int32)

    x_first, in_order = together(*ring_places())
    slot = jnp.broadcast_to(resume_slot[0].astype(BF16), (PIECE, 1))
    s = jnp.concatenate([input_proj[:, HEAD_COLUMNS:], step_proj, slot, jnp.zeros((PIECE, 95), BF16)], axis=1)
    half = (1 - yh) * HALF + core * 2048
    gathered = lax.all_gather(input_proj[:, :HEAD_COLUMNS], ("x", "z"), axis=0, tiled=True)

    first_piece = cut(rows, half, NEAR[0])
    s, first_piece = together(s, first_piece)
    first_near = swap(first_piece, "yh")
    second_piece = cut(rows, half + NEAR[0], NEAR[1], state_pool, z * 512)
    around = [shifted(s, "x", by) for by in (1, -1, 2)]
    my_halo, their_halo = halos(rows)
    *around, first_near, second_piece, my_halo, their_halo = together(*around, first_near, second_piece, my_halo, their_halo)
    second_near = swap(second_piece, "yh")
    s = pile([s, *around])
    around = [shifted(s, "z", by) for by in (1, -1, 2)]
    first_far = swap(first_near, "core")
    own_side = own_tokens(rows, my_halo)
    s, *around, second_near, first_far, own_side = together(s, *around, second_near, first_far, own_side)
    s = [s, *around]
    second_far = swap(second_near[:, : NEAR[1]], "core")
    partner_side = partner_tokens((first_near, second_near), (first_far, second_far), their_halo)
    projected = {}

    def run(name, blocks, places):
        first, width = CHUNKS[name]
        steps = name == "states"
        own, sent = project(own_side, partner_side, blocks, places, first, width + 128 if steps else width, steps)
        projected[name] = [own, swap(sent, "yh")]

    run("states", s, x_first)
    wanted = [s[0][PIECE * i, N + GROUP_HEADS].astype(jnp.int32) for i in (0, 2, 3, 1)]
    picked = saved_state(second_piece, second_near, wanted)
    found = [picked[0]] + [shifted(picked[i], "x", i) for i in (1, 2, 3)]
    out = (jax.ShapeDtypeStruct((ROWS, N), BF16), jax.ShapeDtypeStruct((ROWS, GROUP_HEADS), F32))
    states, step_raw = call(state_kernel, out, N, info, *projected["states"], conv_weight, conv_bias[None])

    valid = (z * ROWS + jnp.arange(ROWS, dtype=jnp.int32) >= offsets[0]).astype(F32)
    step_size = jax.nn.softplus(step_raw + step_bias) * valid[:, None]
    log_decay = -head_rate * step_size
    running = jnp.cumsum(log_decay, axis=0)
    weight = jnp.exp(running[-1:] - running) * step_size
    decay = jnp.exp(running[-1])
    before = behind(decay, 1)
    factors = [jnp.repeat(f, P_SIZE)[:, None] for f in (decay, decay * before)]

    found = found[0] + found[1] + found[2] + found[3]
    initial = jnp.concatenate([found] + [lax.ppermute(found, "z", [(k, 0)]) for k in (1, 2, 3)], axis=0)
    start = jnp.where(z == 0, factors[0] * initial.astype(F32), 0.0)
    gathered, weight, states, start, *factors = together(gathered, weight, states, start, *factors)

    def head(name):
        first, width = CHUNKS[name]
        kernel = lambda *refs: head_kernel(first // P_SIZE, *refs)
        out = jax.ShapeDtypeStruct((width, N), F32)
        return call(kernel, out, width, info, *projected[name], conv_weight, conv_bias[None], weight, states)

    local = {}
    run("a", [gathered], in_order)
    run("b", [gathered], in_order)
    gathered, projected["a"][1] = together(gathered, projected["a"][1])
    run("c", [gathered], in_order)
    projected["a"][0], projected["c"][0] = together(projected["a"][0], projected["c"][0])
    local["a"] = head("a")
    gathered, projected["b"][1], local["a"] = together(gathered, projected["b"][1], local["a"])
    run("d", [gathered], in_order)
    projected["b"][0], projected["d"][0], local["a"] = together(projected["b"][0], projected["d"][0], local["a"])
    local["b"] = head("b")
    result = []
    for names in (("a", "b"), ("c",), ("d",)):
        first = CHUNKS[names[0]][0]
        last = first + sum(CHUNKS[name][1] for name in names)
        own = jnp.concatenate([local[name] if name in local else head(name) for name in names], axis=0) + start[first:last]
        for factor, by in zip(factors, (1, 2)):
            own = own + factor[first:last] * behind(own.astype(BF16), by).astype(F32)
        result.append(own)
    return jnp.concatenate(result, axis=0)[None, None]


def solution(mesh):
    fine = Mesh(mesh.devices.reshape(2, 4, 4, 2, 2), ("yh", "x", "z", "yl", "core"))
    dp, tensor = ("yh", "x"), ("yl", "core")
    return jax.shard_map(
        per_device,
        mesh=fine,
        in_specs=(
            P(dp, "z", None),
            P(dp + ("z",), tensor),
            P(dp + ("z",), tensor),
            P(None, tensor),
            P(tensor),
            P(tensor),
            P(tensor),
            P(dp, tensor, None),
            P(dp),
            P(dp),
        ),
        out_specs=P(dp, "z", tensor, None),
        check_vma=False,
    )
```

time: 583 us -> 279 us (0.48)
  waiting for transfers between devices: 377 us -> 106 us
  blocking collectives: 105 us -> 0 us
  Pallas kernels: 0 us -> 65.8 us
  starting transfers between devices: 3.43 us -> 57.9 us
  matrix products: 53.6 us -> 0 us
    all_gather x3 -> x1, waiting for transfers between devices: 375 us -> 0.02 us  [per_device(): lax.all_gather(input_proj[:, :HEAD_COLUMNS], ('x', 'z'), axis=0, tiled=True)]
    ppermute x1 -> x30, waiting for transfers between devices: 0.01 us -> 106 us  [the longest x9 64.6 us: shifted(): return lax.ppermute(part, axis, [(i, (i + by) % 4) for i in range(4)])]
    all_gather x2 -> x0, blocking collectives: 105 us -> none  [the longest x1 94 us: per_device(): lax.all_gather(step_proj, ('dp', 'ctx'), axis=0, tiled=True)]
    pallas_call x0 -> x15, Pallas kernels: none -> 65.8 us  [the longest x5 44.3 us: project(): pl.pallas_call(kernel, out_shape=(jax.ShapeDtypeStruct((LONG, width), F32...]
    ppermute x1 -> x30, starting transfers between devices: 3.35 us -> 57.9 us  [the longest x7 21 us: behind(): return lax.ppermute(value, 'z', [(i, i + by) for i in range(4 - by)])]
    dot_general x4 -> x0, matrix products: 53.6 us -> none  [the longest x1 27 us: folder(): jnp.dot(matrix, pieces[0], preferred_element_type=jnp.float32)]
    unnamed x6 -> x60, local copies, waits for them, and re-layouts: 0.24 us -> 10.4 us
    mul x2 -> x1, local copies, waits for them, and re-layouts: 7.87 us -> 0.07 us  [per_device(): start = jnp.where(z == 0, factors[0] * initial.astype(F32), 0.0)]
  transfers between devices with their start and end apart: 4 -> 31, of which waited for: 3 -> 14; matrix products, arithmetic and copies ran while one was open for 13% -> 6% of each run, Pallas kernels for 0% -> 21%
where the time goes in v1:
time: 279 us; the launch traced here: 278 us
  waiting for transfers between devices  106 us (38%)
  Pallas kernels  65.8 us (24%)
  starting transfers between devices  57.9 us (21%)
  between operations  18.3 us (7%)
  local copies, waits for them, and re-layouts  18 us (6%)
  other arithmetic  11.8 us (4%)
    ppermute x9, waiting for transfers between devices, shifted(): return lax.ppermute(part, axis, [(i, (i + by) % 4) for i in range(4)])  64.6 us
    pallas_call x5, Pallas kernels, project(): pl.pallas_call(kernel, out_shape=(jax.ShapeDtypeStruct((LONG, width), F32...  44.3 us
    ppermute x7, waiting for transfers between devices, behind(): return lax.ppermute(value, 'z', [(i, i + by) for i in range(4 - by)])  31.7 us
    ppermute x7, starting transfers between devices, behind(): return lax.ppermute(value, 'z', [(i, i + by) for i in range(4 - by)])  21 us
    ppermute x9, starting transfers between devices, swap(): return lax.ppermute(value, axis, [(0, 1), (1, 0)])  14.1 us
    ppermute x9, starting transfers between devices, shifted(): return lax.ppermute(part, axis, [(i, (i + by) % 4) for i in range(4)])  11.4 us
    unnamed x60, local copies, waits for them, and re-layouts  10.4 us
    pallas_call x5, Pallas kernels, call(): pl.pallas_call(kernel, out_shape=out, in_specs=[SMEM] + [VMEM] * (len(arg...  9.62 us
  transfers between devices with their start and end apart: 31, of which 14 were waited for; matrix products, arithmetic and copies ran while one was open for 6% of the time, Pallas kernels for 21%

profile of v1, /device:TPU:64, one launch (start us, length us, event | category | flops | bytes accessed | tf_op | source)
XLA Modules:
  0.0 278.0 jit_solution(11807728249397972323)
XLA Ops:
  6.5 2.3 slice.77
  9.9 2.6 cut.2
  12.7 3.3 %collective-permute-start.3 = (bf16[512,768]{1,0:T(8,128)(2,1)}, bf16[512,768]{1,0:T(8,128)(2,1)S(1)}, u32[]{:S(2)}, u32[]{:S(2)}) collective-permute-start(bf16[512,768]{1,0:T(8,128)(2,1)} %cut.2), channel_id=1, source_target_pairs={{0,64},{64,0},{1,65},{65,1},{2,66},{66,2},{3,67},{67,3},{4,68},{68... | collective-permute-start | bytes 2359304 | tf_op jit(solution)/shard_map/ppermute | solution.py:248
  15.9 1.7 slice.75
  18.7 3.5 %collective-permute-start.4 = (bf16[16,16,256]{2,1,0:T(8,128)(2,1)S(1)}, bf16[16,16,256]{2,1,0:T(8,128)(2,1)S(1)}, u32[]{:S(2)}, u32[]{:S(2)}) collective-permute-start(bf16[16,16,256]{2,1,0:T(8,128)(2,1)S(1)} %bitcast.64), channel_id=1, source_target_pairs={{0,4},{4,8},{8,12},{1,5},{5,9},{9,13},{2,6},{6,10},{10,14},{3,7},{... | collective-permute-start | bytes 393224 | tf_op jit(solution)/shard_map/ppermute | solution.py:254
  23.8 1.7 collective-permute-start.1
  25.5 1.8 collective-permute-start.2
  29.0 1.9 collective-permute-start.5
  31.0 1.9 cut.3
  33.0 5.7 %collective-permute-done.5.halo_ref = bf16[16,16,256]{2,1,0:T(8,128)(2,1)} collective-permute-done((bf16[16,16,256]{2,1,0:T(8,128)(2,1)}, bf16[16,16,256]{2,1,0:T(8,128)(2,1)}, u32[]{:S(2)}, u32[]{:S(2)}) %collective-permute-start.5) | collective-permute-done | bytes 131104 | tf_op jit(solution)/shard_map/ppermute | solution.py:256
  38.7 5.6 %collective-permute-done.2.refs_3_ = bf16[256,384]{1,0:T(8,128)(2,1)} collective-permute-done((bf16[256,384]{1,0:T(8,128)(2,1)S(1)}, bf16[256,384]{1,0:T(8,128)(2,1)}, u32[]{:S(2)}, u32[]{:S(2)}) %collective-permute-start.2) | collective-permute-done | bytes 196640 | tf_op jit(solution)/shard_map/ppermute | solution.py:39
  44.3 1.7 pile.1.refs_2_
  46.1 2.0 collective-permute-start.7
  49.3 2.4 own_tokens.1.refs_0_
  51.7 2.0 copy-done
  53.8 20.8 %collective-permute-done.6.refs_3_ = bf16[1024,384]{1,0:T(8,128)(2,1)S(1)} collective-permute-done((bf16[1024,384]{1,0:T(8,128)(2,1)S(1)}, bf16[1024,384]{1,0:T(8,128)(2,1)S(1)}, u32[]{:S(2)}, u32[]{:S(2)}) %collective-permute-start.6) | collective-permute-done | bytes 786464 | tf_op jit(solution)/shard_map/ppermute | solution.py:39
  76.4 29.4 %collective-permute-done.8.refs_5_ = bf16[1024,384]{1,0:T(8,128)(2,1)S(1)} collective-permute-done((bf16[1024,384]{1,0:T(8,128)(2,1)S(1)}, bf16[1024,384]{1,0:T(8,128)(2,1)S(1)}, u32[]{:S(2)}, u32[]{:S(2)}) %collective-permute-start.8) | collective-permute-done | bytes 786464 | tf_op jit(solution)/shard_map/ppermute | solution.py:39
  112.3 2.0 select_select_fusion.2
  116.1 3.3 %partner_tokens.1.refs_1_ = bf16[16,528,256]{2,1,0:T(8,128)(2,1)} custom-call(s32[1]{0:T(128)} %bitcast.10.at_ref, bf16[16,16,256]{2,1,0:T(8,128)(2,1)} %collective-permute-done.5.halo_ref, bf16[512,768]{1,0:T(8,128)(2,1)S(1)} %copy-done.8, bf16[512,1792]{1,0:T(8,128)(2,1)S(1)} %collective-permute-done.9.refs_1_, bf16[512,768]{1,0:T(8,128)(2,1)S(1)} %copy-done.10, ...), custom_call_target="tpu_custom_call" | custom-call | bytes 8650752 | tf_op jit(solution)/shard_map/partner_tokens/pallas_call | solution.py:125
  119.5 9.8 %project.5 = (f32[528,384]{1,0:T(8,128)S(1)}, bf16[528,512]{1,0:T(8,128)(2,1)}) custom-call(s32[16]{0:T(128)S(1)} %fusion.5.places_ref, bf16[16,528,256]{2,1,0:T(8,128)(2,1)} %copy-done, bf16[16,528,256]{2,1,0:T(8,128)(2,1)} %partner_tokens.1.refs_1_, bf16[1024,384]{1,0:T(8,128)(2,1)S(1)} %copy-done.6, bf16[1024,384]{1,0:T(8,128)(2,1)S(1)} %copy-done.14, ...), custom_call_target="tpu_custom_call" | custom-call | flops 3321888768 | bytes 3145728 | tf_op jit(solution)/shard_map/project/pallas_call | solution.py:191
  129.3 3.2 %collective-permute-start.12 = (bf16[528,512]{1,0:T(8,128)(2,1)}, bf16[528,512]{1,0:T(8,128)(2,1)S(1)}, u32[]{:S(2)}, u32[]{:S(2)}) collective-permute-start(bf16[528,512]{1,0:T(8,128)(2,1)} %get-tuple-element.70), channel_id=1, source_target_pairs={{0,64},{64,0},{1,65},{65,1},{2,66},{66,2},{3,67},{67,3},{4,68},{68... | collective-permute-start | bytes 1622024 | tf_op jit(solution)/shard_map/ppermute | solution.py:248
  132.5 1.8 select_select_fusion
  137.1 3.1 %collective-permute-done.14 = bf16[512,256]{1,0:T(8,128)(2,1)} collective-permute-done((bf16[512,256]{1,0:T(8,128)(2,1)}, bf16[512,256]{1,0:T(8,128)(2,1)}, u32[]{:S(2)}, u32[]{:S(2)}) %collective-permute-start.14) | collective-permute-done | bytes 262176 | tf_op jit(solution)/shard_map/ppermute | solution.py:39
  140.2 5.7 %collective-permute-done.15 = bf16[512,256]{1,0:T(8,128)(2,1)} collective-permute-done((bf16[512,256]{1,0:T(8,128)(2,1)}, bf16[512,256]{1,0:T(8,128)(2,1)}, u32[]{:S(2)}, u32[]{:S(2)}) %collective-permute-start.15) | collective-permute-done | bytes 262176 | tf_op jit(solution)/shard_map/ppermute | solution.py:39
  147.9 4.6 %collective-permute-start.17 = (bf16[512,256]{1,0:T(8,128)(2,1)S(1)}, bf16[512,256]{1,0:T(8,128)(2,1)S(1)}, u32[]{:S(2)}, u32[]{:S(2)}) collective-permute-start(bf16[512,256]{1,0:T(8,128)(2,1)S(1)} %add_add_fusion), channel_id=1, source_target_pairs={{8,0},{9,1},{10,2},{11,3},{24,16},{25,17},{26,18},{27,19},{40,32},... | collective-permute-start | bytes 786440 | tf_op jit(solution)/shard_map/ppermute | solution.py:330
  156.4 3.9 %collective-permute-start.19 = (f32[32]{0:T(128)S(1)}, f32[32]{0:T(128)S(1)}, u32[]{:S(2)}, u32[]{:S(2)}) collective-permute-start(f32[32]{0:T(128)S(1)} %fusion.11), channel_id=1, source_target_pairs={{0,4},{4,8},{8,12},{1,5},{5,9},{9,13},{2,6},{6,10},{10,14},{3,7},{... | collective-permute-start | bytes 392 | tf_op jit(solution)/shard_map/ppermute | solution.py:260
  162.6 2.2 copy-done.1
  164.9 8.6 %project.7 = (f32[528,512]{1,0:T(8,128)S(1)}, bf16[528,512]{1,0:T(8,128)(2,1)S(1)}) custom-call(s32[16]{0:T(128)S(1)} %iota.14.places_ref, bf16[16,528,256]{2,1,0:T(8,128)(2,1)S(1)} %copy-done.1, bf16[16,528,256]{2,1,0:T(8,128)(2,1)} %partner_tokens.1.refs_1_, bf16[4096,2048]{1,0:T(8,128)(2,1)} %all-gather.2.cloned.1.call-done.refs_2_), custom_call_target="tpu_custom_call" | custom-call | flops 4429185024 | bytes 4194304 | tf_op jit(solution)/shard_map/project/pallas_call | solution.py:191
  173.5 1.8 collective-permute-start.20
  175.3 8.6 %project.6 = (f32[528,512]{1,0:T(8,128)S(1)}, bf16[528,512]{1,0:T(8,128)(2,1)S(1)}) custom-call(s32[16]{0:T(128)S(1)} %iota.14.places_ref, bf16[16,528,256]{2,1,0:T(8,128)(2,1)S(1)} %copy-done.1, bf16[16,528,256]{2,1,0:T(8,128)(2,1)} %partner_tokens.1.refs_1_, bf16[4096,2048]{1,0:T(8,128)(2,1)} %all-gather.2.cloned.1.call-done.refs_2_), custom_call_target="tpu_custom_call" | custom-call | flops 4429185024 | bytes 4194304 | tf_op jit(solution)/shard_map/project/pallas_call | solution.py:191
  183.9 1.9 collective-permute-start.21
  185.8 3.8 %collective-permute-done.20.refs_2_ = bf16[528,512]{1,0:T(8,128)(2,1)S(1)} collective-permute-done((bf16[528,512]{1,0:T(8,128)(2,1)S(1)}, bf16[528,512]{1,0:T(8,128)(2,1)S(1)}, u32[]{:S(2)}, u32[]{:S(2)}) %collective-permute-start.20) | collective-permute-done | bytes 540704 | tf_op jit(solution)/shard_map/ppermute | solution.py:248
  189.6 8.6 %project.8 = (f32[528,512]{1,0:T(8,128)S(1)}, bf16[528,512]{1,0:T(8,128)(2,1)S(1)}) custom-call(s32[16]{0:T(128)S(1)} %iota.14.places_ref, bf16[16,528,256]{2,1,0:T(8,128)(2,1)S(1)} %copy-done.1, bf16[16,528,256]{2,1,0:T(8,128)(2,1)} %partner_tokens.1.refs_1_, bf16[4096,2048]{1,0:T(8,128)(2,1)} %all-gather.2.cloned.1.call-done.refs_2_), custom_call_target="tpu_custom_call" | custom-call | flops 4429185024 | bytes 4194304 | tf_op jit(solution)/shard_map/project/pallas_call | solution.py:191
  198.2 2.1 collective-permute-start.24
  200.3 2.1 activate.6
  202.4 8.6 %project.9 = (f32[528,512]{1,0:T(8,128)S(1)}, bf16[528,512]{1,0:T(8,128)(2,1)S(1)}) custom-call(s32[16]{0:T(128)S(1)} %iota.14.places_ref, bf16[16,528,256]{2,1,0:T(8,128)(2,1)S(1)} %bitcast.54, bf16[16,528,256]{2,1,0:T(8,128)(2,1)} %partner_tokens.1.refs_1_, bf16[4096,2048]{1,0:T(8,128)(2,1)} %all-gather.2.cloned.1.call-done.refs_2_), custom_call_target="tpu_custom_call" | custom-call | flops 4429185024 | bytes 4194304 | tf_op jit(solution)/shard_map/project/pallas_call | solution.py:191
  211.1 1.8 collective-permute-start.27
  212.9 2.1 activate.7
  215.0 2.1 activate.8
  217.1 7.0 %collective-permute-start.25 = (bf16[512,256]{1,0:T(8,128)(2,1)S(1)}, bf16[512,256]{1,0:T(8,128)(2,1)S(1)}, u32[]{:S(2)}, u32[]{:S(2)}) collective-permute-start(bf16[512,256]{1,0:T(8,128)(2,1)S(1)} %fusion.13), channel_id=1, source_target_pairs={{0,4},{4,8},{8,12},{1,5},{5,9},{9,13},{2,6},{6,10},{10,14},{3,7},{... | collective-permute-start | bytes 786440 | tf_op jit(solution)/shard_map/ppermute | solution.py:260
  224.3 1.9 collective-permute-start.22
  226.3 2.1 activate.9
  228.3 2.5 collective-permute-done.25
  232.4 4.4 %collective-permute-start.28 = (bf16[512,256]{1,0:T(8,128)(2,1)S(1)}, bf16[512,256]{1,0:T(8,128)(2,1)S(1)}, u32[]{:S(2)}, u32[]{:S(2)}) collective-permute-start(bf16[512,256]{1,0:T(8,128)(2,1)S(1)} %get-tuple-element.102), channel_id=1, source_target_pairs={{0,4},{4,8},{8,12},{1,5},{5,9},{9,13},{2,6},{6,10},{10,14},{3,7},{... | collective-permute-start | bytes 786440 | tf_op jit(solution)/shard_map/ppermute | solution.py:260
  236.8 4.8 %collective-permute-done.22 = bf16[1024,256]{1,0:T(8,128)(2,1)S(1)} collective-permute-done((bf16[1024,256]{1,0:T(8,128)(2,1)S(1)}, bf16[1024,256]{1,0:T(8,128)(2,1)S(1)}, u32[]{:S(2)}, u32[]{:S(2)}) %collective-permute-start.22) | collective-permute-done | bytes 524320 | tf_op jit(solution)/shard_map/ppermute | solution.py:260
  243.2 6.9 %collective-permute-done.26 = bf16[512,256]{1,0:T(8,128)(2,1)S(1)} collective-permute-done((bf16[512,256]{1,0:T(8,128)(2,1)S(1)}, bf16[512,256]{1,0:T(8,128)(2,1)S(1)}, u32[]{:S(2)}, u32[]{:S(2)}) %collective-permute-start.26) | collective-permute-done | bytes 262176 | tf_op jit(solution)/shard_map/ppermute | solution.py:260
  251.7 15.0 %collective-permute-done.23 = bf16[1024,256]{1,0:T(8,128)(2,1)S(1)} collective-permute-done((bf16[1024,256]{1,0:T(8,128)(2,1)S(1)}, bf16[1024,256]{1,0:T(8,128)(2,1)S(1)}, u32[]{:S(2)}, u32[]{:S(2)}) %collective-permute-start.23) | collective-permute-done | bytes 524320 | tf_op jit(solution)/shard_map/ppermute | solution.py:260
  267.0 2.4 collective-permute-done.29
  (144 shorter events, 30.7 us)
Async XLA Ops:
  6.5 156.1 %all-gather.2.cloned.1.call-start = ((), (), s32[]{:S(2)}) async-start(), calls=%async_computation | async-start | bytes 17825792 | tf_op jit(solution)/shard_map/all_gather | solution.py:287
  12.6 18.4 %copy-start.3 = (bf16[2,2048,256]{2,1,0:T(8,128)(2,1)S(1)}, bf16[2,2048,256]{2,1,0:T(8,128)(2,1)}, u32[]{:S(2)}) copy-start(bf16[2,2048,256]{2,1,0:T(8,128)(2,1)} %refs_0_.1) | copy-start | bytes 6291460
  12.7 31.6 %collective-permute-start.3 = (bf16[512,768]{1,0:T(8,128)(2,1)}, bf16[512,768]{1,0:T(8,128)(2,1)S(1)}, u32[]{:S(2)}, u32[]{:S(2)}) collective-permute-start(bf16[512,768]{1,0:T(8,128)(2,1)} %cut.2), channel_id=1, source_target_pairs={{0,64},{64,0},{1,65},{65,1},{2,66},{66,2},{3,67},{67,3},{4,68},{68... | collective-permute-start | bytes 2359304 | tf_op jit(solution)/shard_map/ppermute | solution.py:248
  18.7 9.7 %collective-permute-start.4 = (bf16[16,16,256]{2,1,0:T(8,128)(2,1)S(1)}, bf16[16,16,256]{2,1,0:T(8,128)(2,1)S(1)}, u32[]{:S(2)}, u32[]{:S(2)}) collective-permute-start(bf16[16,16,256]{2,1,0:T(8,128)(2,1)S(1)} %bitcast.64), channel_id=1, source_target_pairs={{0,4},{4,8},{8,12},{1,5},{5,9},{9,13},{2,6},{6,10},{10,14},{3,7},{... | collective-permute-start | bytes 393224 | tf_op jit(solution)/shard_map/ppermute | solution.py:254
  22.2 16.5 %collective-permute-start = (bf16[256,384]{1,0:T(8,128)(2,1)S(1)}, bf16[256,384]{1,0:T(8,128)(2,1)S(1)}, u32[]{:S(2)}, u32[]{:S(2)}) collective-permute-start(bf16[256,384]{1,0:T(8,128)(2,1)S(1)} %maximum_maximum_fusion.refs_0_), channel_id=1, source_target_pairs={{0,16},{16,32},{32,48},{48,0},{1,17},{17,33},{33,49},{49,1},{2,18}... | collective-permute-start | bytes 589832 | tf_op jit(solution)/shard_map/ppermute | solution.py:39
  23.8 14.9 %collective-permute-start.1 = (bf16[256,384]{1,0:T(8,128)(2,1)S(1)}, bf16[256,384]{1,0:T(8,128)(2,1)S(1)}, u32[]{:S(2)}, u32[]{:S(2)}) collective-permute-start(bf16[256,384]{1,0:T(8,128)(2,1)S(1)} %maximum_maximum_fusion.refs_0_), channel_id=1, source_target_pairs={{0,48},{16,0},{32,16},{48,32},{1,49},{17,1},{33,17},{49,33},{2,50}... | collective-permute-start | bytes 589832 | tf_op jit(solution)/shard_map/ppermute | solution.py:39
  25.5 18.7 %collective-permute-start.2 = (bf16[256,384]{1,0:T(8,128)(2,1)S(1)}, bf16[256,384]{1,0:T(8,128)(2,1)}, u32[]{:S(2)}, u32[]{:S(2)}) collective-permute-start(bf16[256,384]{1,0:T(8,128)(2,1)S(1)} %maximum_maximum_fusion.refs_0_), channel_id=1, source_target_pairs={{0,32},{16,48},{32,0},{48,16},{1,33},{17,49},{33,1},{49,17},{2,34}... | collective-permute-start | bytes 589832 | tf_op jit(solution)/shard_map/ppermute | solution.py:39
  29.0 9.7 %collective-permute-start.5 = (bf16[16,16,256]{2,1,0:T(8,128)(2,1)}, bf16[16,16,256]{2,1,0:T(8,128)(2,1)}, u32[]{:S(2)}, u32[]{:S(2)}) collective-permute-start(bf16[16,16,256]{2,1,0:T(8,128)(2,1)} %bitcast.50), channel_id=1, source_target_pairs={{0,68},{4,72},{8,76},{64,4},{68,8},{72,12},{1,69},{5,73},{9,77},{6... | collective-permute-start | bytes 393224 | tf_op jit(solution)/shard_map/ppermute | solution.py:256
  31.0 18.3 %copy-start.12 = (bf16[16,16,256]{2,1,0:T(8,128)(2,1)S(1)}, bf16[16,16,256]{2,1,0:T(8,128)(2,1)}, u32[]{:S(2)}) copy-start(bf16[16,16,256]{2,1,0:T(8,128)(2,1)} %copy-done.11) | copy-start | bytes 393220
  32.9 18.8 %copy-start.2 = (bf16[512,1792]{1,0:T(8,128)(2,1)}, bf16[512,1792]{1,0:T(8,128)(2,1)S(1)}, u32[]{:S(2)}) copy-start(bf16[512,1792]{1,0:T(8,128)(2,1)S(1)} %cut.3) | copy-start | bytes 5505028
  44.3 7.4 %copy-start.7 = (bf16[512,768]{1,0:T(8,128)(2,1)}, bf16[512,768]{1,0:T(8,128)(2,1)S(1)}, u32[]{:S(2)}) copy-start(bf16[512,768]{1,0:T(8,128)(2,1)S(1)} %collective-permute-done.3.refs_0_) | copy-start | bytes 2359300
  44.3 63.3 %collective-permute-start.9 = (bf16[512,1792]{1,0:T(8,128)(2,1)S(1)}, bf16[512,1792]{1,0:T(8,128)(2,1)S(1)}, u32[]{:S(2)}, u32[]{:S(2)}) collective-permute-start(bf16[512,1792]{1,0:T(8,128)(2,1)S(1)} %cut.3), channel_id=1, source_target_pairs={{0,64},{64,0},{1,65},{65,1},{2,66},{66,2},{3,67},{67,3},{4,68},{68... | collective-permute-start | bytes 5505032 | tf_op jit(solution)/shard_map/ppermute | solution.py:248
  46.0 5.7 %copy-start.5 = (bf16[1024,384]{1,0:T(8,128)(2,1)}, bf16[1024,384]{1,0:T(8,128)(2,1)S(1)}, u32[]{:S(2)}) copy-start(bf16[1024,384]{1,0:T(8,128)(2,1)S(1)} %pile.1.refs_2_) | copy-start | bytes 2359300
  46.0 28.5 %collective-permute-start.6 = (bf16[1024,384]{1,0:T(8,128)(2,1)S(1)}, bf16[1024,384]{1,0:T(8,128)(2,1)S(1)}, u32[]{:S(2)}, u32[]{:S(2)}) collective-permute-start(bf16[1024,384]{1,0:T(8,128)(2,1)S(1)} %pile.1.refs_2_), channel_id=1, source_target_pairs={{0,4},{4,8},{8,12},{12,0},{1,5},{5,9},{9,13},{13,1},{2,6},{6,10},{... | collective-permute-start | bytes 2359304 | tf_op jit(solution)/shard_map/ppermute | solution.py:39
  46.1 29.4 %collective-permute-start.7 = (bf16[1024,384]{1,0:T(8,128)(2,1)S(1)}, bf16[1024,384]{1,0:T(8,128)(2,1)S(1)}, u32[]{:S(2)}, u32[]{:S(2)}) collective-permute-start(bf16[1024,384]{1,0:T(8,128)(2,1)S(1)} %pile.1.refs_2_), channel_id=1, source_target_pairs={{0,12},{4,0},{8,4},{12,8},{1,13},{5,1},{9,5},{13,9},{2,14},{6,2},{... | collective-permute-start | bytes 2359304 | tf_op jit(solution)/shard_map/ppermute | solution.py:39
  48.1 57.7 %collective-permute-start.8 = (bf16[1024,384]{1,0:T(8,128)(2,1)S(1)}, bf16[1024,384]{1,0:T(8,128)(2,1)S(1)}, u32[]{:S(2)}, u32[]{:S(2)}) collective-permute-start(bf16[1024,384]{1,0:T(8,128)(2,1)S(1)} %pile.1.refs_2_), channel_id=1, source_target_pairs={{0,8},{4,12},{8,0},{12,4},{1,9},{5,13},{9,1},{13,5},{2,10},{6,14},... | collective-permute-start | bytes 2359304 | tf_op jit(solution)/shard_map/ppermute | solution.py:39
  49.3 57.4 %collective-permute-start.10 = (bf16[512,768]{1,0:T(8,128)(2,1)S(1)}, bf16[512,768]{1,0:T(8,128)(2,1)S(1)}, u32[]{:S(2)}, u32[]{:S(2)}) collective-permute-start(bf16[512,768]{1,0:T(8,128)(2,1)S(1)} %collective-permute-done.3.refs_0_), channel_id=1, source_target_pairs={{0,1},{1,0},{2,3},{3,2},{4,5},{5,4},{6,7},{7,6},{8,9},{9,8},{10,11... | collective-permute-start | bytes 2359304 | tf_op jit(solution)/shard_map/ppermute | solution.py:248
  108.8 7.2 %collective-permute-start.11 = (bf16[512,1280]{1,0:T(8,128)(2,1)}, bf16[512,1280]{1,0:T(8,128)(2,1)S(1)}, u32[]{:S(2)}, u32[]{:S(2)}) collective-permute-start(bf16[512,1280]{1,0:T(8,128)(2,1)} %slice.76), channel_id=1, source_target_pairs={{0,1},{1,0},{2,3},{3,2},{4,5},{5,4},{6,7},{7,6},{8,9},{9,8},{10,11... | collective-permute-start | bytes 3932168 | tf_op jit(solution)/shard_map/ppermute | solution.py:248
  112.2 3.8 %copy-start.8 = (bf16[512,768]{1,0:T(8,128)(2,1)S(1)}, bf16[512,768]{1,0:T(8,128)(2,1)}, u32[]{:S(2)}) copy-start(bf16[512,768]{1,0:T(8,128)(2,1)} %copy-done.7) | copy-start | bytes 2359300
  112.3 3.8 %copy-start.10 = (bf16[512,768]{1,0:T(8,128)(2,1)S(1)}, bf16[512,768]{1,0:T(8,128)(2,1)}, u32[]{:S(2)}) copy-start(bf16[512,768]{1,0:T(8,128)(2,1)} %copy-done.9) | copy-start | bytes 2359300
  114.3 22.8 %collective-permute-start.13 = (bf16[512,256]{1,0:T(8,128)(2,1)}, bf16[512,256]{1,0:T(8,128)(2,1)S(1)}, u32[]{:S(2)}, u32[]{:S(2)}) collective-permute-start(bf16[512,256]{1,0:T(8,128)(2,1)} %get-tuple-element.97), channel_id=1, source_target_pairs={{0,16},{16,32},{32,48},{48,0},{1,17},{17,33},{33,49},{49,1},{2,18}... | collective-permute-start | bytes 786440 | tf_op jit(solution)/shard_map/ppermute | solution.py:39
  114.7 25.5 %collective-permute-start.14 = (bf16[512,256]{1,0:T(8,128)(2,1)}, bf16[512,256]{1,0:T(8,128)(2,1)}, u32[]{:S(2)}, u32[]{:S(2)}) collective-permute-start(bf16[512,256]{1,0:T(8,128)(2,1)} %get-tuple-element.98), channel_id=1, source_target_pairs={{0,32},{16,48},{32,0},{48,16},{1,33},{17,49},{33,1},{49,17},{2,34}... | collective-permute-start | bytes 786440 | tf_op jit(solution)/shard_map/ppermute | solution.py:39
  116.0 3.4 %copy-start.6 = (bf16[1024,384]{1,0:T(8,128)(2,1)S(1)}, bf16[1024,384]{1,0:T(8,128)(2,1)}, u32[]{:S(2)}) copy-start(bf16[1024,384]{1,0:T(8,128)(2,1)} %copy-done.5) | copy-start | bytes 2359300
  119.4 16.8 %copy-start.23 = (f32[2304]{0:T(1024)S(1)}, f32[2304]{0:T(1024)}, u32[]{:S(2)}) copy-start(f32[2304]{0:T(1024)} %param.14) | copy-start | bytes 27652
  119.4 16.8 %copy-start.25 = (f32[32]{0:T(128)S(1)}, f32[32]{0:T(128)}, u32[]{:S(2)}) copy-start(f32[32]{0:T(128)} %param.16) | copy-start | bytes 388
  129.3 23.9 %copy-start.4 = (f32[4,2304]{1,0:T(4,128)S(1)}, f32[4,2304]{1,0:T(4,128)}, u32[]{:S(2)}) copy-start(f32[4,2304]{1,0:T(4,128)} %refs_3_.7) | copy-start | bytes 110596
  129.3 23.9 %collective-permute-start.12 = (bf16[528,512]{1,0:T(8,128)(2,1)}, bf16[528,512]{1,0:T(8,128)(2,1)S(1)}, u32[]{:S(2)}, u32[]{:S(2)}) collective-permute-start(bf16[528,512]{1,0:T(8,128)(2,1)} %get-tuple-element.70), channel_id=1, source_target_pairs={{0,64},{64,0},{1,65},{65,1},{2,66},{66,2},{3,67},{67,3},{4,68},{68... | collective-permute-start | bytes 1622024 | tf_op jit(solution)/shard_map/ppermute | solution.py:248
  134.3 20.3 %copy-start.24 = (f32[32]{0:T(128)S(1)}, f32[32]{0:T(128)}, u32[]{:S(2)}) copy-start(f32[32]{0:T(128)} %param.15) | copy-start | bytes 388
  134.3 11.6 %collective-permute-start.15 = (bf16[512,256]{1,0:T(8,128)(2,1)}, bf16[512,256]{1,0:T(8,128)(2,1)}, u32[]{:S(2)}, u32[]{:S(2)}) collective-permute-start(bf16[512,256]{1,0:T(8,128)(2,1)} %select_select_fusion), channel_id=1, source_target_pairs={{0,48},{16,0},{32,16},{48,32},{1,49},{17,1},{33,17},{49,33},{2,50}... | collective-permute-start | bytes 786440 | tf_op jit(solution)/shard_map/ppermute | solution.py:39
  147.2 13.2 %collective-permute-start.16 = (bf16[512,256]{1,0:T(8,128)(2,1)S(1)}, bf16[512,256]{1,0:T(8,128)(2,1)S(1)}, u32[]{:S(2)}, u32[]{:S(2)}) collective-permute-start(bf16[512,256]{1,0:T(8,128)(2,1)S(1)} %add_add_fusion), channel_id=1, source_target_pairs={{4,0},{5,1},{6,2},{7,3},{20,16},{21,17},{22,18},{23,19},{36,32},{3... | collective-permute-start | bytes 786440 | tf_op jit(solution)/shard_map/ppermute | solution.py:330
  147.9 12.5 %collective-permute-start.17 = (bf16[512,256]{1,0:T(8,128)(2,1)S(1)}, bf16[512,256]{1,0:T(8,128)(2,1)S(1)}, u32[]{:S(2)}, u32[]{:S(2)}) collective-permute-start(bf16[512,256]{1,0:T(8,128)(2,1)S(1)} %add_add_fusion), channel_id=1, source_target_pairs={{8,0},{9,1},{10,2},{11,3},{24,16},{25,17},{26,18},{27,19},{40,32},... | collective-permute-start | bytes 786440 | tf_op jit(solution)/shard_map/ppermute | solution.py:330
  152.5 8.0 %collective-permute-start.18 = (bf16[512,256]{1,0:T(8,128)(2,1)S(1)}, bf16[512,256]{1,0:T(8,128)(2,1)S(1)}, u32[]{:S(2)}, u32[]{:S(2)}) collective-permute-start(bf16[512,256]{1,0:T(8,128)(2,1)S(1)} %add_add_fusion), channel_id=1, source_target_pairs={{12,0},{13,1},{14,2},{15,3},{28,16},{29,17},{30,18},{31,19},{44,32... | collective-permute-start | bytes 786440 | tf_op jit(solution)/shard_map/ppermute | solution.py:330
  156.4 6.0 %collective-permute-start.19 = (f32[32]{0:T(128)S(1)}, f32[32]{0:T(128)S(1)}, u32[]{:S(2)}, u32[]{:S(2)}) collective-permute-start(f32[32]{0:T(128)S(1)} %fusion.11), channel_id=1, source_target_pairs={{0,4},{4,8},{8,12},{1,5},{5,9},{9,13},{2,6},{6,10},{10,14},{3,7},{... | collective-permute-start | bytes 392 | tf_op jit(solution)/shard_map/ppermute | solution.py:260
  162.6 80.5 %copy-start.21 = (f32[2048,1]{0,1:T(1,128)}, f32[2048,1]{0,1:T(1,128)S(1)}, u32[]{:S(2)}) copy-start(f32[2048,1]{0,1:T(1,128)S(1)} %broadcast_in_dim_reshape.7) | copy-start | bytes 24580
  173.5 16.1 %collective-permute-start.20 = (bf16[528,512]{1,0:T(8,128)(2,1)S(1)}, bf16[528,512]{1,0:T(8,128)(2,1)S(1)}, u32[]{:S(2)}, u32[]{:S(2)}) collective-permute-start(bf16[528,512]{1,0:T(8,128)(2,1)S(1)} %get-tuple-element.75), channel_id=1, source_target_pairs={{0,64},{64,0},{1,65},{65,1},{2,66},{66,2},{3,67},{67,3},{4,68},{68... | collective-permute-start | bytes 1622024 | tf_op jit(solution)/shard_map/ppermute | solution.py:248
  183.9 18.5 %slice-start = ((s8[4325376]{0:T(1024)(128)(4,1)}), s8[4194304]{0:T(1024)(128)(4,1)S(1)}, s32[]{:S(2)}) async-start(s8[4325376]{0:T(1024)(128)(4,1)} %bitcast.53), calls=%async_computation.1 | async-start | bytes 8388608
  183.9 18.5 %slice-start.1 = ((s8[4325376]{0:T(1024)(128)(4,1)}), s8[131072]{0:T(1024)(128)(4,1)S(1)}, s32[]{:S(2)}) async-start(s8[4325376]{0:T(1024)(128)(4,1)} %bitcast.53), calls=%async_computation.2 | async-start | bytes 262144
  183.9 18.5 %collective-permute-start.21 = (bf16[528,512]{1,0:T(8,128)(2,1)S(1)}, bf16[528,512]{1,0:T(8,128)(2,1)S(1)}, u32[]{:S(2)}, u32[]{:S(2)}) collective-permute-start(bf16[528,512]{1,0:T(8,128)(2,1)S(1)} %get-tuple-element.77), channel_id=1, source_target_pairs={{0,64},{64,0},{1,65},{65,1},{2,66},{66,2},{3,67},{67,3},{4,68},{68... | collective-permute-start | bytes 1622024 | tf_op jit(solution)/shard_map/ppermute | solution.py:248
  198.2 16.8 %collective-permute-start.24 = (bf16[528,512]{1,0:T(8,128)(2,1)S(1)}, bf16[528,512]{1,0:T(8,128)(2,1)S(1)}, u32[]{:S(2)}, u32[]{:S(2)}) collective-permute-start(bf16[528,512]{1,0:T(8,128)(2,1)S(1)} %get-tuple-element.94), channel_id=1, source_target_pairs={{0,64},{64,0},{1,65},{65,1},{2,66},{66,2},{3,67},{67,3},{4,68},{68... | collective-permute-start | bytes 1622024 | tf_op jit(solution)/shard_map/ppermute | solution.py:248
  211.0 6.0 %copy-start.19 = (f32[2048,256]{1,0:T(8,128)S(1)}, f32[2048,256]{1,0:T(8,128)}, u32[]{:S(2)}) copy-start(f32[2048,256]{1,0:T(8,128)} %multiply_select_fusion) | copy-start | bytes 6291460
  211.1 15.2 %collective-permute-start.27 = (bf16[528,512]{1,0:T(8,128)(2,1)S(1)}, bf16[528,512]{1,0:T(8,128)(2,1)S(1)}, u32[]{:S(2)}, u32[]{:S(2)}) collective-permute-start(bf16[528,512]{1,0:T(8,128)(2,1)S(1)} %get-tuple-element.96), channel_id=1, source_target_pairs={{0,64},{64,0},{1,65},{65,1},{2,66},{66,2},{3,67},{67,3},{4,68},{68... | collective-permute-start | bytes 1622024 | tf_op jit(solution)/shard_map/ppermute | solution.py:248
  217.1 13.7 %collective-permute-start.25 = (bf16[512,256]{1,0:T(8,128)(2,1)S(1)}, bf16[512,256]{1,0:T(8,128)(2,1)S(1)}, u32[]{:S(2)}, u32[]{:S(2)}) collective-permute-start(bf16[512,256]{1,0:T(8,128)(2,1)S(1)} %fusion.13), channel_id=1, source_target_pairs={{0,4},{4,8},{8,12},{1,5},{5,9},{9,13},{2,6},{6,10},{10,14},{3,7},{... | collective-permute-start | bytes 786440 | tf_op jit(solution)/shard_map/ppermute | solution.py:260
  224.3 17.3 %collective-permute-start.22 = (bf16[1024,256]{1,0:T(8,128)(2,1)S(1)}, bf16[1024,256]{1,0:T(8,128)(2,1)S(1)}, u32[]{:S(2)}, u32[]{:S(2)}) collective-permute-start(bf16[1024,256]{1,0:T(8,128)(2,1)S(1)} %fusion.15), channel_id=1, source_target_pairs={{0,4},{4,8},{8,12},{1,5},{5,9},{9,13},{2,6},{6,10},{10,14},{3,7},{... | collective-permute-start | bytes 1572872 | tf_op jit(solution)/shard_map/ppermute | solution.py:260
  231.1 19.0 %collective-permute-start.26 = (bf16[512,256]{1,0:T(8,128)(2,1)S(1)}, bf16[512,256]{1,0:T(8,128)(2,1)S(1)}, u32[]{:S(2)}, u32[]{:S(2)}) collective-permute-start(bf16[512,256]{1,0:T(8,128)(2,1)S(1)} %get-tuple-element.101), channel_id=1, source_target_pairs={{0,8},{4,12},{1,9},{5,13},{2,10},{6,14},{3,11},{7,15},{16,24},{20,... | collective-permute-start | bytes 786440 | tf_op jit(solution)/shard_map/ppermute | solution.py:260
  232.4 17.7 %collective-permute-start.28 = (bf16[512,256]{1,0:T(8,128)(2,1)S(1)}, bf16[512,256]{1,0:T(8,128)(2,1)S(1)}, u32[]{:S(2)}, u32[]{:S(2)}) collective-permute-start(bf16[512,256]{1,0:T(8,128)(2,1)S(1)} %get-tuple-element.102), channel_id=1, source_target_pairs={{0,4},{4,8},{8,12},{1,5},{5,9},{9,13},{2,6},{6,10},{10,14},{3,7},{... | collective-permute-start | bytes 786440 | tf_op jit(solution)/shard_map/ppermute | solution.py:260
  241.8 24.8 %collective-permute-start.23 = (bf16[1024,256]{1,0:T(8,128)(2,1)S(1)}, bf16[1024,256]{1,0:T(8,128)(2,1)S(1)}, u32[]{:S(2)}, u32[]{:S(2)}) collective-permute-start(bf16[1024,256]{1,0:T(8,128)(2,1)S(1)} %fusion), channel_id=1, source_target_pairs={{0,8},{4,12},{1,9},{5,13},{2,10},{6,14},{3,11},{7,15},{16,24},{20,... | collective-permute-start | bytes 1572872 | tf_op jit(solution)/shard_map/ppermute | solution.py:260
  243.2 23.5 %slice-start.3 = ((f32[2048,1]{0,1:T(1,128)}), f32[1024,1]{0,1:T(1,128)S(1)}, s32[]{:S(2)}) async-start(f32[2048,1]{0,1:T(1,128)} %copy-done.21), calls=%async_computation.4 | async-start | bytes 8192 | tf_op jit(solution)/shard_map/slice | solution.py:357
  250.4 19.1 %collective-permute-start.29 = (bf16[512,256]{1,0:T(8,128)(2,1)S(1)}, bf16[512,256]{1,0:T(8,128)(2,1)S(1)}, u32[]{:S(2)}, u32[]{:S(2)}) collective-permute-start(bf16[512,256]{1,0:T(8,128)(2,1)S(1)} %get-tuple-element.100), channel_id=1, source_target_pairs={{0,8},{4,12},{1,9},{5,13},{2,10},{6,14},{3,11},{7,15},{16,24},{20,... | collective-permute-start | bytes 786440 | tf_op jit(solution)/shard_map/ppermute | solution.py:260
  (13 other events, 26.6 us)
Sparse Core Ops, SparseCore 0:
  9.5 140.1 all-gather.1

commit v2 on v1

v2 whole, which is shorter than its diff:
```python
import jax
import jax.numpy as jnp
from jax import lax
from jax.experimental import pallas as pl
from jax.experimental.pallas import tpu as pltpu
from jax.sharding import Mesh
from jax.sharding import PartitionSpec as P

GROUP_HEADS = 32
P_SIZE = 64
N = 256
HALO = 16
ROWS = 512
LONG = ROWS + HALO
PIECE = 256
HALF = 4096
HEAD_COLUMNS = GROUP_HEADS * P_SIZE
F32 = jnp.float32
BF16 = jnp.bfloat16
VMEM_LIMIT = 60 * 1024 * 1024
VMEM = pl.BlockSpec(memory_space=pltpu.VMEM)
SMEM = pl.BlockSpec(memory_space=pltpu.SMEM)
ANY = pl.BlockSpec(memory_space=pltpu.HBM)

CHUNKS = {
    "states": (HEAD_COLUMNS, 256),
    "a": (0, 768),
    "b": (768, 768),
    "c": (1536, 512),
}
SPLIT = 1536
STATE_WIDTH = 384


def together(*values):
    return lax.optimization_barrier(values)


def shifted(part, axis, by):
    return lax.ppermute(part, axis, [(i, (i + by) % 4) for i in range(4)])


def params():
    return pltpu.CompilerParams(vmem_limit_bytes=VMEM_LIMIT)


def pile(parts):
    width = parts[0].shape[1]
    heights = [part.shape[0] for part in parts]

    def kernel(*refs):
        copies = [
            pltpu.make_async_copy(ref, refs[len(parts)].at[pl.ds(sum(heights[:i]), heights[i])], refs[-1].at[i])
            for i, ref in enumerate(refs[: len(parts)])
        ]
        for copy in copies:
            copy.start()
        for copy in copies:
            copy.wait()

    whole = (sum(heights), width)
    return pl.pallas_call(
        kernel,
        out_shape=jax.ShapeDtypeStruct(whole, parts[0].dtype),
        in_specs=[ANY] * len(parts),
        out_specs=VMEM,
        scratch_shapes=[pltpu.SemaphoreType.DMA((len(parts),))],
        compiler_params=params(),
        cost_estimate=pl.CostEstimate(flops=0, bytes_accessed=4 * whole[0] * width, transcendentals=0),
        name="pile",
    )(*parts)


def cut(rows, first, width):
    def kernel(first_ref, rows_ref, out_ref, sem):
        copy = pltpu.make_async_copy(rows_ref.at[:, pl.ds(pl.multiple_of(first_ref[0], PIECE), width)], out_ref, sem)
        copy.start()
        copy.wait()

    return pl.pallas_call(
        kernel,
        out_shape=jax.ShapeDtypeStruct((rows.shape[0], width), rows.dtype),
        in_specs=[SMEM, ANY],
        out_specs=VMEM,
        scratch_shapes=[pltpu.SemaphoreType.DMA],
        compiler_params=params(),
        cost_estimate=pl.CostEstimate(flops=0, bytes_accessed=4 * rows.shape[0] * width, transcendentals=0),
        name="cut",
    )(first[None].astype(jnp.int32), rows)


NEAR = (768, 1280)


def in_blocks(name, pick, halo, at, *sources):
    def kernel(at_ref, halo_ref, *refs):
        out_ref, sems = refs[len(sources) :]
        parts = [(halo_ref, out_ref.at[:, pl.ds(0, HALO)])]
        for i in range(16):
            source, place = pick(at_ref, refs, i)
            parts.append((source, out_ref.at[place, pl.ds(HALO, ROWS)]))
        copies = [pltpu.make_async_copy(source, target, sems.at[i]) for i, (source, target) in enumerate(parts)]
        for copy in copies:
            copy.start()
        for copy in copies:
            copy.wait()

    return pl.pallas_call(
        kernel,
        out_shape=jax.ShapeDtypeStruct((16, LONG, PIECE), halo.dtype),
        in_specs=[SMEM] + [ANY] * (1 + len(sources)),
        out_specs=VMEM,
        scratch_shapes=[pltpu.SemaphoreType.DMA((17,))],
        compiler_params=params(),
        cost_estimate=pl.CostEstimate(flops=0, bytes_accessed=4 * LONG * HALF, transcendentals=0),
        name=name,
    )(at[None].astype(jnp.int32), halo, *sources)


def own_tokens(rows, halo):
    def pick(at_ref, refs, i):
        return refs[0].at[:, pl.ds(pl.multiple_of(at_ref[0] * HALF + i * PIECE, PIECE), PIECE)], i

    return in_blocks("own_tokens", pick, halo, lax.axis_index("yh"), rows)


def partner_tokens(nears, fars, halo):
    def pick(at_ref, refs, i):
        place = at_ref[0] * 8 + i if i < 8 else (1 - at_ref[0]) * 8 + i - 8
        begin, piece = i % 8 * PIECE, 0
        if begin >= NEAR[0]:
            begin, piece = begin - NEAR[0], 1
        return refs[i // 8 * 2 + piece].at[:, pl.ds(begin, PIECE)], place

    return in_blocks("partner_tokens", pick, halo, lax.axis_index("core"), *nears, *fars)


def project(own, theirs, places, blocks, first, width, totals=None, final=True, steps=False):
    n_blocks, n_totals = len(blocks), 2 if totals else 0
    origin = blocks[0][3]
    depth = sum(block[2] for block in blocks)

    def kernel(places_ref, *refs):
        token_refs, total_refs, w_refs = refs[:2], refs[2 : 2 + n_totals], refs[2 + n_totals : 2 + n_totals + n_blocks]
        outs, (acc, their_acc, *sides), held, sems = refs[-8:-6], refs[-6:-2], refs[-2], refs[-1]
        accs = (acc, their_acc)
        copies = []
        for i, (_, row, rows, place) in enumerate(blocks):
            begin = place - origin
            parts = [(w_refs[i].at[pl.ds(row, rows), pl.ds(first, width)], held.at[pl.ds(begin, rows)])]
            for side in range(2):
                for k in range(rows // PIECE):
                    parts.append((token_refs[side].at[places_ref[place // PIECE + k]], sides[side].at[begin // PIECE + k]))
            if i == 0 and totals:
                parts += [(total_refs[side], accs[side]) for side in range(2)]
            copies.append([pltpu.make_async_copy(source, target, sems.at[i, n]) for n, (source, target) in enumerate(parts)])
            for copy in copies[i]:
                copy.start()
        for i, (_, row, rows, place) in enumerate(blocks):
            for copy in copies[i]:
                copy.wait()
            begin = place - origin
            w = held[begin : begin + rows]
            for side in range(2):
                lhs = jnp.concatenate([sides[side][begin // PIECE + k] for k in range(rows // PIECE)], axis=1)
                total = jnp.dot(lhs, w, preferred_element_type=F32)
                if i > 0 or totals:
                    total = total + accs[side][...]
                if i < n_blocks - 1:
                    accs[side][...] = total
                elif side == 0 or not final:
                    outs[side][...] = total
                elif steps:
                    outs[1][:, :N] = total[:, :N].astype(BF16)
                    exact = total[:, N:]
                    high = exact.astype(BF16)
                    outs[1][:, N : N + 128] = high
                    outs[1][:, N + 128 :] = (exact - high.astype(F32)).astype(BF16)
                else:
                    outs[1][...] = total.astype(BF16)

    their_width = width + 128 if steps else width
    return pl.pallas_call(
        kernel,
        out_shape=(
            jax.ShapeDtypeStruct((LONG, width), F32),
            jax.ShapeDtypeStruct((LONG, their_width), BF16 if final else F32),
        ),
        in_specs=[SMEM] + [ANY] * (2 + n_totals + n_blocks),
        out_specs=(VMEM, VMEM),
        scratch_shapes=[pltpu.VMEM((LONG, width), F32)] * 2
        + [pltpu.VMEM((depth // PIECE, LONG, PIECE), BF16)] * 2
        + [pltpu.VMEM((depth, width), BF16), pltpu.SemaphoreType.DMA((n_blocks, 11))],
        compiler_params=params(),
        cost_estimate=pl.CostEstimate(flops=4 * LONG * depth * width, bytes_accessed=8_700_000 + 2 * depth * width, transcendentals=0),
        name="project",
    )(places, own, theirs, *(totals or ()), *[block[0] for block in blocks])


def activate(info_ref, projected, taps_ref, bias_ref, first, masked):
    projected = projected.astype(BF16).astype(F32)
    place = info_ref[0] + lax.broadcasted_iota(jnp.int32, projected.shape, 0)
    masked[...] = jnp.where(place >= info_ref[1], projected, 0.0)
    columns = slice(first, first + projected.shape[1])
    total = bias_ref[:, columns]
    for k in range(4):
        total = total + taps_ref[k : k + 1, columns] * masked[pl.ds(HALO - 3 + k, ROWS), :]
    return (total * jax.nn.sigmoid(total)).astype(BF16)


def state_kernel(info_ref, own_ref, other_ref, taps_ref, bias_ref, states_out, steps_out, masked):
    projected = own_ref[:, :N] + other_ref[:, :N].astype(F32)
    states_out[...] = activate(info_ref, projected, taps_ref, bias_ref, HEAD_COLUMNS, masked)
    steps = own_ref[HALO:, N : N + 128] + other_ref[HALO:, N : N + 128].astype(F32) + other_ref[HALO:, N + 128 :].astype(F32)
    steps_out[...] = steps[:, :GROUP_HEADS]


def head_kernel(first_head, info_ref, own_ref, other_ref, taps_ref, bias_ref, weight_ref, states_ref, out_ref, masked):
    projected = own_ref[...] + other_ref[...].astype(F32)
    activated = activate(info_ref, projected, taps_ref, bias_ref, first_head * P_SIZE, masked).astype(F32)
    lane = lax.broadcasted_iota(jnp.int32, (ROWS, 128), 1)
    scaled = []
    for i in range(activated.shape[1] // 128):
        head = first_head + 2 * i
        factor = jnp.where(lane < P_SIZE, weight_ref[:, head : head + 1], weight_ref[:, head + 1 : head + 2])
        scaled.append((activated[:, i * 128 : (i + 1) * 128] * factor).astype(BF16))
    scaled = jnp.concatenate(scaled, axis=1)
    out_ref[...] = lax.dot_general(scaled, states_ref[...], (((0,), (0,)), ((), ())), preferred_element_type=F32)


def call(kernel, out, width, *args):
    return pl.pallas_call(
        kernel,
        out_shape=out,
        in_specs=[SMEM] + [VMEM] * (len(args) - 1),
        out_specs=jax.tree.map(lambda _: VMEM, out),
        scratch_shapes=[pltpu.VMEM((LONG, width), F32)],
        compiler_params=params(),
        cost_estimate=pl.CostEstimate(flops=ROWS * N * width, bytes_accessed=2 * LONG * width, transcendentals=0),
        name="activate",
    )(*args)


def swap(value, axis):
    return lax.ppermute(value, axis, [(0, 1), (1, 0)])


def halos(rows):
    yh = lax.axis_index("yh")
    last = rows[ROWS - HALO :].reshape(HALO, 2, 16, PIECE).transpose(1, 2, 0, 3)
    mine = lax.ppermute(lax.dynamic_index_in_dim(last, yh, 0, False), "z", [(0, 1), (1, 2), (2, 3)])
    pairs = [(y * 4 + z, (1 - y) * 4 + z + 1) for y in range(2) for z in range(3)]
    return mine, lax.ppermute(lax.dynamic_index_in_dim(last, 1 - yh, 0, False), ("yh", "z"), pairs)


def behind(value, by):
    return lax.ppermute(value, "z", [(i, i + by) for i in range(4 - by)])


def saved_rows(near, far, wanted):
    yh, x = lax.axis_index("yh"), lax.axis_index("x")
    found = jnp.zeros((512, N), BF16)
    for i in range(4):
        picked = jnp.zeros((512, N), BF16)
        for side, value in ((yh, near), (1 - yh, far)):
            for b in range(2):
                picked = jnp.where(wanted[i] == 2 * (side * 4 + x) + b, value[b], picked)
        found = found + (shifted(picked, "x", i) if i else picked)
    return found


def all_rows(found):
    z = lax.axis_index("z")
    near = lax.ppermute(found, "z", [(0, 1), (1, 0), (2, 3), (3, 2)])
    two = jnp.where(z % 2 == 0, jnp.concatenate([found, near]), jnp.concatenate([near, found]))
    far = lax.ppermute(two, "z", [(2, 0), (3, 1), (0, 2), (1, 3)])
    return jnp.where(z < 2, jnp.concatenate([two, far]), jnp.concatenate([far, two]))


def per_device(tokens, input_proj, step_proj, conv_weight, conv_bias, step_bias, head_rate, state_pool, resume_slot, offsets):
    yh, x, z, core = (lax.axis_index(a) for a in ("yh", "x", "z", "core"))
    rows = tokens[0]
    info = jnp.stack([z * ROWS - HALO, offsets[0]]).astype(jnp.int32)

    places = jnp.arange(16, dtype=jnp.int32)
    s = jnp.concatenate([input_proj[:, HEAD_COLUMNS:], step_proj, jnp.zeros((PIECE, 96), BF16), input_proj[:, :SPLIT]], axis=1)
    early = lax.all_gather(s, ("x", "z"), axis=0, tiled=True)
    late = lax.all_gather(input_proj[:, SPLIT:HEAD_COLUMNS], ("x", "z"), axis=0, tiled=True)
    half = (1 - yh) * HALF + core * 2048
    projected = {}

    def run(name, array, first):
        steps = name == "states"
        blocks = [(array, j * 1024, 1024, j * 1024) for j in range(4)]
        width = STATE_WIDTH if steps else CHUNKS[name][1]
        own, sent = project(own_side, partner_side, places, blocks, first, width, steps=steps)
        projected[name] = [own, swap(sent, "yh")]
        return own

    def head(name):
        first, width = CHUNKS[name]
        kernel = lambda *refs: head_kernel(first // P_SIZE, *refs)
        out = jax.ShapeDtypeStruct((width, N), F32)
        return call(kernel, out, width, info, *projected[name], conv_weight, conv_bias[None], weight, states)

    first_near = swap(cut(rows, half, NEAR[0]), "yh")
    my_halo, their_halo = halos(rows)
    second_piece, first_near, my_halo, their_halo = together(cut(rows, half + NEAR[0], NEAR[1]), first_near, my_halo, their_halo)
    second_near = swap(second_piece, "yh")
    first_far = swap(first_near, "core")
    own_side = own_tokens(rows, my_halo)
    my_pool = lax.dynamic_slice_in_dim(state_pool, z * 512, 512, 1)
    second_near, first_far, own_side, my_pool = together(second_near, first_far, own_side, my_pool)
    second_far = swap(second_near, "core")
    partner_side = partner_tokens((first_near, second_near), (first_far, second_far), their_halo)
    their_pool = swap(my_pool, "yh")
    partner_side, their_pool, slots = together(partner_side, their_pool, jnp.concatenate([resume_slot, resume_slot]))
    wanted = [resume_slot[0]] + [shifted(slots, "x", -i)[0] for i in (1, 2, 3)]
    early, partner_side, *wanted = together(early, partner_side, *wanted)

    own = run("states", early, 0)
    early, projected["states"][0], my_pool = together(early, own, my_pool)
    found = saved_rows(my_pool, their_pool, wanted)
    own = run("a", early, STATE_WIDTH)
    early, projected["states"][1], projected["a"][0], found = together(early, projected["states"][1], own, found)
    initial = all_rows(found)
    own = run("b", early, STATE_WIDTH + CHUNKS["b"][0])
    projected["b"][0], projected["states"] = together(own, projected["states"])
    out = (jax.ShapeDtypeStruct((ROWS, N), BF16), jax.ShapeDtypeStruct((ROWS, GROUP_HEADS), F32))
    states, step_raw = call(state_kernel, out, N, info, *projected["states"], conv_weight, conv_bias[None])
    valid = (z * ROWS + jnp.arange(ROWS, dtype=jnp.int32) >= offsets[0]).astype(F32)
    step_size = jax.nn.softplus(step_raw + step_bias) * valid[:, None]
    log_decay = -head_rate * step_size
    running = jnp.cumsum(log_decay, axis=0)
    weight = jnp.exp(running[-1:] - running) * step_size
    def columns(array, name):
        return array[CHUNKS[name][0] : sum(CHUNKS[name])]

    def first_steps(own):
        sent = own.astype(BF16)
        return behind(sent, 1), lax.ppermute(sent, "z", [(0, 3)])

    def relayed(one):
        return lax.ppermute(one, "z", [(1, 2), (2, 3)])

    def from_start(name):
        start = jnp.where(z == 0, columns(factor, name) * columns(initial, name).astype(F32), 0.0)
        return head(name) + start

    def all_before(own, name, one, two, three):
        return own + sum(columns(f, name) * came.astype(F32) for f, came in zip(factors, (one, two, three)))

    projected["a"], projected["b"][0] = together(projected["a"], projected["b"][0])
    decay = jnp.exp(running[-1])
    factor = jnp.repeat(decay, P_SIZE)[:, None]
    a = from_start("a")
    a, b_input = together(a, projected["b"])
    projected["b"] = b_input
    one_a, three_a = first_steps(a)
    b = from_start("b")
    late, b, decay = together(late, b, decay)
    own = run("c", late, 0)
    projected["c"][0], one_a, three_a, b, decay = together(own, one_a, three_a, b, decay)
    two_a = relayed(one_a)
    one_b, three_b = first_steps(b)
    decays = lax.all_gather(decay, "z")
    two = decay * lax.dynamic_index_in_dim(decays, (z + 3) % 4, 0, False)
    three = two * lax.dynamic_index_in_dim(decays, (z + 2) % 4, 0, False)
    factors = jnp.repeat(jnp.stack([decay, two, three]), P_SIZE, axis=1)[:, :, None]
    projected["c"][1], two_a, one_b, three_b, factors = together(projected["c"][1], two_a, one_b, three_b, factors)
    two_b = relayed(one_b)
    c = from_start("c")
    one_c, three_c = first_steps(c)
    two_c = relayed(one_c)
    a = all_before(a, "a", one_a, two_a, three_a)
    b = all_before(b, "b", one_b, two_b, three_b)
    c = all_before(c, "c", one_c, two_c, three_c)
    return jnp.concatenate([a, b, c], axis=0)[None, None]


def solution(mesh):
    fine = Mesh(mesh.devices.reshape(2, 4, 4, 2, 2), ("yh", "x", "z", "yl", "core"))
    dp, tensor = ("yh", "x"), ("yl", "core")
    return jax.shard_map(
        per_device,
        mesh=fine,
        in_specs=(
            P(dp, "z", None),
            P(dp + ("z",), tensor),
            P(dp + ("z",), tensor),
            P(None, tensor),
            P(tensor),
            P(tensor),
            P(tensor),
            P(dp, tensor, None),
            P(dp),
            P(dp),
        ),
        out_specs=P(dp, "z", tensor, None),
        check_vma=False,
    )
```

time: 279 us -> 271 us (0.971)
  waiting for transfers between devices: 106 us -> 86.7 us
  blocking collectives: 0 us -> 12.2 us
  local copies, waits for them, and re-layouts: 18 us -> 12.4 us
  Pallas kernels: 65.8 us -> 70.7 us
    ppermute x9 -> x6, waiting for transfers between devices: 64.6 us -> 3.87 us  [shifted(): return lax.ppermute(part, axis, [(i, (i + by) % 4) for i in range(4)])]
    ppermute x7 -> x3, waiting for transfers between devices: 31.7 us -> 2.63 us  [behind(): return lax.ppermute(value, 'z', [(i, i + by) for i in range(4 - by)])]
    all_gather x1 -> x2, waiting for transfers between devices: 0.02 us -> 28.2 us  [the longest x1 28.2 us: per_device(): early = lax.all_gather(s, ('x', 'z'), axis=0, tiled=True)]
    ppermute x9, waiting for transfers between devices: 3.8 us -> 31 us  [swap(): return lax.ppermute(value, axis, [(0, 1), (1, 0)])]
    unnamed x0 -> x1, blocking collectives: none -> 12.2 us
    ppermute x3 -> x8, waiting for transfers between devices: 0.01 us -> 11.3 us  [the longest x1 6.88 us: all_rows(): far = lax.ppermute(two, 'z', [(2, 0), (3, 1), (0, 2), (1, 3)])]
    ppermute x7 -> x3, starting transfers between devices: 21 us -> 9.79 us  [behind(): return lax.ppermute(value, 'z', [(i, i + by) for i in range(4 - by)])]
    ppermute x3 -> x8, starting transfers between devices: 5.92 us -> 14 us  [the longest x3 8.07 us: relayed(): return lax.ppermute(one, 'z', [(1, 2), (2, 3)])]
  transfers between devices with their start and end apart: 31 -> 30, of which waited for: 14 -> 12; matrix products, arithmetic and copies ran while one was open for 6% -> 6% of each run, Pallas kernels for 21% -> 25%
where the time goes in v2:
time: 271 us; the launch traced here: 268 us
  waiting for transfers between devices  86.7 us (32%)
  Pallas kernels  70.7 us (26%)
  starting transfers between devices  57.5 us (21%)
  between operations  16.4 us (6%)
  local copies, waits for them, and re-layouts  12.4 us (5%)
  other arithmetic  12.4 us (5%)
  blocking collectives  12.2 us (5%)
    pallas_call x4, Pallas kernels, project(): pl.pallas_call(kernel, out_shape=(jax.ShapeDtypeStruct((LONG, width), F32...  40.7 us
    ppermute x9, waiting for transfers between devices, swap(): return lax.ppermute(value, axis, [(0, 1), (1, 0)])  31 us
    all_gather x1, waiting for transfers between devices, per_device(): early = lax.all_gather(s, ('x', 'z'), axis=0, tiled=True)  28.2 us
    ppermute x9, starting transfers between devices, swap(): return lax.ppermute(value, axis, [(0, 1), (1, 0)])  19.4 us
    pallas_call x4, Pallas kernels, call(): pl.pallas_call(kernel, out_shape=out, in_specs=[SMEM] + [VMEM] * (len(arg...  16.5 us
    unnamed x1, blocking collectives  12.2 us
    ppermute x3, starting transfers between devices, behind(): return lax.ppermute(value, 'z', [(i, i + by) for i in range(4 - by)])  9.79 us
    ppermute x1, waiting for transfers between devices, halos(): lax.ppermute(lax.dynamic_index_in_dim(last, 1 - yh, 0, False), ('yh', 'z'...  9.05 us
  transfers between devices with their start and end apart: 30, of which 12 were waited for; matrix products, arithmetic and copies ran while one was open for 6% of the time, Pallas kernels for 25%

profile of v2, /device:TPU:64, one launch (start us, length us, event | category | flops | bytes accessed | tf_op | source)
XLA Modules:
  0.0 268.5 jit_solution(6375598840337392584)
XLA Ops:
  9.7 2.1 cut.3
  11.9 3.3 %collective-permute-start = (bf16[512,768]{1,0:T(8,128)(2,1)}, bf16[512,768]{1,0:T(8,128)(2,1)S(1)}, u32[]{:S(2)}, u32[]{:S(2)}) collective-permute-start(bf16[512,768]{1,0:T(8,128)(2,1)} %cut.3), channel_id=1, source_target_pairs={{0,64},{64,0},{1,65},{65,1},{2,66},{66,2},{3,67},{67,3},{4,68},{68... | collective-permute-start | bytes 2359304 | tf_op jit(solution)/shard_map/ppermute | solution.py:245
  17.6 3.5 %collective-permute-start.1 = (bf16[16,16,256]{2,1,0:T(8,128)(2,1)}, bf16[16,16,256]{2,1,0:T(8,128)(2,1)S(1)}, u32[]{:S(2)}, u32[]{:S(2)}) collective-permute-start(bf16[16,16,256]{2,1,0:T(8,128)(2,1)} %bitcast.72), channel_id=1, source_target_pairs={{0,4},{4,8},{8,12},{1,5},{5,9},{9,13},{2,6},{6,10},{10,14},{3,7},{... | collective-permute-start | bytes 393224 | tf_op jit(solution)/shard_map/ppermute | solution.py:251
  21.2 1.9 collective-permute-start.2
  23.1 2.5 cut.2
  26.3 9.1 %collective-permute-done.2.halo_ref = bf16[16,16,256]{2,1,0:T(8,128)(2,1)S(1)} collective-permute-done((bf16[16,16,256]{2,1,0:T(8,128)(2,1)S(1)}, bf16[16,16,256]{2,1,0:T(8,128)(2,1)S(1)}, u32[]{:S(2)}, u32[]{:S(2)}) %collective-permute-start.2) | collective-permute-done | bytes 131104 | tf_op jit(solution)/shard_map/ppermute | solution.py:253
  35.4 3.3 %collective-permute-start.3 = (bf16[512,1280]{1,0:T(8,128)(2,1)}, bf16[512,1280]{1,0:T(8,128)(2,1)}, u32[]{:S(2)}, u32[]{:S(2)}) collective-permute-start(bf16[512,1280]{1,0:T(8,128)(2,1)} %cut.2), channel_id=1, source_target_pairs={{0,64},{64,0},{1,65},{65,1},{2,66},{66,2},{3,67},{67,3},{4,68},{68... | collective-permute-start | bytes 3932168 | tf_op jit(solution)/shard_map/ppermute | solution.py:245
  38.8 4.4 %own_tokens.1.refs_0_ = bf16[16,528,256]{2,1,0:T(8,128)(2,1)} custom-call(s32[1]{0:T(128)} %bitcast.9.at_ref, bf16[16,16,256]{2,1,0:T(8,128)(2,1)} %copy-done.11, bf16[512,8192]{1,0:T(8,128)(2,1)} %bitcast.83), custom_call_target="tpu_custom_call" | custom-call | bytes 8650752 | tf_op jit(solution)/shard_map/own_tokens/pallas_call | solution.py:108
  43.2 23.6 %collective-permute-done.3.refs_1_ = bf16[512,1280]{1,0:T(8,128)(2,1)} collective-permute-done((bf16[512,1280]{1,0:T(8,128)(2,1)}, bf16[512,1280]{1,0:T(8,128)(2,1)}, u32[]{:S(2)}, u32[]{:S(2)}) %collective-permute-start.3) | collective-permute-done | bytes 1310752 | tf_op jit(solution)/shard_map/ppermute | solution.py:245
  66.8 3.2 %collective-permute-start.6 = (bf16[2,512,256]{2,1,0:T(8,128)(2,1)S(1)}, bf16[2,512,256]{2,1,0:T(8,128)(2,1)S(1)}, u32[]{:S(2)}, u32[]{:S(2)}) collective-permute-start(bf16[2,512,256]{2,1,0:T(8,128)(2,1)S(1)} %constant_dynamic-slice_fusion.2), channel_id=1, source_target_pairs={{0,64},{64,0},{1,65},{65,1},{2,66},{66,2},{3,67},{67,3},{4,68},{68... | collective-permute-start | bytes 1572872 | tf_op jit(solution)/shard_map/ppermute | solution.py:245
  73.8 4.4 %partner_tokens.1.refs_1_ = bf16[16,528,256]{2,1,0:T(8,128)(2,1)} custom-call(s32[1]{0:T(128)} %bitcast.1.at_ref, bf16[16,16,256]{2,1,0:T(8,128)(2,1)} %copy-done.10, bf16[512,768]{1,0:T(8,128)(2,1)} %copy-done.8, bf16[512,1280]{1,0:T(8,128)(2,1)} %collective-permute-done.3.refs_1_, bf16[512,768]{1,0:T(8,128)(2,1)} %collective-permute-done.4.refs_2_, ...), custom_call_target="tpu_custom_call" | custom-call | bytes 8650752 | tf_op jit(solution)/shard_map/partner_tokens/pallas_call | solution.py:108
  78.2 4.5 %collective-permute-done.6 = bf16[2,512,256]{2,1,0:T(8,128)(2,1)S(1)} collective-permute-done((bf16[2,512,256]{2,1,0:T(8,128)(2,1)S(1)}, bf16[2,512,256]{2,1,0:T(8,128)(2,1)S(1)}, u32[]{:S(2)}, u32[]{:S(2)}) %collective-permute-start.6) | collective-permute-done | bytes 524320 | tf_op jit(solution)/shard_map/ppermute | solution.py:245
  82.7 2.8 %collective-permute-start.7 = (s32[2]{0:T(128)S(1)}, s32[2]{0:T(128)S(1)}, u32[]{:S(2)}, u32[]{:S(2)}) collective-permute-start(s32[2]{0:T(128)S(1)} %pad_add_fusion.1), channel_id=1, source_target_pairs={{0,48},{16,0},{32,16},{48,32},{1,49},{17,1},{33,17},{49,33},{2,50}... | collective-permute-start | bytes 32 | tf_op jit(solution)/shard_map/ppermute | solution.py:40
  87.1 3.4 %collective-permute-done.8 = s32[2]{0:T(128)S(1)} collective-permute-done((s32[2]{0:T(128)S(1)}, s32[2]{0:T(128)S(1)}, u32[]{:S(2)}, u32[]{:S(2)}) %collective-permute-start.8) | collective-permute-done | bytes 40 | tf_op jit(solution)/shard_map/ppermute | solution.py:40
  91.0 28.2 %all-gather.4.cloned.1.call-done.refs_2_.refs_3_.refs_4_.refs_5_ = bf16[4096,1920]{1,0:T(8,128)(2,1)} async-done(((bf16[256,1920]{1,0:T(8,128)(2,1)}), bf16[4096,1920]{1,0:T(8,128)(2,1)}) %all-gather.4.cloned.1.call-update) | async-done | bytes 15728656 | tf_op jit(solution)/shard_map/all_gather | solution.py:287
  120.1 8.8 %project.4 = (f32[528,384]{1,0:T(8,128)}, bf16[528,512]{1,0:T(8,128)(2,1)}) custom-call(s32[16]{0:T(128)} %iota.14.places_ref, bf16[16,528,256]{2,1,0:T(8,128)(2,1)} %own_tokens.1.refs_0_, bf16[16,528,256]{2,1,0:T(8,128)(2,1)} %partner_tokens.1.refs_1_, bf16[4096,1920]{1,0:T(8,128)(2,1)} %all-gather.4.cloned.1.call-done.refs_2_.refs_3_.refs_4_.refs_5_, ...), custom_call_target="tpu_custom_call" | custom-call | flops 3321888768 | bytes 11845728 | tf_op jit(solution)/shard_map/project/pallas_call | solution.py:183
  129.3 2.5 collective-permute-start.12
  131.8 1.5 collective-permute-start.13
  133.3 3.0 %collective-permute-start.10 = (bf16[528,512]{1,0:T(8,128)(2,1)}, bf16[528,512]{1,0:T(8,128)(2,1)S(1)}, u32[]{:S(2)}, u32[]{:S(2)}) collective-permute-start(bf16[528,512]{1,0:T(8,128)(2,1)} %get-tuple-element.75), channel_id=1, source_target_pairs={{0,64},{64,0},{1,65},{65,1},{2,66},{66,2},{3,67},{67,3},{4,68},{68... | collective-permute-start | bytes 1622024 | tf_op jit(solution)/shard_map/ppermute | solution.py:245
  136.8 11.5 %project.5 = (f32[528,768]{1,0:T(8,128)}, bf16[528,768]{1,0:T(8,128)(2,1)}) custom-call(s32[16]{0:T(128)} %iota.15.places_ref, bf16[16,528,256]{2,1,0:T(8,128)(2,1)} %own_tokens.1.refs_0_, bf16[16,528,256]{2,1,0:T(8,128)(2,1)} %partner_tokens.1.refs_1_, bf16[4096,1920]{1,0:T(8,128)(2,1)} %all-gather.4.cloned.1.call-done.refs_2_.refs_3_.refs_4_.refs_5_, ...), custom_call_target="tpu_custom_call" | custom-call | flops 6643777536 | bytes 14991456 | tf_op jit(solution)/shard_map/project/pallas_call | solution.py:183
  149.0 1.3 collective-permute-start.15
  150.8 11.5 %project.6 = (f32[528,768]{1,0:T(8,128)}, bf16[528,768]{1,0:T(8,128)(2,1)}) custom-call(s32[16]{0:T(128)} %iota.16.places_ref, bf16[16,528,256]{2,1,0:T(8,128)(2,1)} %own_tokens.1.refs_0_, bf16[16,528,256]{2,1,0:T(8,128)(2,1)} %partner_tokens.1.refs_1_, bf16[4096,1920]{1,0:T(8,128)(2,1)} %all-gather.4.cloned.1.call-done.refs_2_.refs_3_.refs_4_.refs_5_, ...), custom_call_target="tpu_custom_call" | custom-call | flops 6643777536 | bytes 14991456 | tf_op jit(solution)/shard_map/project/pallas_call | solution.py:183
  162.3 2.8 %activate.4 = (bf16[512,256]{1,0:T(8,128)(2,1)}, f32[512,32]{1,0:T(8,128)}) custom-call(s32[2]{0:T(128)} %pad_add_fusion.info_ref.refs_0_, f32[528,384]{1,0:T(8,128)} %get-tuple-element.92.own_ref, bf16[528,512]{1,0:T(8,128)(2,1)} %copy-done.9, f32[4,2304]{1,0:T(4,128)} %refs_3_.5, f32[1,2304]{1,0:T(1,128)} %broadcast_in_dim.51.bias_ref.refs_4_), custom_call_target="tpu_custom_call" | custom-call | flops 33554432 | bytes 270336 | tf_op jit(solution)/shard_map/activate/pallas_call | solution.py:232
  165.1 1.2 broadcast_multiply_fusion
  169.5 3.0 %collective-permute-start.17 = (bf16[528,768]{1,0:T(8,128)(2,1)}, bf16[528,768]{1,0:T(8,128)(2,1)}, u32[]{:S(2)}, u32[]{:S(2)}) collective-permute-start(bf16[528,768]{1,0:T(8,128)(2,1)} %get-tuple-element.98), channel_id=1, source_target_pairs={{0,64},{64,0},{1,65},{65,1},{2,66},{66,2},{3,67},{67,3},{4,68},{68... | collective-permute-start | bytes 2433032 | tf_op jit(solution)/shard_map/ppermute | solution.py:245
  174.7 4.9 %activate.5 = f32[768,256]{1,0:T(8,128)} custom-call(s32[2]{0:T(128)} %pad_add_fusion.info_ref.refs_0_, f32[528,768]{1,0:T(8,128)} %get-tuple-element.90.refs_1_, bf16[528,768]{1,0:T(8,128)(2,1)} %copy-done.7, f32[4,2304]{1,0:T(4,128)} %refs_3_.5, f32[1,2304]{1,0:T(1,128)} %broadcast_in_dim.51.bias_ref.refs_4_, f32[512,32]{1,0:T(8,128)} %exponential_multiply_fusion.refs_5_, ...), custom_call_target="tpu_custom_call" | custom-call | flops 100663296 | bytes 811008 | tf_op jit(solution)/shard_map/activate/pallas_call | solution.py:232
  179.6 6.9 %collective-permute-done.16 = bf16[1024,256]{1,0:T(8,128)(2,1)S(1)} collective-permute-done((bf16[1024,256]{1,0:T(8,128)(2,1)S(1)}, bf16[1024,256]{1,0:T(8,128)(2,1)S(1)}, u32[]{:S(2)}, u32[]{:S(2)}) %collective-permute-start.16) | collective-permute-done | bytes 524320 | tf_op jit(solution)/shard_map/ppermute | solution.py:276
  186.9 2.9 %collective-permute-done.17.refs_2_ = bf16[528,768]{1,0:T(8,128)(2,1)} collective-permute-done((bf16[528,768]{1,0:T(8,128)(2,1)}, bf16[528,768]{1,0:T(8,128)(2,1)}, u32[]{:S(2)}, u32[]{:S(2)}) %collective-permute-start.17) | collective-permute-done | bytes 811040 | tf_op jit(solution)/shard_map/ppermute | solution.py:245
  189.8 3.7 %collective-permute-start.19 = (bf16[768,256]{1,0:T(8,128)(2,1)S(1)}, bf16[768,256]{1,0:T(8,128)(2,1)S(1)}, u32[]{:S(2)}, u32[]{:S(2)}) collective-permute-start(bf16[768,256]{1,0:T(8,128)(2,1)S(1)} %convert_element_type.55), channel_id=1, source_target_pairs={{0,4},{4,8},{8,12},{1,5},{5,9},{9,13},{2,6},{6,10},{10,14},{3,7},{... | collective-permute-start | bytes 1179656 | tf_op jit(solution)/shard_map/ppermute | solution.py:257
  193.5 1.4 collective-permute-start.20
  194.9 4.9 %activate.6 = f32[768,256]{1,0:T(8,128)} custom-call(s32[2]{0:T(128)} %pad_add_fusion.info_ref.refs_0_, f32[528,768]{1,0:T(8,128)} %get-tuple-element.100.refs_1_, bf16[528,768]{1,0:T(8,128)(2,1)} %collective-permute-done.17.refs_2_, f32[4,2304]{1,0:T(4,128)} %refs_3_.5, f32[1,2304]{1,0:T(1,128)} %broadcast_in_dim.51.bias_ref.refs_4_, ...), custom_call_target="tpu_custom_call" | custom-call | flops 100663296 | bytes 811008 | tf_op jit(solution)/shard_map/activate/pallas_call | solution.py:232
  199.8 1.3 select_add_fusion
  201.6 9.0 %project.7 = (f32[528,512]{1,0:T(8,128)}, bf16[528,512]{1,0:T(8,128)(2,1)}) custom-call(s32[16]{0:T(128)} %iota.18.places_ref, bf16[16,528,256]{2,1,0:T(8,128)(2,1)} %own_tokens.1.refs_0_, bf16[16,528,256]{2,1,0:T(8,128)(2,1)} %partner_tokens.1.refs_1_, bf16[4096,512]{1,0:T(8,128)(2,1)} %all-gather.6.cloned.1.call-done.refs_2_.refs_3_.refs_4_.refs_5_, ...), custom_call_target="tpu_custom_call" | custom-call | flops 4429185024 | bytes 12894304 | tf_op jit(solution)/shard_map/project/pallas_call | solution.py:183
  210.6 3.1 %collective-permute-start.18 = (bf16[528,512]{1,0:T(8,128)(2,1)}, bf16[528,512]{1,0:T(8,128)(2,1)}, u32[]{:S(2)}, u32[]{:S(2)}) collective-permute-start(bf16[528,512]{1,0:T(8,128)(2,1)} %get-tuple-element.103), channel_id=1, source_target_pairs={{0,64},{64,0},{1,65},{65,1},{2,66},{66,2},{3,67},{67,3},{4,68},{68... | collective-permute-start | bytes 1622024 | tf_op jit(solution)/shard_map/ppermute | solution.py:245
  213.8 1.9 collective-permute-start.22
  215.7 1.4 collective-permute-start.23
  217.1 1.9 collective-permute-start.21
  220.8 12.2 %all-reduce = f32[128]{0:T(128)S(1)} all-reduce(f32[128]{0:T(128)S(1)} %dynamic-update-slice), channel_id=2, replica_groups=mesh['yh'=2,'x'=4,'z'=4,'yl'=2,'core'=2] {'z'}, use_global_device_ids=true, to_apply=%add | all-reduce | flops 128 | bytes 1024
  233.4 3.9 %activate.7 = f32[512,256]{1,0:T(8,128)} custom-call(s32[2]{0:T(128)} %pad_add_fusion.info_ref.refs_0_, f32[528,512]{1,0:T(8,128)} %get-tuple-element.115.refs_1_, bf16[528,512]{1,0:T(8,128)(2,1)} %collective-permute-done.18.refs_2_, f32[4,2304]{1,0:T(4,128)} %refs_3_.5, f32[1,2304]{1,0:T(1,128)} %broadcast_in_dim.51.bias_ref.refs_4_, ...), custom_call_target="tpu_custom_call" | custom-call | flops 67108864 | bytes 540672 | tf_op jit(solution)/shard_map/activate/pallas_call | solution.py:232
  238.5 4.2 %collective-permute-start.25 = (bf16[512,256]{1,0:T(8,128)(2,1)S(1)}, bf16[512,256]{1,0:T(8,128)(2,1)S(1)}, u32[]{:S(2)}, u32[]{:S(2)}) collective-permute-start(bf16[512,256]{1,0:T(8,128)(2,1)S(1)} %fusion), channel_id=1, source_target_pairs={{0,4},{4,8},{8,12},{1,5},{5,9},{9,13},{2,6},{6,10},{10,14},{3,7},{... | collective-permute-start | bytes 786440 | tf_op jit(solution)/shard_map/ppermute | solution.py:257
  243.4 1.9 collective-permute-start.24
  245.4 1.5 add_add_fusion.1
  246.9 2.6 collective-permute-done.25
  249.6 4.2 %collective-permute-start.26 = (bf16[512,256]{1,0:T(8,128)(2,1)S(1)}, bf16[512,256]{1,0:T(8,128)(2,1)S(1)}, u32[]{:S(2)}, u32[]{:S(2)}) collective-permute-start(bf16[512,256]{1,0:T(8,128)(2,1)S(1)} %collective-permute-done.25), channel_id=1, source_target_pairs={{4,8},{8,12},{5,9},{9,13},{6,10},{10,14},{7,11},{11,15},{20,24},{2... | collective-permute-start | bytes 786440 | tf_op jit(solution)/shard_map/ppermute | solution.py:344
  253.8 3.1 %collective-permute-done.24 = bf16[768,256]{1,0:T(8,128)(2,1)S(1)} collective-permute-done((bf16[768,256]{1,0:T(8,128)(2,1)}, bf16[768,256]{1,0:T(8,128)(2,1)S(1)}, u32[]{:S(2)}, u32[]{:S(2)}) %collective-permute-start.24) | collective-permute-done | bytes 393248 | tf_op jit(solution)/shard_map/ppermute | solution.py:344
  256.9 1.5 add_add_fusion
  258.5 1.3 collective-permute-done.26
  260.1 1.5 maximum_bitcast_fusion
  (124 shorter events, 23.6 us)
Async XLA Ops:
  6.5 32.2 %copy-start = (bf16[2,2048,256]{2,1,0:T(8,128)(2,1)S(1)}, bf16[2,2048,256]{2,1,0:T(8,128)(2,1)}, u32[]{:S(2)}) copy-start(bf16[2,2048,256]{2,1,0:T(8,128)(2,1)} %param.17) | copy-start | bytes 6291460
  6.5 1.9 slice-start
  6.5 112.6 %all-gather.4.cloned.1.call-start = ((), (), s32[]{:S(2)}) async-start(), calls=%async_computation | async-start | bytes 16711680 | tf_op jit(solution)/shard_map/all_gather | solution.py:287
  9.6 191.5 %all-gather.6.cloned.1.call-start = ((), (), s32[]{:S(2)}) async-start(), calls=%async_computation.1 | async-start | bytes 4456448 | tf_op jit(solution)/shard_map/all_gather | solution.py:288
  9.7 5.4 %copy-start.3 = (bf16[256,2304]{1,0:T(8,128)(2,1)S(1)}, bf16[256,2304]{1,0:T(8,128)(2,1)}, u32[]{:S(2)}) copy-start(bf16[256,2304]{1,0:T(8,128)(2,1)} %param.11) | copy-start | bytes 3538948
  11.9 23.5 %collective-permute-start = (bf16[512,768]{1,0:T(8,128)(2,1)}, bf16[512,768]{1,0:T(8,128)(2,1)S(1)}, u32[]{:S(2)}, u32[]{:S(2)}) collective-permute-start(bf16[512,768]{1,0:T(8,128)(2,1)} %cut.3), channel_id=1, source_target_pairs={{0,64},{64,0},{1,65},{65,1},{2,66},{66,2},{3,67},{67,3},{4,68},{68... | collective-permute-start | bytes 2359304 | tf_op jit(solution)/shard_map/ppermute | solution.py:245
  17.6 8.7 %collective-permute-start.1 = (bf16[16,16,256]{2,1,0:T(8,128)(2,1)}, bf16[16,16,256]{2,1,0:T(8,128)(2,1)S(1)}, u32[]{:S(2)}, u32[]{:S(2)}) collective-permute-start(bf16[16,16,256]{2,1,0:T(8,128)(2,1)} %bitcast.72), channel_id=1, source_target_pairs={{0,4},{4,8},{8,12},{1,5},{5,9},{9,13},{2,6},{6,10},{10,14},{3,7},{... | collective-permute-start | bytes 393224 | tf_op jit(solution)/shard_map/ppermute | solution.py:251
  21.2 14.2 %collective-permute-start.2 = (bf16[16,16,256]{2,1,0:T(8,128)(2,1)S(1)}, bf16[16,16,256]{2,1,0:T(8,128)(2,1)S(1)}, u32[]{:S(2)}, u32[]{:S(2)}) collective-permute-start(bf16[16,16,256]{2,1,0:T(8,128)(2,1)S(1)} %bitcast.89), channel_id=1, source_target_pairs={{0,68},{4,72},{8,76},{64,4},{68,8},{72,12},{1,69},{5,73},{9,77},{6... | collective-permute-start | bytes 393224 | tf_op jit(solution)/shard_map/ppermute | solution.py:253
  26.3 12.3 %copy-start.11 = (bf16[16,16,256]{2,1,0:T(8,128)(2,1)}, bf16[16,16,256]{2,1,0:T(8,128)(2,1)S(1)}, u32[]{:S(2)}) copy-start(bf16[16,16,256]{2,1,0:T(8,128)(2,1)S(1)} %collective-permute-done.1.halo_ref) | copy-start | bytes 393220
  35.4 3.3 %copy-start.10 = (bf16[16,16,256]{2,1,0:T(8,128)(2,1)}, bf16[16,16,256]{2,1,0:T(8,128)(2,1)S(1)}, u32[]{:S(2)}) copy-start(bf16[16,16,256]{2,1,0:T(8,128)(2,1)S(1)} %collective-permute-done.2.halo_ref) | copy-start | bytes 393220
  35.4 7.8 %copy-start.8 = (bf16[512,768]{1,0:T(8,128)(2,1)}, bf16[512,768]{1,0:T(8,128)(2,1)S(1)}, u32[]{:S(2)}) copy-start(bf16[512,768]{1,0:T(8,128)(2,1)S(1)} %collective-permute-done.refs_0_) | copy-start | bytes 2359300
  35.4 31.4 %collective-permute-start.3 = (bf16[512,1280]{1,0:T(8,128)(2,1)}, bf16[512,1280]{1,0:T(8,128)(2,1)}, u32[]{:S(2)}, u32[]{:S(2)}) collective-permute-start(bf16[512,1280]{1,0:T(8,128)(2,1)} %cut.2), channel_id=1, source_target_pairs={{0,64},{64,0},{1,65},{65,1},{2,66},{66,2},{3,67},{67,3},{4,68},{68... | collective-permute-start | bytes 3932168 | tf_op jit(solution)/shard_map/ppermute | solution.py:245
  38.7 4.6 %collective-permute-start.4 = (bf16[512,768]{1,0:T(8,128)(2,1)S(1)}, bf16[512,768]{1,0:T(8,128)(2,1)}, u32[]{:S(2)}, u32[]{:S(2)}) collective-permute-start(bf16[512,768]{1,0:T(8,128)(2,1)S(1)} %collective-permute-done.refs_0_), channel_id=1, source_target_pairs={{0,1},{1,0},{2,3},{3,2},{4,5},{5,4},{6,7},{7,6},{8,9},{9,8},{10,11... | collective-permute-start | bytes 2359304 | tf_op jit(solution)/shard_map/ppermute | solution.py:245
  38.7 32.6 %copy-start.12 = (f32[2304]{0:T(1024)S(1)}, f32[2304]{0:T(1024)}, u32[]{:S(2)}) copy-start(f32[2304]{0:T(1024)} %param.14) | copy-start | bytes 27652
  38.8 33.2 %copy-start.14 = (f32[32]{0:T(128)S(1)}, f32[32]{0:T(128)}, u32[]{:S(2)}) copy-start(f32[32]{0:T(128)} %param.16) | copy-start | bytes 388
  66.8 5.9 %collective-permute-start.5 = (bf16[512,1280]{1,0:T(8,128)(2,1)}, bf16[512,1280]{1,0:T(8,128)(2,1)S(1)}, u32[]{:S(2)}, u32[]{:S(2)}) collective-permute-start(bf16[512,1280]{1,0:T(8,128)(2,1)} %collective-permute-done.3.refs_1_), channel_id=1, source_target_pairs={{0,1},{1,0},{2,3},{3,2},{4,5},{5,4},{6,7},{7,6},{8,9},{9,8},{10,11... | collective-permute-start | bytes 3932168 | tf_op jit(solution)/shard_map/ppermute | solution.py:245
  66.8 15.8 %collective-permute-start.6 = (bf16[2,512,256]{2,1,0:T(8,128)(2,1)S(1)}, bf16[2,512,256]{2,1,0:T(8,128)(2,1)S(1)}, u32[]{:S(2)}, u32[]{:S(2)}) collective-permute-start(bf16[2,512,256]{2,1,0:T(8,128)(2,1)S(1)} %constant_dynamic-slice_fusion.2), channel_id=1, source_target_pairs={{0,64},{64,0},{1,65},{65,1},{2,66},{66,2},{3,67},{67,3},{4,68},{68... | collective-permute-start | bytes 1572872 | tf_op jit(solution)/shard_map/ppermute | solution.py:245
  72.7 1.1 copy-start.5
  82.7 4.4 %collective-permute-start.7 = (s32[2]{0:T(128)S(1)}, s32[2]{0:T(128)S(1)}, u32[]{:S(2)}, u32[]{:S(2)}) collective-permute-start(s32[2]{0:T(128)S(1)} %pad_add_fusion.1), channel_id=1, source_target_pairs={{0,48},{16,0},{32,16},{48,32},{1,49},{17,1},{33,17},{49,33},{2,50}... | collective-permute-start | bytes 32 | tf_op jit(solution)/shard_map/ppermute | solution.py:40
  85.4 5.0 %collective-permute-start.8 = (s32[2]{0:T(128)S(1)}, s32[2]{0:T(128)S(1)}, u32[]{:S(2)}, u32[]{:S(2)}) collective-permute-start(s32[2]{0:T(128)S(1)} %pad_add_fusion.1), channel_id=1, source_target_pairs={{0,32},{16,48},{32,0},{48,16},{1,33},{17,49},{33,1},{49,17},{2,34}... | collective-permute-start | bytes 32 | tf_op jit(solution)/shard_map/ppermute | solution.py:40
  86.2 4.8 %collective-permute-start.9 = (s32[2]{0:T(128)S(1)}, s32[2]{0:T(128)S(1)}, u32[]{:S(2)}, u32[]{:S(2)}) collective-permute-start(s32[2]{0:T(128)S(1)} %pad_add_fusion.1), channel_id=1, source_target_pairs={{0,16},{16,32},{32,48},{48,0},{1,17},{17,33},{33,49},{49,1},{2,18}... | collective-permute-start | bytes 32 | tf_op jit(solution)/shard_map/ppermute | solution.py:40
  129.0 19.9 %collective-permute-start.11 = (bf16[512,256]{1,0:T(8,128)(2,1)S(1)}, bf16[512,256]{1,0:T(8,128)(2,1)S(1)}, u32[]{:S(2)}, u32[]{:S(2)}) collective-permute-start(bf16[512,256]{1,0:T(8,128)(2,1)S(1)} %get-tuple-element.123), channel_id=1, source_target_pairs={{0,16},{16,32},{32,48},{48,0},{1,17},{17,33},{33,49},{49,1},{2,18}... | collective-permute-start | bytes 786440 | tf_op jit(solution)/shard_map/ppermute | solution.py:40
  129.3 19.6 %collective-permute-start.12 = (bf16[512,256]{1,0:T(8,128)(2,1)S(1)}, bf16[512,256]{1,0:T(8,128)(2,1)S(1)}, u32[]{:S(2)}, u32[]{:S(2)}) collective-permute-start(bf16[512,256]{1,0:T(8,128)(2,1)S(1)} %get-tuple-element.124), channel_id=1, source_target_pairs={{0,32},{16,48},{32,0},{48,16},{1,33},{17,49},{33,1},{49,17},{2,34}... | collective-permute-start | bytes 786440 | tf_op jit(solution)/shard_map/ppermute | solution.py:40
  131.8 17.1 %collective-permute-start.13 = (bf16[512,256]{1,0:T(8,128)(2,1)S(1)}, bf16[512,256]{1,0:T(8,128)(2,1)S(1)}, u32[]{:S(2)}, u32[]{:S(2)}) collective-permute-start(bf16[512,256]{1,0:T(8,128)(2,1)S(1)} %select_bitcast_fusion), channel_id=1, source_target_pairs={{0,48},{16,0},{32,16},{48,32},{1,49},{17,1},{33,17},{49,33},{2,50}... | collective-permute-start | bytes 786440 | tf_op jit(solution)/shard_map/ppermute | solution.py:40
  133.3 15.7 %collective-permute-start.10 = (bf16[528,512]{1,0:T(8,128)(2,1)}, bf16[528,512]{1,0:T(8,128)(2,1)S(1)}, u32[]{:S(2)}, u32[]{:S(2)}) collective-permute-start(bf16[528,512]{1,0:T(8,128)(2,1)} %get-tuple-element.75), channel_id=1, source_target_pairs={{0,64},{64,0},{1,65},{65,1},{2,66},{66,2},{3,67},{67,3},{4,68},{68... | collective-permute-start | bytes 1622024 | tf_op jit(solution)/shard_map/ppermute | solution.py:245
  148.3 25.4 %collective-permute-start.14 = (bf16[528,768]{1,0:T(8,128)(2,1)}, bf16[528,768]{1,0:T(8,128)(2,1)S(1)}, u32[]{:S(2)}, u32[]{:S(2)}) collective-permute-start(bf16[528,768]{1,0:T(8,128)(2,1)} %get-tuple-element.84), channel_id=1, source_target_pairs={{0,64},{64,0},{1,65},{65,1},{2,66},{66,2},{3,67},{67,3},{4,68},{68... | collective-permute-start | bytes 2433032 | tf_op jit(solution)/shard_map/ppermute | solution.py:245
  149.0 13.3 %copy-start.9 = (bf16[528,512]{1,0:T(8,128)(2,1)}, bf16[528,512]{1,0:T(8,128)(2,1)S(1)}, u32[]{:S(2)}) copy-start(bf16[528,512]{1,0:T(8,128)(2,1)S(1)} %collective-permute-done.10.other_ref) | copy-start | bytes 1622020
  149.0 19.0 %collective-permute-start.15 = (bf16[512,256]{1,0:T(8,128)(2,1)S(1)}, bf16[512,256]{1,0:T(8,128)(2,1)S(1)}, u32[]{:S(2)}, u32[]{:S(2)}) collective-permute-start(bf16[512,256]{1,0:T(8,128)(2,1)S(1)} %fusion.3), channel_id=1, source_target_pairs={{0,4},{4,0},{8,12},{12,8},{1,5},{5,1},{9,13},{13,9},{2,6},{6,2},{1... | collective-permute-start | bytes 786440 | tf_op jit(solution)/shard_map/ppermute | solution.py:274
  150.8 14.3 %copy-start.13 = (f32[32]{0:T(128)S(1)}, f32[32]{0:T(128)}, u32[]{:S(2)}) copy-start(f32[32]{0:T(128)} %param.15) | copy-start | bytes 388
  165.1 7.7 %copy-start.6 = (f32[512,32]{1,0:T(8,128)S(1)}, f32[512,32]{1,0:T(8,128)}, u32[]{:S(2)}) copy-start(f32[512,32]{1,0:T(8,128)} %get-tuple-element.94) | copy-start | bytes 196612
  168.3 18.1 %collective-permute-start.16 = (bf16[1024,256]{1,0:T(8,128)(2,1)S(1)}, bf16[1024,256]{1,0:T(8,128)(2,1)S(1)}, u32[]{:S(2)}, u32[]{:S(2)}) collective-permute-start(bf16[1024,256]{1,0:T(8,128)(2,1)S(1)} %maximum_select_fusion.1), channel_id=1, source_target_pairs={{8,0},{12,4},{0,8},{4,12},{9,1},{13,5},{1,9},{5,13},{10,2},{14,6},... | collective-permute-start | bytes 1572872 | tf_op jit(solution)/shard_map/ppermute | solution.py:276
  169.5 20.3 %collective-permute-start.17 = (bf16[528,768]{1,0:T(8,128)(2,1)}, bf16[528,768]{1,0:T(8,128)(2,1)}, u32[]{:S(2)}, u32[]{:S(2)}) collective-permute-start(bf16[528,768]{1,0:T(8,128)(2,1)} %get-tuple-element.98), channel_id=1, source_target_pairs={{0,64},{64,0},{1,65},{65,1},{2,66},{66,2},{3,67},{67,3},{4,68},{68... | collective-permute-start | bytes 2433032 | tf_op jit(solution)/shard_map/ppermute | solution.py:245
  173.8 0.9 copy-start.7
  179.5 7.1 %copy-start.4 = (f32[768,256]{1,0:T(8,128)S(1)}, f32[768,256]{1,0:T(8,128)}, u32[]{:S(2)}) copy-start(f32[768,256]{1,0:T(8,128)} %activate.5) | copy-start | bytes 2359300
  189.8 23.9 %collective-permute-start.19 = (bf16[768,256]{1,0:T(8,128)(2,1)S(1)}, bf16[768,256]{1,0:T(8,128)(2,1)S(1)}, u32[]{:S(2)}, u32[]{:S(2)}) collective-permute-start(bf16[768,256]{1,0:T(8,128)(2,1)S(1)} %convert_element_type.55), channel_id=1, source_target_pairs={{0,4},{4,8},{8,12},{1,5},{5,9},{9,13},{2,6},{6,10},{10,14},{3,7},{... | collective-permute-start | bytes 1179656 | tf_op jit(solution)/shard_map/ppermute | solution.py:257
  193.5 20.2 %collective-permute-start.20 = (bf16[768,256]{1,0:T(8,128)(2,1)S(1)}, bf16[768,256]{1,0:T(8,128)(2,1)}, u32[]{:S(2)}, u32[]{:S(2)}) collective-permute-start(bf16[768,256]{1,0:T(8,128)(2,1)S(1)} %convert_element_type.55), channel_id=1, source_target_pairs={{0,12},{1,13},{2,14},{3,15},{16,28},{17,29},{18,30},{19,31},{32,44... | collective-permute-start | bytes 1179656 | tf_op jit(solution)/shard_map/ppermute | solution.py:341
  201.6 17.4 %copy-start.15 = (u32[128]{0:T(128)S(1)}, u32[128]{0:T(128)}, u32[]{:S(2)}) copy-start(u32[128]{0:T(128)} %constant.87) | copy-start | bytes 1540
  210.6 22.7 %collective-permute-start.18 = (bf16[528,512]{1,0:T(8,128)(2,1)}, bf16[528,512]{1,0:T(8,128)(2,1)}, u32[]{:S(2)}, u32[]{:S(2)}) collective-permute-start(bf16[528,512]{1,0:T(8,128)(2,1)} %get-tuple-element.103), channel_id=1, source_target_pairs={{0,64},{64,0},{1,65},{65,1},{2,66},{66,2},{3,67},{67,3},{4,68},{68... | collective-permute-start | bytes 1622024 | tf_op jit(solution)/shard_map/ppermute | solution.py:245
  213.8 19.6 %collective-permute-start.22 = (bf16[768,256]{1,0:T(8,128)(2,1)S(1)}, bf16[768,256]{1,0:T(8,128)(2,1)}, u32[]{:S(2)}, u32[]{:S(2)}) collective-permute-start(bf16[768,256]{1,0:T(8,128)(2,1)S(1)} %convert_element_type.56), channel_id=1, source_target_pairs={{0,4},{4,8},{8,12},{1,5},{5,9},{9,13},{2,6},{6,10},{10,14},{3,7},{... | collective-permute-start | bytes 1179656 | tf_op jit(solution)/shard_map/ppermute | solution.py:257
  215.7 17.7 %collective-permute-start.23 = (bf16[768,256]{1,0:T(8,128)(2,1)S(1)}, bf16[768,256]{1,0:T(8,128)(2,1)}, u32[]{:S(2)}, u32[]{:S(2)}) collective-permute-start(bf16[768,256]{1,0:T(8,128)(2,1)S(1)} %convert_element_type.56), channel_id=1, source_target_pairs={{0,12},{1,13},{2,14},{3,15},{16,28},{17,29},{18,30},{19,31},{32,44... | collective-permute-start | bytes 1179656 | tf_op jit(solution)/shard_map/ppermute | solution.py:341
  217.1 16.3 %collective-permute-start.21 = (bf16[768,256]{1,0:T(8,128)(2,1)S(1)}, bf16[768,256]{1,0:T(8,128)(2,1)}, u32[]{:S(2)}, u32[]{:S(2)}) collective-permute-start(bf16[768,256]{1,0:T(8,128)(2,1)S(1)} %collective-permute-done.19), channel_id=1, source_target_pairs={{4,8},{8,12},{5,9},{9,13},{6,10},{10,14},{7,11},{11,15},{20,24},{2... | collective-permute-start | bytes 1179656 | tf_op jit(solution)/shard_map/ppermute | solution.py:344
  238.5 11.1 %collective-permute-start.25 = (bf16[512,256]{1,0:T(8,128)(2,1)S(1)}, bf16[512,256]{1,0:T(8,128)(2,1)S(1)}, u32[]{:S(2)}, u32[]{:S(2)}) collective-permute-start(bf16[512,256]{1,0:T(8,128)(2,1)S(1)} %fusion), channel_id=1, source_target_pairs={{0,4},{4,8},{8,12},{1,5},{5,9},{9,13},{2,6},{6,10},{10,14},{3,7},{... | collective-permute-start | bytes 786440 | tf_op jit(solution)/shard_map/ppermute | solution.py:257
  242.7 15.8 %collective-permute-start.27 = (bf16[512,256]{1,0:T(8,128)(2,1)S(1)}, bf16[512,256]{1,0:T(8,128)(2,1)S(1)}, u32[]{:S(2)}, u32[]{:S(2)}) collective-permute-start(bf16[512,256]{1,0:T(8,128)(2,1)S(1)} %fusion), channel_id=1, source_target_pairs={{0,12},{1,13},{2,14},{3,15},{16,28},{17,29},{18,30},{19,31},{32,44... | collective-permute-start | bytes 786440 | tf_op jit(solution)/shard_map/ppermute | solution.py:341
  243.4 13.6 %collective-permute-start.24 = (bf16[768,256]{1,0:T(8,128)(2,1)}, bf16[768,256]{1,0:T(8,128)(2,1)S(1)}, u32[]{:S(2)}, u32[]{:S(2)}) collective-permute-start(bf16[768,256]{1,0:T(8,128)(2,1)} %collective-permute-done.22), channel_id=1, source_target_pairs={{4,8},{8,12},{5,9},{9,13},{6,10},{10,14},{7,11},{11,15},{20,24},{2... | collective-permute-start | bytes 1179656 | tf_op jit(solution)/shard_map/ppermute | solution.py:344
  245.4 14.4 %copy-start.2 = (f32[512,256]{1,0:T(8,128)S(1)}, f32[512,256]{1,0:T(8,128)}, u32[]{:S(2)}) copy-start(f32[512,256]{1,0:T(8,128)} %activate.7) | copy-start | bytes 1572868
  249.6 10.2 %collective-permute-start.26 = (bf16[512,256]{1,0:T(8,128)(2,1)S(1)}, bf16[512,256]{1,0:T(8,128)(2,1)S(1)}, u32[]{:S(2)}, u32[]{:S(2)}) collective-permute-start(bf16[512,256]{1,0:T(8,128)(2,1)S(1)} %collective-permute-done.25), channel_id=1, source_target_pairs={{4,8},{8,12},{5,9},{9,13},{6,10},{10,14},{7,11},{11,15},{20,24},{2... | collective-permute-start | bytes 786440 | tf_op jit(solution)/shard_map/ppermute | solution.py:344
  259.8 1.9 copy-start.1
Sparse Core Ops, SparseCore 0:
  9.7 109.3 all-gather.3
  121.3 59.8 all-gather.5

commit v3 on v2

--- a/solution.py
+++ b/solution.py
@@ -173,18 +173,16 @@
                 elif steps:
                     outs[1][:, :N] = total[:, :N].astype(BF16)
                     exact = total[:, N:]
-                    high = exact.astype(BF16)
-                    outs[1][:, N : N + 128] = high
-                    outs[1][:, N + 128 :] = (exact - high.astype(F32)).astype(BF16)
+                    high = exact.astype(BF16).astype(F32)
+                    outs[1][:, N:] = (high + pltpu.roll(exact - high, GROUP_HEADS, 1)).astype(BF16)
                 else:
                     outs[1][...] = total.astype(BF16)
 
-    their_width = width + 128 if steps else width
     return pl.pallas_call(
         kernel,
         out_shape=(
             jax.ShapeDtypeStruct((LONG, width), F32),
-            jax.ShapeDtypeStruct((LONG, their_width), BF16 if final else F32),
+            jax.ShapeDtypeStruct((LONG, width), BF16 if final else F32),
         ),
         in_specs=[SMEM] + [ANY] * (2 + n_totals + n_blocks),
         out_specs=(VMEM, VMEM),
@@ -211,7 +209,8 @@
 def state_kernel(info_ref, own_ref, other_ref, taps_ref, bias_ref, states_out, steps_out, masked):
     projected = own_ref[:, :N] + other_ref[:, :N].astype(F32)
     states_out[...] = activate(info_ref, projected, taps_ref, bias_ref, HEAD_COLUMNS, masked)
-    steps = own_ref[HALO:, N : N + 128] + other_ref[HALO:, N : N + 128].astype(F32) + other_ref[HALO:, N + 128 :].astype(F32)
+    sent = other_ref[HALO:, N:].astype(F32)
+    steps = own_ref[HALO:, N:] + sent + pltpu.roll(sent, 128 - GROUP_HEADS, 1)
     steps_out[...] = steps[:, :GROUP_HEADS]
 
 
@@ -324,8 +323,6 @@
     own = run("a", early, STATE_WIDTH)
     early, projected["states"][1], projected["a"][0], found = together(early, projected["states"][1], own, found)
     initial = all_rows(found)
-    own = run("b", early, STATE_WIDTH + CHUNKS["b"][0])
-    projected["b"][0], projected["states"] = together(own, projected["states"])
     out = (jax.ShapeDtypeStruct((ROWS, N), BF16), jax.ShapeDtypeStruct((ROWS, GROUP_HEADS), F32))
     states, step_raw = call(state_kernel, out, N, info, *projected["states"], conv_weight, conv_bias[None])
     valid = (z * ROWS + jnp.arange(ROWS, dtype=jnp.int32) >= offsets[0]).astype(F32)
@@ -333,48 +330,52 @@
     log_decay = -head_rate * step_size
     running = jnp.cumsum(log_decay, axis=0)
     weight = jnp.exp(running[-1:] - running) * step_size
+    early, weight, states, running = together(early, weight, states, running)
+    own = run("b", early, STATE_WIDTH + CHUNKS["b"][0])
+    projected["b"][0] = own
     def columns(array, name):
         return array[CHUNKS[name][0] : sum(CHUNKS[name])]
 
-    def first_steps(own):
-        sent = own.astype(BF16)
-        return behind(sent, 1), lax.ppermute(sent, "z", [(0, 3)])
-
-    def relayed(one):
-        return lax.ppermute(one, "z", [(1, 2), (2, 3)])
+    def first_step(own, *more):
+        return lax.ppermute(jnp.concatenate([own.astype(BF16), *more]), "z", [(0, 1), (1, 0), (2, 3)])
+
+    def second_step(own, came, name):
+        mine, its = columns(jnp.where(z == 0, remote, 1.0), name), columns(jnp.where(z == 0, 1.0, factor), name)
+        return lax.ppermute((mine * own + its * came.astype(F32)).astype(BF16), "z", [(1, 2), (0, 3)])
 
     def from_start(name):
         start = jnp.where(z == 0, columns(factor, name) * columns(initial, name).astype(F32), 0.0)
         return head(name) + start
 
-    def all_before(own, name, one, two, three):
-        return own + sum(columns(f, name) * came.astype(F32) for f, came in zip(factors, (one, two, three)))
+    def all_before(own, name, one, two):
+        for_one, for_two = jnp.where(z == 0, 0.0, factor), jnp.where(z == 3, factor * remote, factor)
+        return own + columns(for_one, name) * one.astype(F32) + columns(for_two, name) * two.astype(F32)
 
     projected["a"], projected["b"][0] = together(projected["a"], projected["b"][0])
     decay = jnp.exp(running[-1])
     factor = jnp.repeat(decay, P_SIZE)[:, None]
     a = from_start("a")
-    a, b_input = together(a, projected["b"])
-    projected["b"] = b_input
-    one_a, three_a = first_steps(a)
+    high = decay.astype(BF16)
+    terms = jnp.concatenate([high, (decay - high.astype(F32)).astype(BF16), jnp.zeros(N - 2 * GROUP_HEADS, BF16)])
+    one_a = first_step(a, jnp.broadcast_to(terms, (16, N)))
+    late, one_a, decay = together(late, one_a, decay)
+    own = run("c", late, 0)
+    projected["c"][0], projected["b"], one_a = together(own, projected["b"], one_a)
+    width = CHUNKS["a"][1]
+    remote = one_a[width, :GROUP_HEADS].astype(F32) + one_a[width, GROUP_HEADS : 2 * GROUP_HEADS].astype(F32)
+    remote = jnp.repeat(remote, P_SIZE)[:, None]
+    one_a = one_a[:width]
+    two_a = second_step(a, one_a, "a")
     b = from_start("b")
-    late, b, decay = together(late, b, decay)
-    own = run("c", late, 0)
-    projected["c"][0], one_a, three_a, b, decay = together(own, one_a, three_a, b, decay)
-    two_a = relayed(one_a)
-    one_b, three_b = first_steps(b)
-    decays = lax.all_gather(decay, "z")
-    two = decay * lax.dynamic_index_in_dim(decays, (z + 3) % 4, 0, False)
-    three = two * lax.dynamic_index_in_dim(decays, (z + 2) % 4, 0, False)
-    factors = jnp.repeat(jnp.stack([decay, two, three]), P_SIZE, axis=1)[:, :, None]
-    projected["c"][1], two_a, one_b, three_b, factors = together(projected["c"][1], two_a, one_b, three_b, factors)
-    two_b = relayed(one_b)
+    one_b = first_step(b)
+    projected["c"][1], two_a, one_b = together(projected["c"][1], two_a, one_b)
+    two_b = second_step(b, one_b, "b")
     c = from_start("c")
-    one_c, three_c = first_steps(c)
-    two_c = relayed(one_c)
-    a = all_before(a, "a", one_a, two_a, three_a)
-    b = all_before(b, "b", one_b, two_b, three_b)
-    c = all_before(c, "c", one_c, two_c, three_c)
+    one_c = first_step(c)
+    two_c = second_step(c, one_c, "c")
+    a = all_before(a, "a", one_a, two_a)
+    b = all_before(b, "b", one_b, two_b)
+    c = all_before(c, "c", one_c, two_c)
     return jnp.concatenate([a, b, c], axis=0)[None, None]
 
 

time: 271 us -> 267 us (0.985)
  waiting for transfers between devices: 86.7 us -> 102 us
  blocking collectives: 12.2 us -> 0 us
  starting transfers between devices: 57.5 us -> 48.8 us
    ppermute x9 -> x6, waiting for transfers between devices: 7.09 us -> 22.7 us  [the longest x3 16.5 us: second_step(): lax.ppermute((mine * own + its * came.astype(F32)).astype(BF16), 'z', [(1...]
    unnamed x1 -> x0, blocking collectives: 12.2 us -> none
    ppermute x9 -> x6, starting transfers between devices: 21.4 us -> 11.5 us  [the longest x3 7.52 us: first_step(): lax.ppermute(jnp.concatenate([own.astype(BF16), *more]), 'z', [(0, 1), (1...]
    convert_element_type x3 -> x6, other arithmetic: 1.26 us -> 4.6 us  [the longest x3 3.94 us: first_step(): own.astype(BF16)]
  transfers between devices with their start and end apart: 30 -> 27, of which waited for: 12 -> 13; matrix products, arithmetic and copies ran while one was open for 6% -> 7% of each run, Pallas kernels for 25% -> 25%
where the time goes in v3:
time: 267 us; the launch traced here: 265 us
  waiting for transfers between devices  102 us (38%)
  Pallas kernels  70.6 us (26%)
  starting transfers between devices  48.8 us (18%)
  between operations  15.7 us (6%)
  other arithmetic  14.7 us (6%)
  local copies, waits for them, and re-layouts  13.3 us (5%)
    pallas_call x4, Pallas kernels, project(): pl.pallas_call(kernel, out_shape=(jax.ShapeDtypeStruct((LONG, width), F32...  40.5 us
    ppermute x9, waiting for transfers between devices, swap(): return lax.ppermute(value, axis, [(0, 1), (1, 0)])  30.3 us
    all_gather x1, waiting for transfers between devices, per_device(): early = lax.all_gather(s, ('x', 'z'), axis=0, tiled=True)  28.3 us
    ppermute x9, starting transfers between devices, swap(): return lax.ppermute(value, axis, [(0, 1), (1, 0)])  19.9 us
    pallas_call x4, Pallas kernels, call(): pl.pallas_call(kernel, out_shape=out, in_specs=[SMEM] + [VMEM] * (len(arg...  16.5 us
    ppermute x3, waiting for transfers between devices, second_step(): lax.ppermute((mine * own + its * came.astype(F32)).astype(BF16), 'z', [(1...  16.5 us
    ppermute x1, waiting for transfers between devices, halos(): lax.ppermute(lax.dynamic_index_in_dim(last, 1 - yh, 0, False), ('yh', 'z'...  9.77 us
    pallas_call x2, Pallas kernels, in_blocks(): pl.pallas_call(kernel, out_shape=jax.ShapeDtypeStruct((16, LONG, PIECE),...  8.87 us
  transfers between devices with their start and end apart: 27, of which 13 were waited for; matrix products, arithmetic and copies ran while one was open for 7% of the time, Pallas kernels for 25%

profile of v3, /device:TPU:64, one launch (start us, length us, event | category | flops | bytes accessed | tf_op | source)
XLA Modules:
  0.0 265.5 jit_solution(17988030857450212622)
XLA Ops:
  9.7 2.0 cut.3
  11.7 3.3 %collective-permute-start = (bf16[512,768]{1,0:T(8,128)(2,1)}, bf16[512,768]{1,0:T(8,128)(2,1)S(1)}, u32[]{:S(2)}, u32[]{:S(2)}) collective-permute-start(bf16[512,768]{1,0:T(8,128)(2,1)} %cut.3), channel_id=1, source_target_pairs={{0,64},{64,0},{1,65},{65,1},{2,66},{66,2},{3,67},{67,3},{4,68},{68... | collective-permute-start | bytes 2359304 | tf_op jit(solution)/shard_map/ppermute | solution.py:244
  16.8 3.5 %collective-permute-start.1 = (bf16[16,16,256]{2,1,0:T(8,128)(2,1)}, bf16[16,16,256]{2,1,0:T(8,128)(2,1)}, u32[]{:S(2)}, u32[]{:S(2)}) collective-permute-start(bf16[16,16,256]{2,1,0:T(8,128)(2,1)} %bitcast.65), channel_id=1, source_target_pairs={{0,4},{4,8},{8,12},{1,5},{5,9},{9,13},{2,6},{6,10},{10,14},{3,7},{... | collective-permute-start | bytes 393224 | tf_op jit(solution)/shard_map/ppermute | solution.py:250
  21.0 1.9 collective-permute-start.2
  22.9 2.7 %cut.2 = bf16[512,1280]{1,0:T(8,128)(2,1)} custom-call(s32[1]{0:T(128)} %bitcast.2.first_ref, bf16[512,8192]{1,0:T(8,128)(2,1)} %bitcast.75), custom_call_target="tpu_custom_call" | custom-call | bytes 2621440 | tf_op jit(solution)/shard_map/cut/pallas_call | solution.py:80
  25.6 9.8 %collective-permute-done.2.halo_ref = bf16[16,16,256]{2,1,0:T(8,128)(2,1)} collective-permute-done((bf16[16,16,256]{2,1,0:T(8,128)(2,1)}, bf16[16,16,256]{2,1,0:T(8,128)(2,1)}, u32[]{:S(2)}, u32[]{:S(2)}) %collective-permute-start.2) | collective-permute-done | bytes 131104 | tf_op jit(solution)/shard_map/ppermute | solution.py:252
  35.4 3.2 %collective-permute-start.3 = (bf16[512,1280]{1,0:T(8,128)(2,1)}, bf16[512,1280]{1,0:T(8,128)(2,1)}, u32[]{:S(2)}, u32[]{:S(2)}) collective-permute-start(bf16[512,1280]{1,0:T(8,128)(2,1)} %cut.2), channel_id=1, source_target_pairs={{0,64},{64,0},{1,65},{65,1},{2,66},{66,2},{3,67},{67,3},{4,68},{68... | collective-permute-start | bytes 3932168 | tf_op jit(solution)/shard_map/ppermute | solution.py:244
  39.5 4.4 %own_tokens.1.refs_0_ = bf16[16,528,256]{2,1,0:T(8,128)(2,1)} custom-call(s32[1]{0:T(128)} %bitcast.9.at_ref, bf16[16,16,256]{2,1,0:T(8,128)(2,1)} %collective-permute-done.1.halo_ref, bf16[512,8192]{1,0:T(8,128)(2,1)} %bitcast.76), custom_call_target="tpu_custom_call" | custom-call | bytes 8650752 | tf_op jit(solution)/shard_map/own_tokens/pallas_call | solution.py:108
  44.0 22.8 %collective-permute-done.3.refs_1_ = bf16[512,1280]{1,0:T(8,128)(2,1)} collective-permute-done((bf16[512,1280]{1,0:T(8,128)(2,1)}, bf16[512,1280]{1,0:T(8,128)(2,1)}, u32[]{:S(2)}, u32[]{:S(2)}) %collective-permute-start.3) | collective-permute-done | bytes 1310752 | tf_op jit(solution)/shard_map/ppermute | solution.py:244
  66.7 3.2 %collective-permute-start.6 = (bf16[2,512,256]{2,1,0:T(8,128)(2,1)S(1)}, bf16[2,512,256]{2,1,0:T(8,128)(2,1)S(1)}, u32[]{:S(2)}, u32[]{:S(2)}) collective-permute-start(bf16[2,512,256]{2,1,0:T(8,128)(2,1)S(1)} %constant_dynamic-slice_fusion), channel_id=1, source_target_pairs={{0,64},{64,0},{1,65},{65,1},{2,66},{66,2},{3,67},{67,3},{4,68},{68... | collective-permute-start | bytes 1572872 | tf_op jit(solution)/shard_map/ppermute | solution.py:244
  73.6 4.5 %partner_tokens.1.refs_1_ = bf16[16,528,256]{2,1,0:T(8,128)(2,1)} custom-call(s32[1]{0:T(128)} %bitcast.1.at_ref, bf16[16,16,256]{2,1,0:T(8,128)(2,1)} %collective-permute-done.2.halo_ref, bf16[512,768]{1,0:T(8,128)(2,1)} %copy-done.11, bf16[512,1280]{1,0:T(8,128)(2,1)} %collective-permute-done.3.refs_1_, bf16[512,768]{1,0:T(8,128)(2,1)} %collective-permute-done.4.refs_2_, ...), custom_call_target="tpu_custom_call" | custom-call | bytes 8650752 | tf_op jit(solution)/shard_map/partner_tokens/pallas_call | solution.py:108
  78.1 4.5 %collective-permute-done.6 = bf16[2,512,256]{2,1,0:T(8,128)(2,1)S(1)} collective-permute-done((bf16[2,512,256]{2,1,0:T(8,128)(2,1)S(1)}, bf16[2,512,256]{2,1,0:T(8,128)(2,1)S(1)}, u32[]{:S(2)}, u32[]{:S(2)}) %collective-permute-start.6) | collective-permute-done | bytes 524320 | tf_op jit(solution)/shard_map/ppermute | solution.py:244
  82.6 2.8 %collective-permute-start.7 = (s32[2]{0:T(128)S(1)}, s32[2]{0:T(128)S(1)}, u32[]{:S(2)}, u32[]{:S(2)}) collective-permute-start(s32[2]{0:T(128)S(1)} %pad_add_fusion.1), channel_id=1, source_target_pairs={{0,48},{16,0},{32,16},{48,32},{1,49},{17,1},{33,17},{49,33},{2,50}... | collective-permute-start | bytes 32 | tf_op jit(solution)/shard_map/ppermute | solution.py:40
  87.0 3.4 %collective-permute-done.8 = s32[2]{0:T(128)S(1)} collective-permute-done((s32[2]{0:T(128)S(1)}, s32[2]{0:T(128)S(1)}, u32[]{:S(2)}, u32[]{:S(2)}) %collective-permute-start.8) | collective-permute-done | bytes 40 | tf_op jit(solution)/shard_map/ppermute | solution.py:40
  90.9 28.3 %all-gather.3.cloned.1.call-done.refs_2_.refs_3_.refs_4_.refs_5_ = bf16[4096,1920]{1,0:T(8,128)(2,1)} async-done(((bf16[256,1920]{1,0:T(8,128)(2,1)}), bf16[4096,1920]{1,0:T(8,128)(2,1)}) %all-gather.3.cloned.1.call-update) | async-done | bytes 15728656 | tf_op jit(solution)/shard_map/all_gather | solution.py:286
  120.1 8.9 %project.4 = (f32[528,384]{1,0:T(8,128)}, bf16[528,384]{1,0:T(8,128)(2,1)}) custom-call(s32[16]{0:T(128)} %iota.14.places_ref, bf16[16,528,256]{2,1,0:T(8,128)(2,1)} %own_tokens.1.refs_0_, bf16[16,528,256]{2,1,0:T(8,128)(2,1)} %partner_tokens.1.refs_1_, bf16[4096,1920]{1,0:T(8,128)(2,1)} %all-gather.3.cloned.1.call-done.refs_2_.refs_3_.refs_4_.refs_5_, ...), custom_call_target="tpu_custom_call" | custom-call | flops 3321888768 | bytes 11845728 | tf_op jit(solution)/shard_map/project/pallas_call | solution.py:181
  129.4 2.5 collective-permute-start.12
  131.9 1.5 collective-permute-start.13
  133.4 3.0 %collective-permute-start.10 = (bf16[528,384]{1,0:T(8,128)(2,1)}, bf16[528,384]{1,0:T(8,128)(2,1)S(1)}, u32[]{:S(2)}, u32[]{:S(2)}) collective-permute-start(bf16[528,384]{1,0:T(8,128)(2,1)} %get-tuple-element.69), channel_id=1, source_target_pairs={{0,64},{64,0},{1,65},{65,1},{2,66},{66,2},{3,67},{67,3},{4,68},{68... | collective-permute-start | bytes 1216520 | tf_op jit(solution)/shard_map/ppermute | solution.py:244
  136.9 11.4 %project.5 = (f32[528,768]{1,0:T(8,128)}, bf16[528,768]{1,0:T(8,128)(2,1)}) custom-call(s32[16]{0:T(128)} %iota.15.places_ref, bf16[16,528,256]{2,1,0:T(8,128)(2,1)} %own_tokens.1.refs_0_, bf16[16,528,256]{2,1,0:T(8,128)(2,1)} %partner_tokens.1.refs_1_, bf16[4096,1920]{1,0:T(8,128)(2,1)} %all-gather.3.cloned.1.call-done.refs_2_.refs_3_.refs_4_.refs_5_, ...), custom_call_target="tpu_custom_call" | custom-call | flops 6643777536 | bytes 14991456 | tf_op jit(solution)/shard_map/project/pallas_call | solution.py:181
  149.0 1.3 collective-permute-start.15
  150.3 2.8 %activate.4 = (bf16[512,256]{1,0:T(8,128)(2,1)}, f32[512,32]{1,0:T(8,128)}) custom-call(s32[2]{0:T(128)} %pad_add_fusion.info_ref.refs_0_, f32[528,384]{1,0:T(8,128)} %get-tuple-element.80.own_ref, bf16[528,384]{1,0:T(8,128)(2,1)} %copy-done.12, f32[4,2304]{1,0:T(4,128)} %refs_3_.5, f32[1,2304]{1,0:T(1,128)} %broadcast_in_dim.74.bias_ref.refs_4_), custom_call_target="tpu_custom_call" | custom-call | flops 33554432 | bytes 270336 | tf_op jit(solution)/shard_map/activate/pallas_call | solution.py:231
  154.3 1.2 reduce-window.6
  155.9 1.8 exponential_multiply_fusion.refs_5_
  158.3 1.9 collective-permute-start.16
  160.8 11.4 %project.6 = (f32[528,768]{1,0:T(8,128)}, bf16[528,768]{1,0:T(8,128)(2,1)}) custom-call(s32[16]{0:T(128)} %iota.16.places_ref, bf16[16,528,256]{2,1,0:T(8,128)(2,1)} %own_tokens.1.refs_0_, bf16[16,528,256]{2,1,0:T(8,128)(2,1)} %partner_tokens.1.refs_1_, bf16[4096,1920]{1,0:T(8,128)(2,1)} %all-gather.3.cloned.1.call-done.refs_2_.refs_3_.refs_4_.refs_5_, ...), custom_call_target="tpu_custom_call" | custom-call | flops 6643777536 | bytes 14991456 | tf_op jit(solution)/shard_map/project/pallas_call | solution.py:181
  173.1 5.0 %activate.5 = f32[768,256]{1,0:T(8,128)} custom-call(s32[2]{0:T(128)} %pad_add_fusion.info_ref.refs_0_, f32[528,768]{1,0:T(8,128)} %get-tuple-element.86.refs_1_, bf16[528,768]{1,0:T(8,128)(2,1)} %copy-done.9, f32[4,2304]{1,0:T(4,128)} %refs_3_.5, f32[1,2304]{1,0:T(1,128)} %broadcast_in_dim.74.bias_ref.refs_4_, f32[512,32]{1,0:T(8,128)} %exponential_multiply_fusion.refs_5_, ...), custom_call_target="tpu_custom_call" | custom-call | flops 100663296 | bytes 811008 | tf_op jit(solution)/shard_map/activate/pallas_call | solution.py:231
  178.1 7.4 %collective-permute-done.16 = bf16[1024,256]{1,0:T(8,128)(2,1)S(1)} collective-permute-done((bf16[1024,256]{1,0:T(8,128)(2,1)S(1)}, bf16[1024,256]{1,0:T(8,128)(2,1)S(1)}, u32[]{:S(2)}, u32[]{:S(2)}) %collective-permute-start.16) | collective-permute-done | bytes 524320 | tf_op jit(solution)/shard_map/ppermute | solution.py:275
  186.7 2.9 %collective-permute-start.17 = (bf16[784,256]{1,0:T(8,128)(2,1)}, bf16[784,256]{1,0:T(8,128)(2,1)S(1)}, u32[]{:S(2)}, u32[]{:S(2)}) collective-permute-start(bf16[784,256]{1,0:T(8,128)(2,1)} %pad_maximum_fusion), channel_id=1, source_target_pairs={{0,4},{4,0},{8,12},{1,5},{5,1},{9,13},{2,6},{6,2},{10,14},{3,7},{7... | collective-permute-start | bytes 1204232 | tf_op jit(solution)/shard_map/ppermute | solution.py:340
  189.6 3.1 %collective-permute-start.18 = (bf16[528,768]{1,0:T(8,128)(2,1)}, bf16[528,768]{1,0:T(8,128)(2,1)S(1)}, u32[]{:S(2)}, u32[]{:S(2)}) collective-permute-start(bf16[528,768]{1,0:T(8,128)(2,1)} %get-tuple-element.95), channel_id=1, source_target_pairs={{0,64},{64,0},{1,65},{65,1},{2,66},{66,2},{3,67},{67,3},{4,68},{68... | collective-permute-start | bytes 2433032 | tf_op jit(solution)/shard_map/ppermute | solution.py:244
  193.1 4.1 %collective-permute-done.17 = bf16[784,256]{1,0:T(8,128)(2,1)S(1)} collective-permute-done((bf16[784,256]{1,0:T(8,128)(2,1)}, bf16[784,256]{1,0:T(8,128)(2,1)S(1)}, u32[]{:S(2)}, u32[]{:S(2)}) %collective-permute-start.17) | collective-permute-done | bytes 401440 | tf_op jit(solution)/shard_map/ppermute | solution.py:340
  197.8 8.8 %project.7 = (f32[528,512]{1,0:T(8,128)}, bf16[528,512]{1,0:T(8,128)(2,1)}) custom-call(s32[16]{0:T(128)} %iota.18.places_ref, bf16[16,528,256]{2,1,0:T(8,128)(2,1)} %own_tokens.1.refs_0_, bf16[16,528,256]{2,1,0:T(8,128)(2,1)} %partner_tokens.1.refs_1_, bf16[4096,512]{1,0:T(8,128)(2,1)} %all-gather.5.cloned.1.call-done.refs_2_.refs_3_.refs_4_.refs_5_, ...), custom_call_target="tpu_custom_call" | custom-call | flops 4429185024 | bytes 12894304 | tf_op jit(solution)/shard_map/project/pallas_call | solution.py:181
  206.6 3.0 %collective-permute-done.18.refs_2_ = bf16[528,768]{1,0:T(8,128)(2,1)S(1)} collective-permute-done((bf16[528,768]{1,0:T(8,128)(2,1)}, bf16[528,768]{1,0:T(8,128)(2,1)S(1)}, u32[]{:S(2)}, u32[]{:S(2)}) %collective-permute-start.18) | collective-permute-done | bytes 811040 | tf_op jit(solution)/shard_map/ppermute | solution.py:244
  209.9 3.4 %collective-permute-start.19 = (bf16[528,512]{1,0:T(8,128)(2,1)}, bf16[528,512]{1,0:T(8,128)(2,1)}, u32[]{:S(2)}, u32[]{:S(2)}) collective-permute-start(bf16[528,512]{1,0:T(8,128)(2,1)} %get-tuple-element.98), channel_id=1, source_target_pairs={{0,64},{64,0},{1,65},{65,1},{2,66},{66,2},{3,67},{67,3},{4,68},{68... | collective-permute-start | bytes 1622024 | tf_op jit(solution)/shard_map/ppermute | solution.py:244
  213.4 4.9 %activate.6 = f32[768,256]{1,0:T(8,128)} custom-call(s32[2]{0:T(128)} %pad_add_fusion.info_ref.refs_0_, f32[528,768]{1,0:T(8,128)} %get-tuple-element.99.refs_1_, bf16[528,768]{1,0:T(8,128)(2,1)} %copy-done.10, f32[4,2304]{1,0:T(4,128)} %refs_3_.5, f32[1,2304]{1,0:T(1,128)} %broadcast_in_dim.74.bias_ref.refs_4_, f32[512,32]{1,0:T(8,128)} %exponential_multiply_fusion.refs_5_, ...), custom_call_target="tpu_custom_call" | custom-call | flops 100663296 | bytes 811008 | tf_op jit(solution)/shard_map/activate/pallas_call | solution.py:231
  218.3 2.5 fusion.19
  220.8 1.4 collective-permute-start.20
  222.2 1.6 collective-permute-start.21
  224.0 7.3 %collective-permute-done.20 = bf16[768,256]{1,0:T(8,128)(2,1)} collective-permute-done((bf16[768,256]{1,0:T(8,128)(2,1)}, bf16[768,256]{1,0:T(8,128)(2,1)}, u32[]{:S(2)}, u32[]{:S(2)}) %collective-permute-start.20) | collective-permute-done | bytes 393248 | tf_op jit(solution)/shard_map/ppermute | solution.py:344
  231.3 3.9 %activate.7 = f32[512,256]{1,0:T(8,128)} custom-call(s32[2]{0:T(128)} %pad_add_fusion.info_ref.refs_0_, f32[528,512]{1,0:T(8,128)} %get-tuple-element.103.refs_1_, bf16[528,512]{1,0:T(8,128)(2,1)} %collective-permute-done.19.refs_2_, f32[4,2304]{1,0:T(4,128)} %refs_3_.5, f32[1,2304]{1,0:T(1,128)} %broadcast_in_dim.74.bias_ref.refs_4_, ...), custom_call_target="tpu_custom_call" | custom-call | flops 67108864 | bytes 540672 | tf_op jit(solution)/shard_map/activate/pallas_call | solution.py:231
  235.2 1.3 fusion.17
  236.4 3.1 %collective-permute-start.23 = (bf16[512,256]{1,0:T(8,128)(2,1)S(1)}, bf16[512,256]{1,0:T(8,128)(2,1)S(1)}, u32[]{:S(2)}, u32[]{:S(2)}) collective-permute-start(bf16[512,256]{1,0:T(8,128)(2,1)S(1)} %fusion.17), channel_id=1, source_target_pairs={{0,4},{4,0},{8,12},{1,5},{5,1},{9,13},{2,6},{6,2},{10,14},{3,7},{7... | collective-permute-start | bytes 786440 | tf_op jit(solution)/shard_map/ppermute | solution.py:340
  239.9 1.3 collective-permute-start.22
  241.3 2.1 collective-permute-done.23
  243.6 1.3 collective-permute-start.24
  244.9 8.3 %collective-permute-done.22 = bf16[768,256]{1,0:T(8,128)(2,1)S(1)} collective-permute-done((bf16[768,256]{1,0:T(8,128)(2,1)S(1)}, bf16[768,256]{1,0:T(8,128)(2,1)S(1)}, u32[]{:S(2)}, u32[]{:S(2)}) %collective-permute-start.22) | collective-permute-done | bytes 393248 | tf_op jit(solution)/shard_map/ppermute | solution.py:344
  253.2 1.8 fusion.1
  256.3 1.5 maximum_bitcast_fusion
  (123 shorter events, 22.3 us)
Async XLA Ops:
  6.5 32.9 %copy-start = (bf16[2,2048,256]{2,1,0:T(8,128)(2,1)S(1)}, bf16[2,2048,256]{2,1,0:T(8,128)(2,1)}, u32[]{:S(2)}) copy-start(bf16[2,2048,256]{2,1,0:T(8,128)(2,1)} %param.17) | copy-start | bytes 6291460
  6.5 1.9 slice-start
  6.5 112.6 %all-gather.3.cloned.1.call-start = ((), (), s32[]{:S(2)}) async-start(), calls=%async_computation | async-start | bytes 16711680 | tf_op jit(solution)/shard_map/all_gather | solution.py:286
  9.6 183.4 %all-gather.5.cloned.1.call-start = ((), (), s32[]{:S(2)}) async-start(), calls=%async_computation.1 | async-start | bytes 4456448 | tf_op jit(solution)/shard_map/all_gather | solution.py:287
  11.7 23.6 %collective-permute-start = (bf16[512,768]{1,0:T(8,128)(2,1)}, bf16[512,768]{1,0:T(8,128)(2,1)S(1)}, u32[]{:S(2)}, u32[]{:S(2)}) collective-permute-start(bf16[512,768]{1,0:T(8,128)(2,1)} %cut.3), channel_id=1, source_target_pairs={{0,64},{64,0},{1,65},{65,1},{2,66},{66,2},{3,67},{67,3},{4,68},{68... | collective-permute-start | bytes 2359304 | tf_op jit(solution)/shard_map/ppermute | solution.py:244
  16.8 8.8 %collective-permute-start.1 = (bf16[16,16,256]{2,1,0:T(8,128)(2,1)}, bf16[16,16,256]{2,1,0:T(8,128)(2,1)}, u32[]{:S(2)}, u32[]{:S(2)}) collective-permute-start(bf16[16,16,256]{2,1,0:T(8,128)(2,1)} %bitcast.65), channel_id=1, source_target_pairs={{0,4},{4,8},{8,12},{1,5},{5,9},{9,13},{2,6},{6,10},{10,14},{3,7},{... | collective-permute-start | bytes 393224 | tf_op jit(solution)/shard_map/ppermute | solution.py:250
  21.0 14.4 %collective-permute-start.2 = (bf16[16,16,256]{2,1,0:T(8,128)(2,1)}, bf16[16,16,256]{2,1,0:T(8,128)(2,1)}, u32[]{:S(2)}, u32[]{:S(2)}) collective-permute-start(bf16[16,16,256]{2,1,0:T(8,128)(2,1)} %bitcast.64), channel_id=1, source_target_pairs={{0,68},{4,72},{8,76},{64,4},{68,8},{72,12},{1,69},{5,73},{9,77},{6... | collective-permute-start | bytes 393224 | tf_op jit(solution)/shard_map/ppermute | solution.py:252
  22.9 15.7 %copy-start.5 = (bf16[256,2304]{1,0:T(8,128)(2,1)S(1)}, bf16[256,2304]{1,0:T(8,128)(2,1)}, u32[]{:S(2)}) copy-start(bf16[256,2304]{1,0:T(8,128)(2,1)} %param.11) | copy-start | bytes 3538948
  35.4 8.6 %copy-start.11 = (bf16[512,768]{1,0:T(8,128)(2,1)}, bf16[512,768]{1,0:T(8,128)(2,1)S(1)}, u32[]{:S(2)}) copy-start(bf16[512,768]{1,0:T(8,128)(2,1)S(1)} %collective-permute-done.refs_0_) | copy-start | bytes 2359300
  35.4 31.4 %collective-permute-start.3 = (bf16[512,1280]{1,0:T(8,128)(2,1)}, bf16[512,1280]{1,0:T(8,128)(2,1)}, u32[]{:S(2)}, u32[]{:S(2)}) collective-permute-start(bf16[512,1280]{1,0:T(8,128)(2,1)} %cut.2), channel_id=1, source_target_pairs={{0,64},{64,0},{1,65},{65,1},{2,66},{66,2},{3,67},{67,3},{4,68},{68... | collective-permute-start | bytes 3932168 | tf_op jit(solution)/shard_map/ppermute | solution.py:244
  39.3 4.6 %collective-permute-start.4 = (bf16[512,768]{1,0:T(8,128)(2,1)S(1)}, bf16[512,768]{1,0:T(8,128)(2,1)}, u32[]{:S(2)}, u32[]{:S(2)}) collective-permute-start(bf16[512,768]{1,0:T(8,128)(2,1)S(1)} %collective-permute-done.refs_0_), channel_id=1, source_target_pairs={{0,1},{1,0},{2,3},{3,2},{4,5},{5,4},{6,7},{7,6},{8,9},{9,8},{10,11... | collective-permute-start | bytes 2359304 | tf_op jit(solution)/shard_map/ppermute | solution.py:244
  39.5 31.8 %copy-start.13 = (f32[2304]{0:T(1024)S(1)}, f32[2304]{0:T(1024)}, u32[]{:S(2)}) copy-start(f32[2304]{0:T(1024)} %param.14) | copy-start | bytes 27652
  39.5 32.4 %copy-start.15 = (f32[32]{0:T(128)S(1)}, f32[32]{0:T(128)}, u32[]{:S(2)}) copy-start(f32[32]{0:T(128)} %param.16) | copy-start | bytes 388
  66.7 5.8 %collective-permute-start.5 = (bf16[512,1280]{1,0:T(8,128)(2,1)}, bf16[512,1280]{1,0:T(8,128)(2,1)S(1)}, u32[]{:S(2)}, u32[]{:S(2)}) collective-permute-start(bf16[512,1280]{1,0:T(8,128)(2,1)} %collective-permute-done.3.refs_1_), channel_id=1, source_target_pairs={{0,1},{1,0},{2,3},{3,2},{4,5},{5,4},{6,7},{7,6},{8,9},{9,8},{10,11... | collective-permute-start | bytes 3932168 | tf_op jit(solution)/shard_map/ppermute | solution.py:244
  66.7 15.8 %collective-permute-start.6 = (bf16[2,512,256]{2,1,0:T(8,128)(2,1)S(1)}, bf16[2,512,256]{2,1,0:T(8,128)(2,1)S(1)}, u32[]{:S(2)}, u32[]{:S(2)}) collective-permute-start(bf16[2,512,256]{2,1,0:T(8,128)(2,1)S(1)} %constant_dynamic-slice_fusion), channel_id=1, source_target_pairs={{0,64},{64,0},{1,65},{65,1},{2,66},{66,2},{3,67},{67,3},{4,68},{68... | collective-permute-start | bytes 1572872 | tf_op jit(solution)/shard_map/ppermute | solution.py:244
  72.6 1.1 copy-start.8
  82.6 4.4 %collective-permute-start.7 = (s32[2]{0:T(128)S(1)}, s32[2]{0:T(128)S(1)}, u32[]{:S(2)}, u32[]{:S(2)}) collective-permute-start(s32[2]{0:T(128)S(1)} %pad_add_fusion.1), channel_id=1, source_target_pairs={{0,48},{16,0},{32,16},{48,32},{1,49},{17,1},{33,17},{49,33},{2,50}... | collective-permute-start | bytes 32 | tf_op jit(solution)/shard_map/ppermute | solution.py:40
  85.3 5.0 %collective-permute-start.8 = (s32[2]{0:T(128)S(1)}, s32[2]{0:T(128)S(1)}, u32[]{:S(2)}, u32[]{:S(2)}) collective-permute-start(s32[2]{0:T(128)S(1)} %pad_add_fusion.1), channel_id=1, source_target_pairs={{0,32},{16,48},{32,0},{48,16},{1,33},{17,49},{33,1},{49,17},{2,34}... | collective-permute-start | bytes 32 | tf_op jit(solution)/shard_map/ppermute | solution.py:40
  86.1 4.8 %collective-permute-start.9 = (s32[2]{0:T(128)S(1)}, s32[2]{0:T(128)S(1)}, u32[]{:S(2)}, u32[]{:S(2)}) collective-permute-start(s32[2]{0:T(128)S(1)} %pad_add_fusion.1), channel_id=1, source_target_pairs={{0,16},{16,32},{32,48},{48,0},{1,17},{17,33},{33,49},{49,1},{2,18}... | collective-permute-start | bytes 32 | tf_op jit(solution)/shard_map/ppermute | solution.py:40
  129.0 19.9 %collective-permute-start.11 = (bf16[512,256]{1,0:T(8,128)(2,1)S(1)}, bf16[512,256]{1,0:T(8,128)(2,1)S(1)}, u32[]{:S(2)}, u32[]{:S(2)}) collective-permute-start(bf16[512,256]{1,0:T(8,128)(2,1)S(1)} %get-tuple-element.117), channel_id=1, source_target_pairs={{0,16},{16,32},{32,48},{48,0},{1,17},{17,33},{33,49},{49,1},{2,18}... | collective-permute-start | bytes 786440 | tf_op jit(solution)/shard_map/ppermute | solution.py:40
  129.4 19.6 %collective-permute-start.12 = (bf16[512,256]{1,0:T(8,128)(2,1)S(1)}, bf16[512,256]{1,0:T(8,128)(2,1)S(1)}, u32[]{:S(2)}, u32[]{:S(2)}) collective-permute-start(bf16[512,256]{1,0:T(8,128)(2,1)S(1)} %get-tuple-element.118), channel_id=1, source_target_pairs={{0,32},{16,48},{32,0},{48,16},{1,33},{17,49},{33,1},{49,17},{2,34}... | collective-permute-start | bytes 786440 | tf_op jit(solution)/shard_map/ppermute | solution.py:40
  131.9 17.1 %collective-permute-start.13 = (bf16[512,256]{1,0:T(8,128)(2,1)S(1)}, bf16[512,256]{1,0:T(8,128)(2,1)S(1)}, u32[]{:S(2)}, u32[]{:S(2)}) collective-permute-start(bf16[512,256]{1,0:T(8,128)(2,1)S(1)} %select_bitcast_fusion), channel_id=1, source_target_pairs={{0,48},{16,0},{32,16},{48,32},{1,49},{17,1},{33,17},{49,33},{2,50}... | collective-permute-start | bytes 786440 | tf_op jit(solution)/shard_map/ppermute | solution.py:40
  133.4 15.6 %collective-permute-start.10 = (bf16[528,384]{1,0:T(8,128)(2,1)}, bf16[528,384]{1,0:T(8,128)(2,1)S(1)}, u32[]{:S(2)}, u32[]{:S(2)}) collective-permute-start(bf16[528,384]{1,0:T(8,128)(2,1)} %get-tuple-element.69), channel_id=1, source_target_pairs={{0,64},{64,0},{1,65},{65,1},{2,66},{66,2},{3,67},{67,3},{4,68},{68... | collective-permute-start | bytes 1216520 | tf_op jit(solution)/shard_map/ppermute | solution.py:244
  148.3 4.8 %copy-start.14 = (f32[32]{0:T(128)S(1)}, f32[32]{0:T(128)}, u32[]{:S(2)}) copy-start(f32[32]{0:T(128)} %param.15) | copy-start | bytes 388
  148.3 23.9 %collective-permute-start.14 = (bf16[528,768]{1,0:T(8,128)(2,1)}, bf16[528,768]{1,0:T(8,128)(2,1)S(1)}, u32[]{:S(2)}, u32[]{:S(2)}) collective-permute-start(bf16[528,768]{1,0:T(8,128)(2,1)} %get-tuple-element.78), channel_id=1, source_target_pairs={{0,64},{64,0},{1,65},{65,1},{2,66},{66,2},{3,67},{67,3},{4,68},{68... | collective-permute-start | bytes 2433032 | tf_op jit(solution)/shard_map/ppermute | solution.py:244
  149.0 1.3 copy-start.12
  149.0 9.1 %collective-permute-start.15 = (bf16[512,256]{1,0:T(8,128)(2,1)S(1)}, bf16[512,256]{1,0:T(8,128)(2,1)S(1)}, u32[]{:S(2)}, u32[]{:S(2)}) collective-permute-start(bf16[512,256]{1,0:T(8,128)(2,1)S(1)} %fusion.14), channel_id=1, source_target_pairs={{0,4},{4,0},{8,12},{12,8},{1,5},{5,1},{9,13},{13,9},{2,6},{6,2},{1... | collective-permute-start | bytes 786440 | tf_op jit(solution)/shard_map/ppermute | solution.py:273
  158.3 27.1 %collective-permute-start.16 = (bf16[1024,256]{1,0:T(8,128)(2,1)S(1)}, bf16[1024,256]{1,0:T(8,128)(2,1)S(1)}, u32[]{:S(2)}, u32[]{:S(2)}) collective-permute-start(bf16[1024,256]{1,0:T(8,128)(2,1)S(1)} %maximum_select_fusion.1), channel_id=1, source_target_pairs={{8,0},{12,4},{0,8},{4,12},{9,1},{13,5},{1,9},{5,13},{10,2},{14,6},... | collective-permute-start | bytes 1572872 | tf_op jit(solution)/shard_map/ppermute | solution.py:275
  172.2 0.9 copy-start.9
  178.1 7.6 %copy-start.2 = (f32[768,256]{1,0:T(8,128)S(1)}, f32[768,256]{1,0:T(8,128)}, u32[]{:S(2)}) copy-start(f32[768,256]{1,0:T(8,128)} %activate.5) | copy-start | bytes 2359300
  186.7 10.5 %collective-permute-start.17 = (bf16[784,256]{1,0:T(8,128)(2,1)}, bf16[784,256]{1,0:T(8,128)(2,1)S(1)}, u32[]{:S(2)}, u32[]{:S(2)}) collective-permute-start(bf16[784,256]{1,0:T(8,128)(2,1)} %pad_maximum_fusion), channel_id=1, source_target_pairs={{0,4},{4,0},{8,12},{1,5},{5,1},{9,13},{2,6},{6,2},{10,14},{3,7},{7... | collective-permute-start | bytes 1204232 | tf_op jit(solution)/shard_map/ppermute | solution.py:340
  189.6 20.0 %collective-permute-start.18 = (bf16[528,768]{1,0:T(8,128)(2,1)}, bf16[528,768]{1,0:T(8,128)(2,1)S(1)}, u32[]{:S(2)}, u32[]{:S(2)}) collective-permute-start(bf16[528,768]{1,0:T(8,128)(2,1)} %get-tuple-element.95), channel_id=1, source_target_pairs={{0,64},{64,0},{1,65},{65,1},{2,66},{66,2},{3,67},{67,3},{4,68},{68... | collective-permute-start | bytes 2433032 | tf_op jit(solution)/shard_map/ppermute | solution.py:244
  197.2 21.1 %copy-start.6 = (bf16[784,256]{1,0:T(8,128)(2,1)}, bf16[784,256]{1,0:T(8,128)(2,1)S(1)}, u32[]{:S(2)}) copy-start(bf16[784,256]{1,0:T(8,128)(2,1)S(1)} %collective-permute-done.17) | copy-start | bytes 1204228
  209.7 3.7 %copy-start.10 = (bf16[528,768]{1,0:T(8,128)(2,1)}, bf16[528,768]{1,0:T(8,128)(2,1)S(1)}, u32[]{:S(2)}) copy-start(bf16[528,768]{1,0:T(8,128)(2,1)S(1)} %collective-permute-done.18.refs_2_) | copy-start | bytes 2433028
  209.9 21.3 %collective-permute-start.19 = (bf16[528,512]{1,0:T(8,128)(2,1)}, bf16[528,512]{1,0:T(8,128)(2,1)}, u32[]{:S(2)}, u32[]{:S(2)}) collective-permute-start(bf16[528,512]{1,0:T(8,128)(2,1)} %get-tuple-element.98), channel_id=1, source_target_pairs={{0,64},{64,0},{1,65},{65,1},{2,66},{66,2},{3,67},{67,3},{4,68},{68... | collective-permute-start | bytes 1622024 | tf_op jit(solution)/shard_map/ppermute | solution.py:244
  220.8 18.7 %copy-start.3 = (f32[768,256]{1,0:T(8,128)S(1)}, f32[768,256]{1,0:T(8,128)}, u32[]{:S(2)}) copy-start(f32[768,256]{1,0:T(8,128)} %activate.6) | copy-start | bytes 2359300
  220.8 10.5 %collective-permute-start.20 = (bf16[768,256]{1,0:T(8,128)(2,1)}, bf16[768,256]{1,0:T(8,128)(2,1)}, u32[]{:S(2)}, u32[]{:S(2)}) collective-permute-start(bf16[768,256]{1,0:T(8,128)(2,1)} %get-tuple-element.116), channel_id=1, source_target_pairs={{4,8},{0,12},{5,9},{1,13},{6,10},{2,14},{7,11},{3,15},{20,24},{16,... | collective-permute-start | bytes 1179656 | tf_op jit(solution)/shard_map/ppermute | solution.py:344
  222.2 9.1 %collective-permute-start.21 = (bf16[768,256]{1,0:T(8,128)(2,1)}, bf16[768,256]{1,0:T(8,128)(2,1)S(1)}, u32[]{:S(2)}, u32[]{:S(2)}) collective-permute-start(bf16[768,256]{1,0:T(8,128)(2,1)} %get-tuple-element.115), channel_id=1, source_target_pairs={{0,4},{4,0},{8,12},{1,5},{5,1},{9,13},{2,6},{6,2},{10,14},{3,7},{7... | collective-permute-start | bytes 1179656 | tf_op jit(solution)/shard_map/ppermute | solution.py:340
  235.2 8.2 %copy-start.4 = (f32[512,256]{1,0:T(8,128)S(1)}, f32[512,256]{1,0:T(8,128)}, u32[]{:S(2)}) copy-start(f32[512,256]{1,0:T(8,128)} %activate.7) | copy-start | bytes 1572868
  235.2 18.0 %copy-start.7 = (bf16[784,256]{1,0:T(8,128)(2,1)S(1)}, bf16[784,256]{1,0:T(8,128)(2,1)}, u32[]{:S(2)}) copy-start(bf16[784,256]{1,0:T(8,128)(2,1)} %copy-done.6) | copy-start | bytes 1204228
  236.4 6.9 %collective-permute-start.23 = (bf16[512,256]{1,0:T(8,128)(2,1)S(1)}, bf16[512,256]{1,0:T(8,128)(2,1)S(1)}, u32[]{:S(2)}, u32[]{:S(2)}) collective-permute-start(bf16[512,256]{1,0:T(8,128)(2,1)S(1)} %fusion.17), channel_id=1, source_target_pairs={{0,4},{4,0},{8,12},{1,5},{5,1},{9,13},{2,6},{6,2},{10,14},{3,7},{7... | collective-permute-start | bytes 786440 | tf_op jit(solution)/shard_map/ppermute | solution.py:340
  239.9 13.3 %collective-permute-start.22 = (bf16[768,256]{1,0:T(8,128)(2,1)S(1)}, bf16[768,256]{1,0:T(8,128)(2,1)S(1)}, u32[]{:S(2)}, u32[]{:S(2)}) collective-permute-start(bf16[768,256]{1,0:T(8,128)(2,1)S(1)} %fusion.7), channel_id=1, source_target_pairs={{4,8},{0,12},{5,9},{1,13},{6,10},{2,14},{7,11},{3,15},{20,24},{16,... | collective-permute-start | bytes 1179656 | tf_op jit(solution)/shard_map/ppermute | solution.py:344
  243.6 12.4 %collective-permute-start.24 = (bf16[512,256]{1,0:T(8,128)(2,1)S(1)}, bf16[512,256]{1,0:T(8,128)(2,1)S(1)}, u32[]{:S(2)}, u32[]{:S(2)}) collective-permute-start(bf16[512,256]{1,0:T(8,128)(2,1)S(1)} %fusion.11), channel_id=1, source_target_pairs={{4,8},{0,12},{5,9},{1,13},{6,10},{2,14},{7,11},{3,15},{20,24},{16,... | collective-permute-start | bytes 786440 | tf_op jit(solution)/shard_map/ppermute | solution.py:344
  256.3 2.4 copy-start.1
Sparse Core Ops, SparseCore 0:
  9.7 109.3 all-gather.2
  121.3 66.1 all-gather.4

commit v4 on v3

--- a/solution.py
+++ b/solution.py
@@ -24,11 +24,11 @@
 
 CHUNKS = {
     "states": (HEAD_COLUMNS, 256),
-    "a": (0, 768),
-    "b": (768, 768),
-    "c": (1536, 512),
+    "a": (0, 896),
+    "b": (896, 768),
+    "c": (1664, 384),
 }
-SPLIT = 1536
+SPLIT = 1664
 STATE_WIDTH = 384
 
 

time: 267 us -> 271 us (1.015)
    ppermute x3, waiting for transfers between devices: 16.5 us -> 10.1 us  [second_step(): lax.ppermute((mine * own + its * came.astype(F32)).astype(BF16), 'z', [(1...]
    all_gather x1, waiting for transfers between devices: 28.3 us -> 33.6 us  [per_device(): early = lax.all_gather(s, ('x', 'z'), axis=0, tiled=True)]
    ppermute x1, waiting for transfers between devices: 7.4 us -> 3.21 us  [all_rows(): far = lax.ppermute(two, 'z', [(2, 0), (3, 1), (0, 2), (1, 3)])]
    ppermute x3, waiting for transfers between devices: 6.21 us -> 9.86 us  [first_step(): lax.ppermute(jnp.concatenate([own.astype(BF16), *more]), 'z', [(0, 1), (1...]
    unnamed x36 -> x44, local copies, waits for them, and re-layouts: 5.17 us -> 1.73 us
  transfers between devices with their start and end apart: 27 -> 27, of which waited for: 13 -> 12; matrix products, arithmetic and copies ran while one was open for 7% -> 7% of each run, Pallas kernels for 25% -> 27%
where the time goes in v4:
time: 271 us; the launch traced here: 270 us
  waiting for transfers between devices  104 us (38%)
  Pallas kernels  72.9 us (27%)
  starting transfers between devices  49.3 us (18%)
  other arithmetic  17 us (6%)
  between operations  15.8 us (6%)
  local copies, waits for them, and re-layouts  10.9 us (4%)
    pallas_call x4, Pallas kernels, project(): pl.pallas_call(kernel, out_shape=(jax.ShapeDtypeStruct((LONG, width), F32...  42.7 us
    all_gather x1, waiting for transfers between devices, per_device(): early = lax.all_gather(s, ('x', 'z'), axis=0, tiled=True)  33.6 us
    ppermute x9, waiting for transfers between devices, swap(): return lax.ppermute(value, axis, [(0, 1), (1, 0)])  32.6 us
    ppermute x9, starting transfers between devices, swap(): return lax.ppermute(value, axis, [(0, 1), (1, 0)])  19.7 us
    pallas_call x4, Pallas kernels, call(): pl.pallas_call(kernel, out_shape=out, in_specs=[SMEM] + [VMEM] * (len(arg...  16.5 us
    ppermute x1, waiting for transfers between devices, halos(): lax.ppermute(lax.dynamic_index_in_dim(last, 1 - yh, 0, False), ('yh', 'z'...  11.1 us
    ppermute x3, waiting for transfers between devices, second_step(): lax.ppermute((mine * own + its * came.astype(F32)).astype(BF16), 'z', [(1...  10.1 us
    ppermute x3, waiting for transfers between devices, first_step(): lax.ppermute(jnp.concatenate([own.astype(BF16), *more]), 'z', [(0, 1), (1...  9.86 us
  transfers between devices with their start and end apart: 27, of which 12 were waited for; matrix products, arithmetic and copies ran while one was open for 7% of the time, Pallas kernels for 27%

profile of v4, /device:TPU:64, one launch (start us, length us, event | category | flops | bytes accessed | tf_op | source)
XLA Modules:
  0.0 270.2 jit_solution(10059987889953403366)
XLA Ops:
  8.3 1.9 concatenate.27
  10.3 2.0 cut.3
  12.3 3.3 %collective-permute-start = (bf16[512,768]{1,0:T(8,128)(2,1)}, bf16[512,768]{1,0:T(8,128)(2,1)S(1)}, u32[]{:S(2)}, u32[]{:S(2)}) collective-permute-start(bf16[512,768]{1,0:T(8,128)(2,1)} %cut.3), channel_id=1, source_target_pairs={{0,64},{64,0},{1,65},{65,1},{2,66},{66,2},{3,67},{67,3},{4,68},{68... | collective-permute-start | bytes 2359304 | tf_op jit(solution)/shard_map/ppermute | solution.py:244
  16.7 3.5 %collective-permute-start.1 = (bf16[16,16,256]{2,1,0:T(8,128)(2,1)S(1)}, bf16[16,16,256]{2,1,0:T(8,128)(2,1)S(1)}, u32[]{:S(2)}, u32[]{:S(2)}) collective-permute-start(bf16[16,16,256]{2,1,0:T(8,128)(2,1)S(1)} %bitcast.79), channel_id=1, source_target_pairs={{0,4},{4,8},{8,12},{1,5},{5,9},{9,13},{2,6},{6,10},{10,14},{3,7},{... | collective-permute-start | bytes 393224 | tf_op jit(solution)/shard_map/ppermute | solution.py:250
  20.3 1.9 collective-permute-start.2
  22.3 2.5 cut.2
  24.8 11.1 %collective-permute-done.2.halo_ref = bf16[16,16,256]{2,1,0:T(8,128)(2,1)S(1)} collective-permute-done((bf16[16,16,256]{2,1,0:T(8,128)(2,1)S(1)}, bf16[16,16,256]{2,1,0:T(8,128)(2,1)S(1)}, u32[]{:S(2)}, u32[]{:S(2)}) %collective-permute-start.2) | collective-permute-done | bytes 131104 | tf_op jit(solution)/shard_map/ppermute | solution.py:252
  35.9 3.3 %collective-permute-start.3 = (bf16[512,1280]{1,0:T(8,128)(2,1)}, bf16[512,1280]{1,0:T(8,128)(2,1)}, u32[]{:S(2)}, u32[]{:S(2)}) collective-permute-start(bf16[512,1280]{1,0:T(8,128)(2,1)} %cut.2), channel_id=1, source_target_pairs={{0,64},{64,0},{1,65},{65,1},{2,66},{66,2},{3,67},{67,3},{4,68},{68... | collective-permute-start | bytes 3932168 | tf_op jit(solution)/shard_map/ppermute | solution.py:244
  39.3 4.5 %own_tokens.1.refs_0_ = bf16[16,528,256]{2,1,0:T(8,128)(2,1)} custom-call(s32[1]{0:T(128)} %bitcast.9.at_ref, bf16[16,16,256]{2,1,0:T(8,128)(2,1)} %copy-done.12, bf16[512,8192]{1,0:T(8,128)(2,1)} %bitcast.72), custom_call_target="tpu_custom_call" | custom-call | bytes 8650752 | tf_op jit(solution)/shard_map/own_tokens/pallas_call | solution.py:108
  43.8 23.5 %collective-permute-done.3.refs_1_ = bf16[512,1280]{1,0:T(8,128)(2,1)} collective-permute-done((bf16[512,1280]{1,0:T(8,128)(2,1)}, bf16[512,1280]{1,0:T(8,128)(2,1)}, u32[]{:S(2)}, u32[]{:S(2)}) %collective-permute-start.3) | collective-permute-done | bytes 1310752 | tf_op jit(solution)/shard_map/ppermute | solution.py:244
  67.3 3.2 %collective-permute-start.6 = (bf16[2,512,256]{2,1,0:T(8,128)(2,1)S(1)}, bf16[2,512,256]{2,1,0:T(8,128)(2,1)S(1)}, u32[]{:S(2)}, u32[]{:S(2)}) collective-permute-start(bf16[2,512,256]{2,1,0:T(8,128)(2,1)S(1)} %constant_dynamic-slice_fusion), channel_id=1, source_target_pairs={{0,64},{64,0},{1,65},{65,1},{2,66},{66,2},{3,67},{67,3},{4,68},{68... | collective-permute-start | bytes 1572872 | tf_op jit(solution)/shard_map/ppermute | solution.py:244
  73.9 4.6 %partner_tokens.1.refs_1_ = bf16[16,528,256]{2,1,0:T(8,128)(2,1)} custom-call(s32[1]{0:T(128)} %bitcast.1.at_ref, bf16[16,16,256]{2,1,0:T(8,128)(2,1)} %copy-done.11, bf16[512,768]{1,0:T(8,128)(2,1)} %copy-done.8, bf16[512,1280]{1,0:T(8,128)(2,1)} %collective-permute-done.3.refs_1_, bf16[512,768]{1,0:T(8,128)(2,1)} %collective-permute-done.4.refs_2_, ...), custom_call_target="tpu_custom_call" | custom-call | bytes 8650752 | tf_op jit(solution)/shard_map/partner_tokens/pallas_call | solution.py:108
  78.5 4.6 %collective-permute-done.6 = bf16[2,512,256]{2,1,0:T(8,128)(2,1)S(1)} collective-permute-done((bf16[2,512,256]{2,1,0:T(8,128)(2,1)S(1)}, bf16[2,512,256]{2,1,0:T(8,128)(2,1)S(1)}, u32[]{:S(2)}, u32[]{:S(2)}) %collective-permute-start.6) | collective-permute-done | bytes 524320 | tf_op jit(solution)/shard_map/ppermute | solution.py:244
  83.2 2.8 %collective-permute-start.7 = (s32[2]{0:T(128)S(1)}, s32[2]{0:T(128)S(1)}, u32[]{:S(2)}, u32[]{:S(2)}) collective-permute-start(s32[2]{0:T(128)S(1)} %pad_add_fusion.1), channel_id=1, source_target_pairs={{0,48},{16,0},{32,16},{48,32},{1,49},{17,1},{33,17},{49,33},{2,50}... | collective-permute-start | bytes 32 | tf_op jit(solution)/shard_map/ppermute | solution.py:40
  87.6 3.4 %collective-permute-done.8 = s32[2]{0:T(128)S(1)} collective-permute-done((s32[2]{0:T(128)S(1)}, s32[2]{0:T(128)S(1)}, u32[]{:S(2)}, u32[]{:S(2)}) %collective-permute-start.8) | collective-permute-done | bytes 40 | tf_op jit(solution)/shard_map/ppermute | solution.py:40
  91.5 33.6 %all-gather.3.cloned.1.call-done.refs_2_.refs_3_.refs_4_.refs_5_ = bf16[4096,2048]{1,0:T(8,128)(2,1)} async-done(((bf16[256,2048]{1,0:T(8,128)(2,1)}), bf16[4096,2048]{1,0:T(8,128)(2,1)}) %all-gather.3.cloned.1.call-update) | async-done | bytes 16777232 | tf_op jit(solution)/shard_map/all_gather | solution.py:286
  126.1 8.8 %project.4 = (f32[528,384]{1,0:T(8,128)}, bf16[528,384]{1,0:T(8,128)(2,1)}) custom-call(s32[16]{0:T(128)} %iota.14.places_ref, bf16[16,528,256]{2,1,0:T(8,128)(2,1)} %own_tokens.1.refs_0_, bf16[16,528,256]{2,1,0:T(8,128)(2,1)} %partner_tokens.1.refs_1_, bf16[4096,2048]{1,0:T(8,128)(2,1)} %all-gather.3.cloned.1.call-done.refs_2_.refs_3_.refs_4_.refs_5_, ...), custom_call_target="tpu_custom_call" | custom-call | flops 3321888768 | bytes 11845728 | tf_op jit(solution)/shard_map/project/pallas_call | solution.py:181
  135.3 2.5 collective-permute-start.12
  137.8 1.5 collective-permute-start.13
  139.3 3.0 %collective-permute-start.10 = (bf16[528,384]{1,0:T(8,128)(2,1)S(1)}, bf16[528,384]{1,0:T(8,128)(2,1)S(1)}, u32[]{:S(2)}, u32[]{:S(2)}) collective-permute-start(bf16[528,384]{1,0:T(8,128)(2,1)S(1)} %copy-done.18), channel_id=1, source_target_pairs={{0,64},{64,0},{1,65},{65,1},{2,66},{66,2},{3,67},{67,3},{4,68},{68... | collective-permute-start | bytes 1216520 | tf_op jit(solution)/shard_map/ppermute | solution.py:244
  142.8 13.7 %project.5 = (f32[528,896]{1,0:T(8,128)}, bf16[528,896]{1,0:T(8,128)(2,1)}) custom-call(s32[16]{0:T(128)} %iota.15.places_ref, bf16[16,528,256]{2,1,0:T(8,128)(2,1)} %own_tokens.1.refs_0_, bf16[16,528,256]{2,1,0:T(8,128)(2,1)} %partner_tokens.1.refs_1_, bf16[4096,2048]{1,0:T(8,128)(2,1)} %all-gather.3.cloned.1.call-done.refs_2_.refs_3_.refs_4_.refs_5_, ...), custom_call_target="tpu_custom_call" | custom-call | flops 7751073792 | bytes 16040032 | tf_op jit(solution)/shard_map/project/pallas_call | solution.py:181
  158.6 2.8 %activate.4 = (bf16[512,256]{1,0:T(8,128)(2,1)}, f32[512,32]{1,0:T(8,128)}) custom-call(s32[2]{0:T(128)} %pad_add_fusion.info_ref.refs_0_, f32[528,384]{1,0:T(8,128)} %get-tuple-element.80.own_ref, bf16[528,384]{1,0:T(8,128)(2,1)} %copy-done.9, f32[4,2304]{1,0:T(4,128)} %refs_3_.5, f32[1,2304]{1,0:T(1,128)} %broadcast_in_dim.77.bias_ref.refs_4_), custom_call_target="tpu_custom_call" | custom-call | flops 33554432 | bytes 270336 | tf_op jit(solution)/shard_map/activate/pallas_call | solution.py:231
  164.3 1.9 exponential_multiply_fusion.refs_5_
  166.7 11.4 %project.6 = (f32[528,768]{1,0:T(8,128)}, bf16[528,768]{1,0:T(8,128)(2,1)}) custom-call(s32[16]{0:T(128)} %iota.16.places_ref, bf16[16,528,256]{2,1,0:T(8,128)(2,1)} %own_tokens.1.refs_0_, bf16[16,528,256]{2,1,0:T(8,128)(2,1)} %partner_tokens.1.refs_1_, bf16[4096,2048]{1,0:T(8,128)(2,1)} %all-gather.3.cloned.1.call-done.refs_2_.refs_3_.refs_4_.refs_5_, ...), custom_call_target="tpu_custom_call" | custom-call | flops 6643777536 | bytes 14991456 | tf_op jit(solution)/shard_map/project/pallas_call | solution.py:181
  178.4 1.6 collective-permute-start.16
  180.1 3.2 %collective-permute-start.18 = (bf16[528,768]{1,0:T(8,128)(2,1)}, bf16[528,768]{1,0:T(8,128)(2,1)}, u32[]{:S(2)}, u32[]{:S(2)}) collective-permute-start(bf16[528,768]{1,0:T(8,128)(2,1)} %get-tuple-element.95), channel_id=1, source_target_pairs={{0,64},{64,0},{1,65},{65,1},{2,66},{66,2},{3,67},{67,3},{4,68},{68... | collective-permute-start | bytes 2433032 | tf_op jit(solution)/shard_map/ppermute | solution.py:244
  183.4 5.4 %activate.5 = f32[896,256]{1,0:T(8,128)} custom-call(s32[2]{0:T(128)} %pad_add_fusion.info_ref.refs_0_, f32[528,896]{1,0:T(8,128)} %get-tuple-element.86.refs_1_, bf16[528,896]{1,0:T(8,128)(2,1)} %collective-permute-done.14.refs_2_, f32[4,2304]{1,0:T(4,128)} %refs_3_.5, f32[1,2304]{1,0:T(1,128)} %broadcast_in_dim.77.bias_ref.refs_4_, ...), custom_call_target="tpu_custom_call" | custom-call | flops 117440512 | bytes 946176 | tf_op jit(solution)/shard_map/activate/pallas_call | solution.py:231
  188.7 3.2 %collective-permute-done.16 = bf16[1024,256]{1,0:T(8,128)(2,1)} collective-permute-done((bf16[1024,256]{1,0:T(8,128)(2,1)S(1)}, bf16[1024,256]{1,0:T(8,128)(2,1)}, u32[]{:S(2)}, u32[]{:S(2)}) %collective-permute-start.16) | collective-permute-done | bytes 524320 | tf_op jit(solution)/shard_map/ppermute | solution.py:275
  191.9 1.4 maximum_select_fusion
  193.7 2.9 %collective-permute-start.17 = (bf16[912,256]{1,0:T(8,128)(2,1)S(1)}, bf16[912,256]{1,0:T(8,128)(2,1)S(1)}, u32[]{:S(2)}, u32[]{:S(2)}) collective-permute-start(bf16[912,256]{1,0:T(8,128)(2,1)S(1)} %pad_maximum_fusion), channel_id=1, source_target_pairs={{0,4},{4,0},{8,12},{1,5},{5,1},{9,13},{2,6},{6,2},{10,14},{3,7},{7... | collective-permute-start | bytes 1400840 | tf_op jit(solution)/shard_map/ppermute | solution.py:340
  197.8 6.2 %collective-permute-done.17 = bf16[912,256]{1,0:T(8,128)(2,1)S(1)} collective-permute-done((bf16[912,256]{1,0:T(8,128)(2,1)S(1)}, bf16[912,256]{1,0:T(8,128)(2,1)S(1)}, u32[]{:S(2)}, u32[]{:S(2)}) %collective-permute-start.17) | collective-permute-done | bytes 466976 | tf_op jit(solution)/shard_map/ppermute | solution.py:340
  204.6 8.7 %project.7 = (f32[528,384]{1,0:T(8,128)}, bf16[528,384]{1,0:T(8,128)(2,1)}) custom-call(s32[16]{0:T(128)} %iota.18.places_ref, bf16[16,528,256]{2,1,0:T(8,128)(2,1)} %own_tokens.1.refs_0_, bf16[16,528,256]{2,1,0:T(8,128)(2,1)} %partner_tokens.1.refs_1_, bf16[4096,384]{1,0:T(8,128)(2,1)} %all-gather.5.cloned.1.call-done.refs_2_.refs_3_.refs_4_.refs_5_, ...), custom_call_target="tpu_custom_call" | custom-call | flops 3321888768 | bytes 11845728 | tf_op jit(solution)/shard_map/project/pallas_call | solution.py:181
  214.1 1.3 collective-permute-start.20
  215.4 4.9 %activate.6 = f32[768,256]{1,0:T(8,128)} custom-call(s32[2]{0:T(128)} %pad_add_fusion.info_ref.refs_0_, f32[528,768]{1,0:T(8,128)} %get-tuple-element.99.refs_1_, bf16[528,768]{1,0:T(8,128)(2,1)} %collective-permute-done.18.refs_2_, f32[4,2304]{1,0:T(4,128)} %refs_3_.5, f32[1,2304]{1,0:T(1,128)} %broadcast_in_dim.77.bias_ref.refs_4_, ...), custom_call_target="tpu_custom_call" | custom-call | flops 100663296 | bytes 811008 | tf_op jit(solution)/shard_map/activate/pallas_call | solution.py:231
  220.3 1.4 fusion.18
  221.7 4.4 %collective-permute-start.21 = (bf16[768,256]{1,0:T(8,128)(2,1)S(1)}, bf16[768,256]{1,0:T(8,128)(2,1)S(1)}, u32[]{:S(2)}, u32[]{:S(2)}) collective-permute-start(bf16[768,256]{1,0:T(8,128)(2,1)S(1)} %fusion.18), channel_id=1, source_target_pairs={{0,4},{4,0},{8,12},{1,5},{5,1},{9,13},{2,6},{6,2},{10,14},{3,7},{7... | collective-permute-start | bytes 1179656 | tf_op jit(solution)/shard_map/ppermute | solution.py:340
  226.1 3.2 %collective-permute-start.19 = (bf16[528,384]{1,0:T(8,128)(2,1)}, bf16[528,384]{1,0:T(8,128)(2,1)S(1)}, u32[]{:S(2)}, u32[]{:S(2)}) collective-permute-start(bf16[528,384]{1,0:T(8,128)(2,1)} %get-tuple-element.98), channel_id=1, source_target_pairs={{0,64},{64,0},{1,65},{65,1},{2,66},{66,2},{3,67},{67,3},{4,68},{68... | collective-permute-start | bytes 1216520 | tf_op jit(solution)/shard_map/ppermute | solution.py:244
  229.4 1.9 collective-permute-done.21
  231.4 4.4 %collective-permute-done.19.refs_2_ = bf16[528,384]{1,0:T(8,128)(2,1)S(1)} collective-permute-done((bf16[528,384]{1,0:T(8,128)(2,1)}, bf16[528,384]{1,0:T(8,128)(2,1)S(1)}, u32[]{:S(2)}, u32[]{:S(2)}) %collective-permute-start.19) | collective-permute-done | bytes 405536 | tf_op jit(solution)/shard_map/ppermute | solution.py:244
  235.9 1.9 fusion.7
  239.0 3.4 %activate.7 = f32[384,256]{1,0:T(8,128)} custom-call(s32[2]{0:T(128)} %pad_add_fusion.info_ref.refs_0_, f32[528,384]{1,0:T(8,128)} %get-tuple-element.103.refs_1_, bf16[528,384]{1,0:T(8,128)(2,1)} %copy-done.10, f32[4,2304]{1,0:T(4,128)} %refs_3_.5, f32[1,2304]{1,0:T(1,128)} %broadcast_in_dim.77.bias_ref.refs_4_, ...), custom_call_target="tpu_custom_call" | custom-call | flops 50331648 | bytes 405504 | tf_op jit(solution)/shard_map/activate/pallas_call | solution.py:231
  243.7 1.3 collective-permute-start.23
  245.0 1.4 fusion.1
  246.5 1.7 collective-permute-done.23
  248.4 1.3 collective-permute-start.24
  249.7 1.4 fusion.5
  251.1 10.1 %collective-permute-done.24 = bf16[384,256]{1,0:T(8,128)(2,1)S(1)} collective-permute-done((bf16[384,256]{1,0:T(8,128)(2,1)S(1)}, bf16[384,256]{1,0:T(8,128)(2,1)S(1)}, u32[]{:S(2)}, u32[]{:S(2)}) %collective-permute-start.24) | collective-permute-done | bytes 196640 | tf_op jit(solution)/shard_map/ppermute | solution.py:344
  261.4 1.5 maximum_bitcast_fusion
  (135 shorter events, 20.9 us)
Async XLA Ops:
  6.5 32.6 %copy-start = (bf16[2,2048,256]{2,1,0:T(8,128)(2,1)S(1)}, bf16[2,2048,256]{2,1,0:T(8,128)(2,1)}, u32[]{:S(2)}) copy-start(bf16[2,2048,256]{2,1,0:T(8,128)(2,1)} %param.17) | copy-start | bytes 6291460
  6.5 1.8 slice-start
  6.5 1.8 slice-start.1
  6.5 118.6 %all-gather.3.cloned.1.call-start = ((), (), s32[]{:S(2)}) async-start(), calls=%async_computation | async-start | bytes 17825792 | tf_op jit(solution)/shard_map/all_gather | solution.py:286
  10.3 187.5 %all-gather.5.cloned.1.call-start = ((), (), s32[]{:S(2)}) async-start(), calls=%async_computation.1 | async-start | bytes 3342336 | tf_op jit(solution)/shard_map/all_gather | solution.py:287
  12.3 23.5 %collective-permute-start = (bf16[512,768]{1,0:T(8,128)(2,1)}, bf16[512,768]{1,0:T(8,128)(2,1)S(1)}, u32[]{:S(2)}, u32[]{:S(2)}) collective-permute-start(bf16[512,768]{1,0:T(8,128)(2,1)} %cut.3), channel_id=1, source_target_pairs={{0,64},{64,0},{1,65},{65,1},{2,66},{66,2},{3,67},{67,3},{4,68},{68... | collective-permute-start | bytes 2359304 | tf_op jit(solution)/shard_map/ppermute | solution.py:244
  16.7 8.1 %collective-permute-start.1 = (bf16[16,16,256]{2,1,0:T(8,128)(2,1)S(1)}, bf16[16,16,256]{2,1,0:T(8,128)(2,1)S(1)}, u32[]{:S(2)}, u32[]{:S(2)}) collective-permute-start(bf16[16,16,256]{2,1,0:T(8,128)(2,1)S(1)} %bitcast.79), channel_id=1, source_target_pairs={{0,4},{4,8},{8,12},{1,5},{5,9},{9,13},{2,6},{6,10},{10,14},{3,7},{... | collective-permute-start | bytes 393224 | tf_op jit(solution)/shard_map/ppermute | solution.py:250
  20.3 15.6 %collective-permute-start.2 = (bf16[16,16,256]{2,1,0:T(8,128)(2,1)S(1)}, bf16[16,16,256]{2,1,0:T(8,128)(2,1)S(1)}, u32[]{:S(2)}, u32[]{:S(2)}) collective-permute-start(bf16[16,16,256]{2,1,0:T(8,128)(2,1)S(1)} %bitcast.80), channel_id=1, source_target_pairs={{0,68},{4,72},{8,76},{64,4},{68,8},{72,12},{1,69},{5,73},{9,77},{6... | collective-permute-start | bytes 393224 | tf_op jit(solution)/shard_map/ppermute | solution.py:252
  24.8 14.4 %copy-start.12 = (bf16[16,16,256]{2,1,0:T(8,128)(2,1)}, bf16[16,16,256]{2,1,0:T(8,128)(2,1)S(1)}, u32[]{:S(2)}) copy-start(bf16[16,16,256]{2,1,0:T(8,128)(2,1)S(1)} %collective-permute-done.1.halo_ref) | copy-start | bytes 393220
  35.9 7.9 %copy-start.11 = (bf16[16,16,256]{2,1,0:T(8,128)(2,1)}, bf16[16,16,256]{2,1,0:T(8,128)(2,1)S(1)}, u32[]{:S(2)}) copy-start(bf16[16,16,256]{2,1,0:T(8,128)(2,1)S(1)} %collective-permute-done.2.halo_ref) | copy-start | bytes 393220
  35.9 7.9 %copy-start.8 = (bf16[512,768]{1,0:T(8,128)(2,1)}, bf16[512,768]{1,0:T(8,128)(2,1)S(1)}, u32[]{:S(2)}) copy-start(bf16[512,768]{1,0:T(8,128)(2,1)S(1)} %collective-permute-done.refs_0_) | copy-start | bytes 2359300
  35.9 31.4 %collective-permute-start.3 = (bf16[512,1280]{1,0:T(8,128)(2,1)}, bf16[512,1280]{1,0:T(8,128)(2,1)}, u32[]{:S(2)}, u32[]{:S(2)}) collective-permute-start(bf16[512,1280]{1,0:T(8,128)(2,1)} %cut.2), channel_id=1, source_target_pairs={{0,64},{64,0},{1,65},{65,1},{2,66},{66,2},{3,67},{67,3},{4,68},{68... | collective-permute-start | bytes 3932168 | tf_op jit(solution)/shard_map/ppermute | solution.py:244
  39.2 4.7 %collective-permute-start.4 = (bf16[512,768]{1,0:T(8,128)(2,1)S(1)}, bf16[512,768]{1,0:T(8,128)(2,1)}, u32[]{:S(2)}, u32[]{:S(2)}) collective-permute-start(bf16[512,768]{1,0:T(8,128)(2,1)S(1)} %collective-permute-done.refs_0_), channel_id=1, source_target_pairs={{0,1},{1,0},{2,3},{3,2},{4,5},{5,4},{6,7},{7,6},{8,9},{9,8},{10,11... | collective-permute-start | bytes 2359304 | tf_op jit(solution)/shard_map/ppermute | solution.py:244
  39.2 31.3 %copy-start.5 = (bf16[256,2304]{1,0:T(8,128)(2,1)S(1)}, bf16[256,2304]{1,0:T(8,128)(2,1)}, u32[]{:S(2)}) copy-start(bf16[256,2304]{1,0:T(8,128)(2,1)} %param.11) | copy-start | bytes 3538948
  39.2 33.4 %copy-start.16 = (f32[2304]{0:T(1024)S(1)}, f32[2304]{0:T(1024)}, u32[]{:S(2)}) copy-start(f32[2304]{0:T(1024)} %param.14) | copy-start | bytes 27652
  39.2 34.0 %copy-start.19 = (f32[32]{0:T(128)S(1)}, f32[32]{0:T(128)}, u32[]{:S(2)}) copy-start(f32[32]{0:T(128)} %param.16) | copy-start | bytes 388
  67.3 6.6 %collective-permute-start.5 = (bf16[512,1280]{1,0:T(8,128)(2,1)}, bf16[512,1280]{1,0:T(8,128)(2,1)}, u32[]{:S(2)}, u32[]{:S(2)}) collective-permute-start(bf16[512,1280]{1,0:T(8,128)(2,1)} %collective-permute-done.3.refs_1_), channel_id=1, source_target_pairs={{0,1},{1,0},{2,3},{3,2},{4,5},{5,4},{6,7},{7,6},{8,9},{9,8},{10,11... | collective-permute-start | bytes 3932168 | tf_op jit(solution)/shard_map/ppermute | solution.py:244
  67.3 15.8 %collective-permute-start.6 = (bf16[2,512,256]{2,1,0:T(8,128)(2,1)S(1)}, bf16[2,512,256]{2,1,0:T(8,128)(2,1)S(1)}, u32[]{:S(2)}, u32[]{:S(2)}) collective-permute-start(bf16[2,512,256]{2,1,0:T(8,128)(2,1)S(1)} %constant_dynamic-slice_fusion), channel_id=1, source_target_pairs={{0,64},{64,0},{1,65},{65,1},{2,66},{66,2},{3,67},{67,3},{4,68},{68... | collective-permute-start | bytes 1572872 | tf_op jit(solution)/shard_map/ppermute | solution.py:244
  83.2 4.4 %collective-permute-start.7 = (s32[2]{0:T(128)S(1)}, s32[2]{0:T(128)S(1)}, u32[]{:S(2)}, u32[]{:S(2)}) collective-permute-start(s32[2]{0:T(128)S(1)} %pad_add_fusion.1), channel_id=1, source_target_pairs={{0,48},{16,0},{32,16},{48,32},{1,49},{17,1},{33,17},{49,33},{2,50}... | collective-permute-start | bytes 32 | tf_op jit(solution)/shard_map/ppermute | solution.py:40
  85.9 5.0 %collective-permute-start.8 = (s32[2]{0:T(128)S(1)}, s32[2]{0:T(128)S(1)}, u32[]{:S(2)}, u32[]{:S(2)}) collective-permute-start(s32[2]{0:T(128)S(1)} %pad_add_fusion.1), channel_id=1, source_target_pairs={{0,32},{16,48},{32,0},{48,16},{1,33},{17,49},{33,1},{49,17},{2,34}... | collective-permute-start | bytes 32 | tf_op jit(solution)/shard_map/ppermute | solution.py:40
  86.7 4.8 %collective-permute-start.9 = (s32[2]{0:T(128)S(1)}, s32[2]{0:T(128)S(1)}, u32[]{:S(2)}, u32[]{:S(2)}) collective-permute-start(s32[2]{0:T(128)S(1)} %pad_add_fusion.1), channel_id=1, source_target_pairs={{0,16},{16,32},{32,48},{48,0},{1,17},{17,33},{33,49},{49,1},{2,18}... | collective-permute-start | bytes 32 | tf_op jit(solution)/shard_map/ppermute | solution.py:40
  134.9 4.5 %copy-start.18 = (bf16[528,384]{1,0:T(8,128)(2,1)S(1)}, bf16[528,384]{1,0:T(8,128)(2,1)}, u32[]{:S(2)}) copy-start(bf16[528,384]{1,0:T(8,128)(2,1)} %get-tuple-element.69) | copy-start | bytes 1216516
  135.0 22.2 %collective-permute-start.11 = (bf16[512,256]{1,0:T(8,128)(2,1)S(1)}, bf16[512,256]{1,0:T(8,128)(2,1)S(1)}, u32[]{:S(2)}, u32[]{:S(2)}) collective-permute-start(bf16[512,256]{1,0:T(8,128)(2,1)S(1)} %get-tuple-element.105), channel_id=1, source_target_pairs={{0,16},{16,32},{32,48},{48,0},{1,17},{17,33},{33,49},{49,1},{2,18}... | collective-permute-start | bytes 786440 | tf_op jit(solution)/shard_map/ppermute | solution.py:40
  135.3 21.9 %collective-permute-start.12 = (bf16[512,256]{1,0:T(8,128)(2,1)S(1)}, bf16[512,256]{1,0:T(8,128)(2,1)S(1)}, u32[]{:S(2)}, u32[]{:S(2)}) collective-permute-start(bf16[512,256]{1,0:T(8,128)(2,1)S(1)} %get-tuple-element.106), channel_id=1, source_target_pairs={{0,32},{16,48},{32,0},{48,16},{1,33},{17,49},{33,1},{49,17},{2,34}... | collective-permute-start | bytes 786440 | tf_op jit(solution)/shard_map/ppermute | solution.py:40
  137.8 19.4 %collective-permute-start.13 = (bf16[512,256]{1,0:T(8,128)(2,1)S(1)}, bf16[512,256]{1,0:T(8,128)(2,1)S(1)}, u32[]{:S(2)}, u32[]{:S(2)}) collective-permute-start(bf16[512,256]{1,0:T(8,128)(2,1)S(1)} %select_bitcast_fusion), channel_id=1, source_target_pairs={{0,48},{16,0},{32,16},{48,32},{1,49},{17,1},{33,17},{49,33},{2,50}... | collective-permute-start | bytes 786440 | tf_op jit(solution)/shard_map/ppermute | solution.py:40
  139.3 18.0 %collective-permute-start.10 = (bf16[528,384]{1,0:T(8,128)(2,1)S(1)}, bf16[528,384]{1,0:T(8,128)(2,1)S(1)}, u32[]{:S(2)}, u32[]{:S(2)}) collective-permute-start(bf16[528,384]{1,0:T(8,128)(2,1)S(1)} %copy-done.18), channel_id=1, source_target_pairs={{0,64},{64,0},{1,65},{65,1},{2,66},{66,2},{3,67},{67,3},{4,68},{68... | collective-permute-start | bytes 1216520 | tf_op jit(solution)/shard_map/ppermute | solution.py:244
  156.6 4.8 %copy-start.17 = (f32[32]{0:T(128)S(1)}, f32[32]{0:T(128)}, u32[]{:S(2)}) copy-start(f32[32]{0:T(128)} %param.15) | copy-start | bytes 388
  156.6 26.8 %collective-permute-start.14 = (bf16[528,896]{1,0:T(8,128)(2,1)}, bf16[528,896]{1,0:T(8,128)(2,1)}, u32[]{:S(2)}, u32[]{:S(2)}) collective-permute-start(bf16[528,896]{1,0:T(8,128)(2,1)} %get-tuple-element.78), channel_id=1, source_target_pairs={{0,64},{64,0},{1,65},{65,1},{2,66},{66,2},{3,67},{67,3},{4,68},{68... | collective-permute-start | bytes 2838536 | tf_op jit(solution)/shard_map/ppermute | solution.py:244
  157.3 20.8 %collective-permute-start.15 = (bf16[512,256]{1,0:T(8,128)(2,1)S(1)}, bf16[512,256]{1,0:T(8,128)(2,1)S(1)}, u32[]{:S(2)}, u32[]{:S(2)}) collective-permute-start(bf16[512,256]{1,0:T(8,128)(2,1)S(1)} %fusion.14), channel_id=1, source_target_pairs={{0,4},{4,0},{8,12},{12,8},{1,5},{5,1},{9,13},{13,9},{2,6},{6,2},{1... | collective-permute-start | bytes 786440 | tf_op jit(solution)/shard_map/ppermute | solution.py:273
  178.4 13.5 %collective-permute-start.16 = (bf16[1024,256]{1,0:T(8,128)(2,1)S(1)}, bf16[1024,256]{1,0:T(8,128)(2,1)}, u32[]{:S(2)}, u32[]{:S(2)}) collective-permute-start(bf16[1024,256]{1,0:T(8,128)(2,1)S(1)} %maximum_select_fusion.1), channel_id=1, source_target_pairs={{8,0},{12,4},{0,8},{4,12},{9,1},{13,5},{1,9},{5,13},{10,2},{14,6},... | collective-permute-start | bytes 1572872 | tf_op jit(solution)/shard_map/ppermute | solution.py:275
  180.1 33.2 %collective-permute-start.18 = (bf16[528,768]{1,0:T(8,128)(2,1)}, bf16[528,768]{1,0:T(8,128)(2,1)}, u32[]{:S(2)}, u32[]{:S(2)}) collective-permute-start(bf16[528,768]{1,0:T(8,128)(2,1)} %get-tuple-element.95), channel_id=1, source_target_pairs={{0,64},{64,0},{1,65},{65,1},{2,66},{66,2},{3,67},{67,3},{4,68},{68... | collective-permute-start | bytes 2433032 | tf_op jit(solution)/shard_map/ppermute | solution.py:244
  188.7 4.7 %copy-start.2 = (f32[896,256]{1,0:T(8,128)S(1)}, f32[896,256]{1,0:T(8,128)}, u32[]{:S(2)}) copy-start(f32[896,256]{1,0:T(8,128)} %activate.5) | copy-start | bytes 2752516
  193.7 10.3 %collective-permute-start.17 = (bf16[912,256]{1,0:T(8,128)(2,1)S(1)}, bf16[912,256]{1,0:T(8,128)(2,1)S(1)}, u32[]{:S(2)}, u32[]{:S(2)}) collective-permute-start(bf16[912,256]{1,0:T(8,128)(2,1)S(1)} %pad_maximum_fusion), channel_id=1, source_target_pairs={{0,4},{4,0},{8,12},{1,5},{5,1},{9,13},{2,6},{6,2},{10,14},{3,7},{7... | collective-permute-start | bytes 1400840 | tf_op jit(solution)/shard_map/ppermute | solution.py:340
  197.0 23.3 %copy-start.13 = (f32[768]{0:T(1024)}, f32[768]{0:T(1024)S(1)}, u32[]{:S(2)}) copy-start(f32[768]{0:T(1024)S(1)} %mul.260) | copy-start | bytes 9220
  204.0 9.6 %copy-start.6 = (bf16[912,256]{1,0:T(8,128)(2,1)}, bf16[912,256]{1,0:T(8,128)(2,1)S(1)}, u32[]{:S(2)}) copy-start(bf16[912,256]{1,0:T(8,128)(2,1)S(1)} %collective-permute-done.17) | copy-start | bytes 1400836
  214.1 21.8 %collective-permute-start.20 = (bf16[896,256]{1,0:T(8,128)(2,1)S(1)}, bf16[896,256]{1,0:T(8,128)(2,1)}, u32[]{:S(2)}, u32[]{:S(2)}) collective-permute-start(bf16[896,256]{1,0:T(8,128)(2,1)S(1)} %fusion.3), channel_id=1, source_target_pairs={{4,8},{0,12},{5,9},{1,13},{6,10},{2,14},{7,11},{3,15},{20,24},{16,... | collective-permute-start | bytes 1376264 | tf_op jit(solution)/shard_map/ppermute | solution.py:344
  220.3 15.6 %copy-start.3 = (f32[768,256]{1,0:T(8,128)S(1)}, f32[768,256]{1,0:T(8,128)}, u32[]{:S(2)}) copy-start(f32[768,256]{1,0:T(8,128)} %activate.6) | copy-start | bytes 2359300
  221.7 9.7 %collective-permute-start.21 = (bf16[768,256]{1,0:T(8,128)(2,1)S(1)}, bf16[768,256]{1,0:T(8,128)(2,1)S(1)}, u32[]{:S(2)}, u32[]{:S(2)}) collective-permute-start(bf16[768,256]{1,0:T(8,128)(2,1)S(1)} %fusion.18), channel_id=1, source_target_pairs={{0,4},{4,0},{8,12},{1,5},{5,1},{9,13},{2,6},{6,2},{10,14},{3,7},{7... | collective-permute-start | bytes 1179656 | tf_op jit(solution)/shard_map/ppermute | solution.py:340
  226.1 9.7 %collective-permute-start.19 = (bf16[528,384]{1,0:T(8,128)(2,1)}, bf16[528,384]{1,0:T(8,128)(2,1)S(1)}, u32[]{:S(2)}, u32[]{:S(2)}) collective-permute-start(bf16[528,384]{1,0:T(8,128)(2,1)} %get-tuple-element.98), channel_id=1, source_target_pairs={{0,64},{64,0},{1,65},{65,1},{2,66},{66,2},{3,67},{67,3},{4,68},{68... | collective-permute-start | bytes 1216520 | tf_op jit(solution)/shard_map/ppermute | solution.py:244
  229.4 13.1 %copy-start.15 = (f32[384]{0:T(512)S(1)}, f32[384]{0:T(512)}, u32[]{:S(2)}) copy-start(f32[384]{0:T(512)} %mul.276) | copy-start | bytes 4612
  235.8 3.2 %copy-start.10 = (bf16[528,384]{1,0:T(8,128)(2,1)}, bf16[528,384]{1,0:T(8,128)(2,1)S(1)}, u32[]{:S(2)}) copy-start(bf16[528,384]{1,0:T(8,128)(2,1)S(1)} %collective-permute-done.19.refs_2_) | copy-start | bytes 1216516
  235.8 9.2 %copy-start.7 = (bf16[912,256]{1,0:T(8,128)(2,1)S(1)}, bf16[912,256]{1,0:T(8,128)(2,1)}, u32[]{:S(2)}) copy-start(bf16[912,256]{1,0:T(8,128)(2,1)} %copy-done.6) | copy-start | bytes 1400836
  237.8 11.9 %collective-permute-start.22 = (bf16[768,256]{1,0:T(8,128)(2,1)}, bf16[768,256]{1,0:T(8,128)(2,1)}, u32[]{:S(2)}, u32[]{:S(2)}) collective-permute-start(bf16[768,256]{1,0:T(8,128)(2,1)} %fusion.7), channel_id=1, source_target_pairs={{4,8},{0,12},{5,9},{1,13},{6,10},{2,14},{7,11},{3,15},{20,24},{16,... | collective-permute-start | bytes 1179656 | tf_op jit(solution)/shard_map/ppermute | solution.py:344
  242.5 5.7 %copy-start.4 = (f32[384,256]{1,0:T(8,128)S(1)}, f32[384,256]{1,0:T(8,128)}, u32[]{:S(2)}) copy-start(f32[384,256]{1,0:T(8,128)} %activate.7) | copy-start | bytes 1179652
  243.7 4.5 %collective-permute-start.23 = (bf16[384,256]{1,0:T(8,128)(2,1)S(1)}, bf16[384,256]{1,0:T(8,128)(2,1)S(1)}, u32[]{:S(2)}, u32[]{:S(2)}) collective-permute-start(bf16[384,256]{1,0:T(8,128)(2,1)S(1)} %fusion.17), channel_id=1, source_target_pairs={{0,4},{4,0},{8,12},{1,5},{5,1},{9,13},{2,6},{6,2},{10,14},{3,7},{7... | collective-permute-start | bytes 589832 | tf_op jit(solution)/shard_map/ppermute | solution.py:340
  245.0 4.7 %copy-start.14 = (f32[768]{0:T(1024)S(1)}, f32[768]{0:T(1024)}, u32[]{:S(2)}) copy-start(f32[768]{0:T(1024)} %copy-done.13) | copy-start | bytes 9220
  248.4 12.8 %collective-permute-start.24 = (bf16[384,256]{1,0:T(8,128)(2,1)S(1)}, bf16[384,256]{1,0:T(8,128)(2,1)S(1)}, u32[]{:S(2)}, u32[]{:S(2)}) collective-permute-start(bf16[384,256]{1,0:T(8,128)(2,1)S(1)} %fusion.11), channel_id=1, source_target_pairs={{4,8},{0,12},{5,9},{1,13},{6,10},{2,14},{7,11},{3,15},{20,24},{16,... | collective-permute-start | bytes 589832 | tf_op jit(solution)/shard_map/ppermute | solution.py:344
  261.1 2.2 copy-start.1
  (1 other events, 1.3 us)
Sparse Core Ops, SparseCore 0:
  10.4 114.6 all-gather.2
  127.3 50.8 all-gather.4
